TPU v7x, 32 devices: a whole 2x2x4 slice. The times are simulated.
32 devices in a mesh: dp: 8 (over y, x, core), fsdp: 4 (over z).
Axes of the slice: x: 2, y: 2, z: 4, core: 2. Of those that a mesh axis runs over, the one named last changes fastest.
Arguments:
- latents: bfloat16 [32, 768, 1024], P(('dp', 'fsdp')), may hold values from -6 to 6
- lengths: int32 [32, 4], P(('dp', 'fsdp')), may hold values from 1 to 512, 768 in all within a row
- cotangent: bfloat16 [32, 768, 1024], P(('dp', 'fsdp')), may hold values from -6 to 6
- matrices: float32 [6, 1024, 1024], P(None, ('dp', 'fsdp')), may hold values from -2 to 2
- norm_params: float32 [4, 1024], P(None, ('dp', 'fsdp')), may hold values from -2 to 2
- moment1_mat: float32 [6, 1024, 1024], P(None, ('dp', 'fsdp')), may hold values from -256 to 256
- moment2_mat: float32 [6, 1024, 1024], P(None, ('dp', 'fsdp')), may hold values from 24.576 to 1228.8
- moment1_norm: float32 [4, 1024], P(None, ('dp', 'fsdp')), may hold values from -256 to 256
- moment2_norm: float32 [4, 1024], P(None, ('dp', 'fsdp')), may hold values from 24.576 to 1228.8
Outputs:
- out_latents: bfloat16 [32, 768, 1024], P(('dp', 'fsdp'))
- grad_latents: bfloat16 [32, 768, 1024], P(('dp', 'fsdp'))
- grad_matrices: float32 [6, 1024, 1024], P(None, ('dp', 'fsdp'))
- grad_norms: float32 [4, 1024], P(None, ('dp', 'fsdp'))
- update_matrices: float32 [6, 1024, 1024], P(None, ('dp', 'fsdp'))
- update_norms: float32 [4, 1024], P(None, ('dp', 'fsdp'))
- new_moment1_mat: float32 [6, 1024, 1024], P(None, ('dp', 'fsdp'))
- new_moment2_mat: float32 [6, 1024, 1024], P(None, ('dp', 'fsdp'))
- new_moment1_norm: float32 [4, 1024], P(None, ('dp', 'fsdp'))
- new_moment2_norm: float32 [4, 1024], P(None, ('dp', 'fsdp'))
- trust_ratios: float32 [10], replicated
Inputs may be any that keep to these rules, and one draw needn't show every extreme that they name: The first 3 entries of a row are the lengths of its image latent sets in order; the last is the padding at the row's end. Every row sums to 768 and its largest entry is 512.
All inputs are finite; a program needn't handle non-finite values.
Results may differ from a plain program's by a relative error of at most 0.012.
The roundings to bfloat16 on the way count: a program that leaves them out, or rounds other values in their place, can miss the bound.
Values may be sent and summed in bfloat16 or wider, within the bound.
No kernel may reach another device: no remote copies, remote signals or barrier semaphores. Data moves between devices by JAX's collectives and lax.ppermute only.
A program may use at most 192 MiB of HBM per device.

v0:
```python
import math

import jax
import jax.numpy as jnp
from jax import lax
from jax.sharding import PartitionSpec as P

HEADS = 8


ln_eps = 1e-05
beta_one = 0.9
beta_two = 0.999
adam_eps = 1e-06
decay_rate = 0.01
adam_step = 100.0
masked_score = -1000000000.0
gelu_coef = 0.7978845608


def segment_ids(lengths_row, row_len):
    set_ends = jnp.cumsum(lengths_row[:-1])
    positions = jnp.arange(row_len, dtype=jnp.int32)
    return jnp.sum((positions[:, None] >= set_ends[None, :]).astype(jnp.int32), axis=1)


def gelu_curve(upward):
    return (
        0.5 * upward * (1.0 + jnp.tanh(gelu_coef * (upward + 0.044715 * upward * upward * upward)))
    )


def norm_parts(value):
    centered = value - jnp.mean(value, -1, keepdims=True)
    inv_std = lax.rsqrt(jnp.mean(centered * centered, -1, keepdims=True) + ln_eps)
    return (centered * inv_std, inv_std)


def norm_back(grad_out, normed, inv_std, gain):
    grad_normed = grad_out * gain
    return inv_std * (
        grad_normed
        - jnp.mean(grad_normed, -1, keepdims=True)
        - normed * jnp.mean(grad_normed * normed, -1, keepdims=True)
    )


def block_scores(q_block, key_heads, seg_block, segment, score_scale):
    scores = (
        jnp.einsum("qhd,khd->hqk", q_block, key_heads, preferred_element_type=jnp.float32)
        * score_scale
    )
    match = seg_block[:, None] == segment[None, :]
    return jnp.where(match[None], scores, masked_score)


def lamb_parts(weight, grad, first, second, sum_axes):
    m_one = beta_one * first + (1.0 - beta_one) * grad
    m_two = beta_two * second + (1.0 - beta_two) * grad * grad
    step_dir = (
        m_one
        / (1.0 - beta_one**adam_step)
        / (jnp.sqrt(m_two / (1.0 - beta_two**adam_step)) + adam_eps)
        + decay_rate * weight
    )
    return (
        m_one,
        m_two,
        step_dir,
        jnp.sum(weight * weight, axis=sum_axes),
        jnp.sum(step_dir * step_dir, axis=sum_axes),
    )


def on_device(
    latents,
    lengths,
    cotangent,
    matrices,
    norm_params,
    moment1_mat,
    moment2_mat,
    moment1_norm,
    moment2_norm,
):
    row_len = latents.shape[1]
    width = latents.shape[2]
    head_dim = width // HEADS
    block_rows = row_len // max(1, row_len // 768)
    set_count = lengths.shape[1] - 1
    score_scale = 1.0 / math.sqrt(head_dim)
    low_mats = matrices.astype(jnp.bfloat16)
    low_norms = norm_params.astype(jnp.bfloat16)
    weights, norms_low = (
        lax.all_gather(low_mats, ("dp", "fsdp"), axis=1, tiled=True),
        lax.all_gather(low_norms, ("dp", "fsdp"), axis=1, tiled=True),
    )
    norm_vals = norms_low.astype(jnp.float32)
    segment = segment_ids(lengths[0], row_len)
    live_rows = (segment < set_count).astype(jnp.float32)[:, None]
    inputs = latents[0].astype(jnp.float32)
    normed_one, inv_one = norm_parts(inputs)
    h_one = (normed_one * norm_vals[0] + norm_vals[1]).astype(jnp.bfloat16)
    qkv = jnp.einsum("td,ide->tie", h_one, weights[:3], preferred_element_type=jnp.float32).astype(
        jnp.bfloat16
    )
    heads_all = qkv.reshape(row_len, 3, HEADS, head_dim)
    queries = heads_all[:, 0]
    key_heads = heads_all[:, 1]
    values = heads_all[:, 2]
    scores = block_scores(queries, key_heads, segment, segment, score_scale)
    row_max = jnp.max(scores, -1, keepdims=True)
    exp_scores = jnp.exp(scores - row_max)
    denom_sum = jnp.sum(exp_scores, -1, keepdims=True)
    probs_low = (exp_scores / denom_sum).astype(jnp.bfloat16)
    block_outs = jnp.einsum("hqk,khd->qhd", probs_low, values, preferred_element_type=jnp.float32)
    block_lse = [row_max + jnp.log(denom_sum)]
    attended = block_outs.reshape(row_len, width).astype(jnp.bfloat16)
    branch = jnp.dot(attended, weights[3], preferred_element_type=jnp.float32)
    middle = inputs + live_rows * branch
    normed_two, inv_two = norm_parts(middle)
    h_two = (normed_two * norm_vals[2] + norm_vals[3]).astype(jnp.bfloat16)
    upward = jnp.dot(h_two, weights[4], preferred_element_type=jnp.float32)
    activ, gelu_pull = jax.vjp(gelu_curve, upward)
    activ_low = activ.astype(jnp.bfloat16)
    result = middle + live_rows * jnp.dot(activ_low, weights[5], preferred_element_type=jnp.float32)
    weights_back, norms_back = (
        lax.all_gather(low_mats, ("dp", "fsdp"), axis=1, tiled=True),
        lax.all_gather(low_norms, ("dp", "fsdp"), axis=1, tiled=True),
    )
    gains_back = norms_back.astype(jnp.float32)
    grad_out = cotangent[0].astype(jnp.float32)
    grad_mlp = (live_rows * grad_out).astype(jnp.bfloat16)
    grad_five = jnp.einsum("tf,td->fd", activ_low, grad_mlp, preferred_element_type=jnp.float32)
    grad_activ = jnp.einsum(
        "td,fd->tf", grad_mlp, weights_back[5], preferred_element_type=jnp.float32
    )
    grad_up = gelu_pull(grad_activ)[0].astype(jnp.bfloat16)
    grad_four = jnp.einsum("te,tf->ef", h_two, grad_up, preferred_element_type=jnp.float32)
    grad_htwo = jnp.einsum(
        "tf,ef->te", grad_up, weights_back[4], preferred_element_type=jnp.float32
    )
    gain_two = jnp.sum(grad_htwo * normed_two, 0)
    shift_two = jnp.sum(grad_htwo, 0)
    grad_middle = grad_out + norm_back(grad_htwo, normed_two, inv_two, gains_back[2])
    mlp_mats_local = jnp.stack([grad_four, grad_five])
    mlp_norms_local = jnp.stack([gain_two, shift_two])
    grad_branch = (live_rows * grad_middle).astype(jnp.bfloat16)
    grad_three = jnp.einsum("te,td->ed", attended, grad_branch, preferred_element_type=jnp.float32)
    grad_attn = jnp.einsum(
        "td,ed->te", grad_branch, weights_back[3], preferred_element_type=jnp.float32
    )
    grad_attn = grad_attn.astype(jnp.bfloat16).reshape(row_len, HEADS, head_dim)
    grad_q_parts = []
    grad_keys = jnp.zeros((row_len, HEADS, head_dim), jnp.float32)
    grad_values = jnp.zeros((row_len, HEADS, head_dim), jnp.float32)
    for number, offset in enumerate(range(0, row_len, block_rows)):
        scores = block_scores(queries, key_heads, segment, segment, score_scale)
        probs = jnp.exp(scores - block_lse[number])
        probs_low = probs.astype(jnp.bfloat16)
        grad_values = jnp.einsum(
            "hqk,qhd->khd", probs_low, grad_attn, preferred_element_type=jnp.float32
        )
        grad_probs = jnp.einsum(
            "qhd,khd->hqk", grad_attn, values, preferred_element_type=jnp.float32
        )
        row_dot = jnp.sum(grad_probs * probs, -1, keepdims=True)
        grad_scores = (probs * (grad_probs - row_dot)).astype(jnp.bfloat16)
        grad_q_parts.append(
            jnp.einsum("hqk,khd->qhd", grad_scores, key_heads, preferred_element_type=jnp.float32)
            * score_scale
        )
        grad_keys = (
            jnp.einsum("hqk,qhd->khd", grad_scores, queries, preferred_element_type=jnp.float32)
            * score_scale
        )
    grad_queries = grad_q_parts[0]
    grad_qkv = (
        jnp.stack([grad_queries, grad_keys, grad_values], 1)
        .reshape(row_len, 3, width)
        .astype(jnp.bfloat16)
    )
    grad_proj = jnp.einsum("td,tie->ide", h_one, grad_qkv, preferred_element_type=jnp.float32)
    grad_hone = jnp.einsum(
        "tie,ide->td", grad_qkv, weights_back[:3], preferred_element_type=jnp.float32
    )
    gain_one = jnp.sum(grad_hone * normed_one, 0)
    shift_one = jnp.sum(grad_hone, 0)
    grad_input = grad_middle + norm_back(grad_hone, normed_one, inv_one, gains_back[0])
    attn_mats_local = jnp.concatenate([grad_proj, grad_three[None]], 0)
    attn_norms_local = jnp.stack([gain_one, shift_one])
    attn_mats, attn_norms = (
        lax.psum_scatter(attn_mats_local, ("dp", "fsdp"), scatter_dimension=1, tiled=True),
        lax.psum_scatter(attn_norms_local, ("dp", "fsdp"), scatter_dimension=1, tiled=True),
    )
    mlp_mats, mlp_norms = (
        lax.psum_scatter(mlp_mats_local, ("dp", "fsdp"), scatter_dimension=1, tiled=True),
        lax.psum_scatter(mlp_norms_local, ("dp", "fsdp"), scatter_dimension=1, tiled=True),
    )
    grad_mats = jnp.concatenate([attn_mats, mlp_mats], 0)
    grad_norms = jnp.concatenate([attn_norms, mlp_norms], 0)
    m1_mat, m2_mat, dir_mat, wsq_mat, usq_mat = lamb_parts(
        matrices, grad_mats, moment1_mat, moment2_mat, (1, 2)
    )
    m1_norm, m2_norm, dir_norm, wsq_norm, usq_norm = lamb_parts(
        norm_params, grad_norms, moment1_norm, moment2_norm, (1,)
    )
    weight_sq, update_sq = lax.psum(
        (jnp.concatenate([wsq_mat, wsq_norm]), jnp.concatenate([usq_mat, usq_norm])), ("dp", "fsdp")
    )
    ratios = jnp.sqrt(weight_sq) / jnp.sqrt(update_sq)
    scaled_mats = ratios[:6][:, None, None] * dir_mat
    scaled_norms = ratios[6:][:, None] * dir_norm
    return (
        result.astype(jnp.bfloat16)[None],
        grad_input.astype(jnp.bfloat16)[None],
        grad_mats,
        grad_norms,
        scaled_mats,
        scaled_norms,
        m1_mat,
        m2_mat,
        m1_norm,
        m2_norm,
        ratios,
    )


def solution(mesh):
    return jax.shard_map(
        on_device,
        mesh=mesh,
        in_specs=(
            P(("dp", "fsdp"), None, None),
            P(("dp", "fsdp"), None),
            P(("dp", "fsdp"), None, None),
            P(None, ("dp", "fsdp"), None),
            P(None, ("dp", "fsdp")),
            P(None, ("dp", "fsdp"), None),
            P(None, ("dp", "fsdp"), None),
            P(None, ("dp", "fsdp")),
            P(None, ("dp", "fsdp")),
        ),
        out_specs=(
            P(("dp", "fsdp"), None, None),
            P(("dp", "fsdp"), None, None),
            P(None, ("dp", "fsdp"), None),
            P(None, ("dp", "fsdp")),
            P(None, ("dp", "fsdp"), None),
            P(None, ("dp", "fsdp")),
            P(None, ("dp", "fsdp"), None),
            P(None, ("dp", "fsdp"), None),
            P(None, ("dp", "fsdp")),
            P(None, ("dp", "fsdp")),
            P(),
        ),
        check_vma=False,
    )
```

profile of v0, /device:TPU:0, one launch (start us, length us, event | category | flops | bytes accessed | tf_op | source)
XLA Modules:
  0.0 966.6 jit_solution(15879115312450331735)
XLA Ops:
  7.2 2.9 multiply_reduce_fusion.6
  10.2 1.4 multiply_reduce_fusion.8
  11.6 70.4 %all-gather = bf16[32,32,4]{1,2,0:T(4,128)(2,1)S(1)} all-gather(bf16[1,32,4]{1,2,0:T(4,128)(2,1)S(1)} %get-tuple-element.64), channel_id=1, replica_groups=mesh['dp'=8,'fsdp'=4] {'dp','fsdp'}, dimensions={0}, use_global_device_ids=true | all-gather | bytes 8448 | tf_op jit(solution)/shard_map/all_gather | solution.py:96
  83.0 1.7 convert_reduce_fusion
  85.4 1.2 broadcast_compare_fusion
  86.6 23.7 %all-gather.3.cloned.1.call-done = bf16[6,1024,1024]{2,1,0:T(8,128)(2,1)} async-done(((bf16[6,32,1024]{2,1,0:T(8,128)(2,1)}), bf16[6,1024,1024]{2,1,0:T(8,128)(2,1)}) %all-gather.3.cloned.1.call-update) | async-done | bytes 12582928 | tf_op jit(solution)/shard_map/all_gather | solution.py:95
  110.3 8.4 fusion.37
  118.7 1.2 copy.156
  119.9 2.0 fusion.69
  121.9 3.5 copy.152
  125.4 10.0 %fusion.71 = (f32[8,768]{1,0:T(8,128)S(1)}, f32[8,768,768]{1,2,0:T(8,128)}) fusion(bf16[768,1,8,128]{3,2,0,1:T(8,128)(2,1)S(1)} %get-tuple-element.55, bf16[768,1,8,128]{3,2,0,1:T(8,128)(2,1)} %get-tuple-element.56, pred[768,768]{0,1:T(8,128)(4,1)} %broadcast_compare_fusion), kind=kOutput, calls=%fused_computation.137 | convolution fusion | flops 1222109184 | bytes 22634496 | tf_op jit(solution)/shard_map/qhd,khd->hqk/dot_general | solution.py:50
  135.4 9.0 fusion
  144.4 8.9 fusion.46
  153.4 4.2 fusion.72
  158.1 4.1 fusion.43
  162.3 3.9 fusion.34
  166.2 2.4 multiply_reduce_fusion.1
  168.6 1.3 fusion.11
  169.9 1.7 copy-done.3
  171.6 3.0 fusion.45
  174.6 13.0 %copy.155 = bf16[768,1024]{0,1:T(8,128)(2,1)S(1)} copy(bf16[768,1024]{1,0:T(8,128)(2,1)} %fusion.45) | data formatting | bytes 3145728 | tf_op jit(solution)/shard_map/reshape | solution.py:153
  187.6 10.9 %fusion.47 = bf16[8,128,768]{2,1,0:T(8,128)(2,1)} fusion(bf16[768,8,128]{0,2,1:T(8,128)(2,1)S(1)} %bitcast.174, f32[8,768,768]{1,2,0:T(8,128)} %get-tuple-element.66, f32[8,768]{1,0:T(8,128)S(1)} %log_add_fusion), kind=kOutput, calls=%fused_computation.81 | convolution fusion | flops 1218183168 | bytes 22044672 | tf_op jit(solution)/shard_map/hqk,qhd->khd/dot_general | solution.py:161
  198.5 11.9 %multiply_reduce_fusion = (f32[8,768]{1,0:T(8,128)S(1)}, f32[8,768,768]{1,2,0:T(8,128)}) fusion(f32[8,768,768]{1,2,0:T(8,128)} %get-tuple-element.66, f32[8,768]{1,0:T(8,128)S(1)} %log_add_fusion, bf16[768,8,128]{0,2,1:T(8,128)(2,1)S(1)} %bitcast.175, bf16[768,1,8,128]{0,3,2,1:T(8,128)(2,1)S(1)} %copy-done.9), kind=kOutput, calls=%fused_computation.1 | convolution fusion | flops 1222109184 | bytes 40943616 | tf_op jit(solution)/shard_map/qhd,khd->hqk/dot_general | solution.py:164
  210.4 12.9 %multiply_convert_fusion = bf16[8,768,768]{1,2,0:T(8,128)(2,1)S(1)} fusion(f32[8,768,768]{1,2,0:T(8,128)} %get-tuple-element.71, f32[8,768,768]{1,2,0:T(8,128)} %get-tuple-element.66, f32[8,768]{1,0:T(8,128)S(1)} %get-tuple-element.70, f32[8,768]{1,0:T(8,128)S(1)} %log_add_fusion), kind=kLoop, calls=%fused_computation | loop fusion | flops 18874368 | bytes 47235072 | tf_op jit(solution)/shard_map/convert_element_type | solution.py:168
  223.4 4.4 multiply_convert_fusion.1
  227.8 1.6 multiply_convert_fusion.2
  230.2 4.0 convolution_bitcast_fusion.3
  234.2 4.3 convolution_bitcast_fusion.1
  238.5 4.1 convolution_bitcast_fusion.2
  242.6 2.6 copy.132
  245.2 2.6 copy.131
  247.8 1.7 copy.130
  250.6 7.9 convolution_bitcast_fusion
  258.5 6.8 pad_maximum_fusion
  265.4 10.0 %fusion.27 = (f32[1024]{0:T(1024)S(1)}, f32[768]{0:T(1024)S(1)}, f32[768]{0:T(1024)S(1)}, f32[1024]{0:T(1024)S(1)}, f32[768,1024,1]{1,0,2:T(8,128)}) fusion(bf16[1,768,1024]{2,1,0:T(8,128)(2,1)S(1)} %copy-done, f32[768]{0:T(1024)S(1)} %add_rsqrt_fusion.1, f32[768]{0:T(1024)S(1)} %broadcast_multiply_fusion.6, f32[1024]{0:T(1024)S(1)} %bitcast.189, ...), kind=kOutput, calls=%fused_computation.44 | convolution fusion | flops 4844417024 | bytes 15753216 | tf_op jit(solution)/shard_map/tie,ide->td/dot_general | solution.py:184
  276.4 8.4 pad_maximum_fusion.1
  284.8 20.5 %copy.135 = f32[4,1024,1024]{2,0,1:T(4,128)} copy(f32[4,1024,1024]{1,2,0:T(8,128)} %pad_maximum_fusion) | data formatting | bytes 33554432 | tf_op jit(solution)/shard_map/concatenate | solution.py:190
  305.3 15.4 %copy.136 = f32[2,1024,1024]{2,0,1:T(2,128)} copy(f32[2,1024,1024]{2,1,0:T(8,128)} %pad_maximum_fusion.1) | data formatting | bytes 16777216 | tf_op jit(solution)/shard_map/stack | solution.py:146
  321.5 6.7 fusion.60
  328.2 54.9 %reduce-scatter.9.cloned.1.call-done = f32[32,2]{1,0:T(8,128)} async-done(((f32[1024,2]{1,0:T(8,128)}), f32[32,2]{1,0:T(8,128)}) %reduce-scatter.9.cloned.1.call-update) | async-done | bytes 272
  383.9 132.6 %reduce-scatter.7.cloned.1.call-done = f32[32,2]{1,0:T(8,128)} async-done(((f32[1024,2]{1,0:T(8,128)}), f32[32,2]{1,0:T(8,128)}) %reduce-scatter.7.cloned.1.call-update) | async-done | bytes 272
  518.0 391.8 %all-reduce.6.cloned.1.call-done = (f32[4,1024,1024]{2,0,1:T(4,128)}, f32[2,1024,1024]{2,0,1:T(2,128)}) async-done(((f32[4,1024,1024]{2,0,1:T(4,128)}, f32[2,1024,1024]{2,0,1:T(2,128)}), (f32[4,1024,1024]{2,0,1:T(4,128)}, f32[2,1024,1024]{2,0,1:T(2,128)})) %all-reduce.6.cloned.1.call-update) | async-done | bytes 25165840
  909.8 1.1 constant_dynamic-slice_fusion.1
  911.2 1.1 constant_dynamic-slice_fusion
  912.4 3.4 multiply_reduce_fusion.5
  916.0 2.1 fusion.53
  918.1 39.8 %all-reduce.2 = (f32[10]{0:T(128)S(1)}, f32[10]{0:T(128)S(1)}) all-reduce(f32[10]{0:T(128)S(1)} %pad_maximum_fusion.9, f32[10]{0:T(128)S(1)} %pad_maximum_fusion.8), channel_id=1, replica_groups=mesh['dp'=8,'fsdp'=4] {'dp','fsdp'}, use_global_device_ids=true, to_apply=%region_26.27 | all-reduce | flops 20 | bytes 160 | tf_op jit(solution)/shard_map/psum | solution.py:208
  958.0 1.0 broadcast_multiply_fusion
  (109 shorter events, 9.5 us)
Async XLA Ops:
  7.2 77.6 %copy-start = (bf16[1,768,1024]{2,1,0:T(8,128)(2,1)S(1)}, bf16[1,768,1024]{2,1,0:T(8,128)(2,1)}, u32[]{:S(2)}) copy-start(bf16[1,768,1024]{2,1,0:T(8,128)(2,1)} %param.9) | copy-start | bytes 4718596
  7.2 103.1 %all-gather.3.cloned.1.call-start = ((), (), s32[]{:S(2)}) async-start(), calls=%async_computation.2 | async-start | bytes 12976128 | tf_op jit(solution)/shard_map/all_gather | solution.py:95
  10.2 372.9 %reduce-scatter.9.cloned.1.call-start = ((), (), s32[]{:S(2)}) async-start(), calls=%async_computation.4 | async-start | bytes 540672
  121.9 13.5 %copy-start.6 = (bf16[768,1,8,128]{3,2,0,1:T(8,128)(2,1)}, bf16[768,1,8,128]{3,2,0,1:T(8,128)(2,1)S(1)}, u32[]{:S(2)}) copy-start(bf16[768,1,8,128]{3,2,0,1:T(8,128)(2,1)S(1)} %get-tuple-element.55) | copy-start | bytes 4718596
  135.4 9.1 copy-start.8
  153.4 4.3 copy-start.26
  153.4 8.9 slice-start
  153.4 8.9 slice-start.1
  157.6 11.0 %copy-start.1 = (f32[768,1024]{1,0:T(8,128)}, f32[768,1024]{1,0:T(8,128)S(1)}, u32[]{:S(2)}) copy-start(f32[768,1024]{1,0:T(8,128)S(1)} %get-tuple-element.68) | copy-start | bytes 9437188
  158.1 4.1 copy-start.15
  158.1 4.1 slice-start.2
  162.3 4.0 copy-start.28
  166.2 2.4 copy-start.30
  169.9 1.7 copy-start.3
  187.6 10.9 %copy-start.9 = (bf16[768,1,8,128]{0,3,2,1:T(8,128)(2,1)S(1)}, bf16[768,1,8,128]{0,3,2,1:T(8,128)(2,1)}, u32[]{:S(2)}) copy-start(bf16[768,1,8,128]{0,3,2,1:T(8,128)(2,1)} %copy.152) | copy-start | bytes 4718596
  210.4 12.9 %copy-start.10 = (bf16[768,1,8,128]{3,2,0,1:T(8,128)(2,1)S(1)}, bf16[768,1,8,128]{3,2,0,1:T(8,128)(2,1)}, u32[]{:S(2)}) copy-start(bf16[768,1,8,128]{3,2,0,1:T(8,128)(2,1)} %get-tuple-element.56) | copy-start | bytes 4718596
  223.4 4.4 copy-start.7
  227.8 1.9 copy-start.4
  227.8 2.4 copy-start.27
  230.2 4.0 copy-start.16
  230.2 4.0 copy-start.29
  234.2 4.3 copy-start.2
  234.2 4.3 copy-start.31
  250.5 265.9 %reduce-scatter.7.cloned.1.call-start = ((), (), s32[]{:S(2)}) async-start(), calls=%async_computation.3 | async-start | bytes 540672
  250.6 7.9 copy-start.11
  258.5 6.9 copy-start.17
  258.5 6.8 copy-start.18
  258.5 6.8 copy-start.19
  276.4 633.4 %all-reduce.6.cloned.1.call-start = ((), (), s32[]{:S(2)}) async-start(), calls=%async_computation.5 | async-start | bytes 50331648
  320.7 0.7 copy-start.23
  320.7 0.7 copy-start.25
  321.4 195.8 %copy-start.20 = (f32[4,32]{1,0:T(4,128)S(1)}, f32[4,32]{1,0:T(4,128)}, u32[]{:S(2)}) copy-start(f32[4,32]{1,0:T(4,128)} %param.13) | copy-start | bytes 1540
  321.4 195.8 %copy-start.21 = (f32[4,32]{1,0:T(4,128)S(1)}, f32[4,32]{1,0:T(4,128)}, u32[]{:S(2)}) copy-start(f32[4,32]{1,0:T(4,128)} %param.16) | copy-start | bytes 1540
  321.4 195.8 %copy-start.22 = (f32[4,32]{1,0:T(4,128)S(1)}, f32[4,32]{1,0:T(4,128)}, u32[]{:S(2)}) copy-start(f32[4,32]{1,0:T(4,128)} %param.17) | copy-start | bytes 1540
  328.2 584.3 %copy-start.13 = (f32[6,32,1024]{2,1,0:T(8,128)S(1)}, f32[6,32,1024]{2,1,0:T(8,128)}, u32[]{:S(2)}) copy-start(f32[6,32,1024]{2,1,0:T(8,128)} %param.12) | copy-start | bytes 2359300
  911.2 4.8 copy-start.12
  912.3 3.6 copy-start.5
  912.4 3.5 copy-start.14
  957.9 1.8 copy-start.24
Sparse Core Ops, SparseCore 0:
  11.6 98.6 all-gather.2
  250.6 132.3 reduce-scatter.8
  386.0 130.4 reduce-scatter.6
  522.7 387.0 all-reduce.5
where the time goes:
time: 977 us; the launch traced here: 967 us
  waiting for transfers between devices  603 us (62%)
  matrix products  111 us (11%)
  blocking collectives  110 us (11%)
  local copies, waits for them, and re-layouts  72.6 us (7%)
  other arithmetic  55.1 us (6%)
  between operations  14.7 us (2%)
    unnamed x7, waiting for transfers between devices  579 us
    all_gather x1, blocking collectives, on_device(): lax.all_gather(low_norms, ('dp', 'fsdp'), axis=1, tiled=True)  70.4 us
    psum x1, blocking collectives, on_device(): lax.psum((jnp.concatenate([wsq_mat, wsq_norm]), jnp.concatenate([usq_mat,...  39.8 us
    all_gather x1, waiting for transfers between devices, on_device(): lax.all_gather(low_mats, ('dp', 'fsdp'), axis=1, tiled=True)  23.7 us
    concatenate x1, local copies, waits for them, and re-layouts, on_device(): attn_mats_local = jnp.concatenate([grad_proj, grad_three[None]], 0)  20.5 us
  transfers between devices with their start and end apart: 4, of which 4 were waited for; matrix products, arithmetic and copies ran while one was open for 9% of the time, Pallas kernels for 0%

commit v1 on v0

--- a/solution.py
+++ b/solution.py
@@ -3,6 +3,8 @@
 import jax
 import jax.numpy as jnp
 from jax import lax
+from jax.experimental import pallas as pl
+from jax.experimental.pallas import tpu as pltpu
 from jax.sharding import PartitionSpec as P
 
 HEADS = 8
@@ -70,6 +72,120 @@
         jnp.sum(weight * weight, axis=sum_axes),
         jnp.sum(step_dir * step_dir, axis=sum_axes),
     )
+
+
+AXES = ("dp", "fsdp")
+
+
+def swap(value, mask, count):
+    return lax.ppermute(value, AXES, [(i, i ^ mask) for i in range(count)])
+
+
+def device_index():
+    return lax.axis_index("dp") * lax.axis_size("fsdp") + lax.axis_index("fsdp")
+
+
+def hyper_sum(value, count):
+    mask = 1
+    while mask < count:
+        value = value + swap(value, mask, count)
+        mask *= 2
+    return value
+
+
+def gather_part(shard, order, inner, pair, count):
+    parts = [shard] + [swap(shard, k, count) for k in range(1, inner)]
+    masks = list(range(inner))
+    held = jnp.stack(parts)
+    for bit in order:
+        held = jnp.concatenate([held, swap(held, bit, count)])
+        masks = masks + [m ^ bit for m in masks]
+    return masks + [m ^ pair for m in masks], (held, swap(held, pair, count))
+
+
+def place_kernel(rows, layout, me_ref, *refs):
+    out_ref, sem = refs[-2], refs[-1]
+    me = me_ref[0]
+    copies = []
+    for number, (masks, first, column) in enumerate(layout):
+        half = len(masks) // 2
+        for side in range(2):
+            src = refs[2 * number + side]
+            mats, width = src.shape[1], src.shape[3]
+            for j in range(half):
+                row = pl.multiple_of((me ^ masks[side * half + j]) * rows, rows)
+                copies.append(
+                    pltpu.make_async_copy(
+                        src.at[j],
+                        out_ref.at[first : first + mats, pl.ds(row, rows), column : column + width],
+                        sem,
+                    )
+                )
+    for copy in copies:
+        copy.start()
+    for copy in copies:
+        copy.wait()
+
+
+def place(me, parts, mats, rows, count, width):
+    layout = [(masks, first, column) for (masks, _), first, column in parts]
+    arrays = [a for (_, pair), _, _ in parts for a in pair]
+    return pl.pallas_call(
+        lambda *refs: place_kernel(rows, layout, *refs),
+        out_shape=jax.ShapeDtypeStruct((mats, rows * count, width), jnp.bfloat16),
+        in_specs=[pl.BlockSpec(memory_space=pltpu.SMEM)]
+        + [pl.BlockSpec(memory_space=pl.ANY)] * len(arrays),
+        out_specs=pl.BlockSpec(memory_space=pl.ANY),
+        scratch_shapes=[pltpu.SemaphoreType.DMA],
+    )(me, *arrays)
+
+
+def split_kernel(rows, masks, column, width, me_ref, src_ref, send_ref, keep_ref, sem):
+    me = me_ref[0]
+    half = len(masks) // 2
+    copies = []
+    for number, mask in enumerate(masks):
+        row = pl.multiple_of((me ^ mask) * rows, rows)
+        dst = keep_ref.at[number] if number < half else send_ref.at[number - half]
+        copies.append(
+            pltpu.make_async_copy(
+                src_ref.at[:, pl.ds(row, rows), column : column + width], dst, sem
+            )
+        )
+    for copy in copies:
+        copy.start()
+    for copy in copies:
+        copy.wait()
+
+
+def scatter_part(me, grads, column, width, order, inner, pair, count):
+    rows = grads.shape[1] // count
+    masks = list(range(inner))
+    for bit in order[::-1]:
+        masks = masks + [m ^ bit for m in masks]
+    masks = masks + [m ^ pair for m in masks]
+    half = len(masks) // 2
+    shape = jax.ShapeDtypeStruct((half, grads.shape[0], rows, width), jnp.bfloat16)
+    send, keep = pl.pallas_call(
+        lambda *refs: split_kernel(rows, masks, column, width, *refs),
+        out_shape=(shape, shape),
+        in_specs=[
+            pl.BlockSpec(memory_space=pltpu.SMEM),
+            pl.BlockSpec(memory_space=pl.ANY),
+        ],
+        out_specs=[pl.BlockSpec(memory_space=pl.ANY)] * 2,
+        scratch_shapes=[pltpu.SemaphoreType.DMA],
+    )(me, grads)
+    taken = swap(send, pair, count)
+    held = keep.astype(jnp.float32) + taken.astype(jnp.float32)
+    for bit in order:
+        size = held.shape[0] // 2
+        taken = swap(held[size:].astype(jnp.bfloat16), bit, count)
+        held = held[:size] + taken.astype(jnp.float32)
+    total = held[0]
+    for k in range(1, inner):
+        total = total + swap(held[k].astype(jnp.bfloat16), k, count).astype(jnp.float32)
+    return total
 
 
 def on_device(
@@ -91,10 +207,28 @@
     score_scale = 1.0 / math.sqrt(head_dim)
     low_mats = matrices.astype(jnp.bfloat16)
     low_norms = norm_params.astype(jnp.bfloat16)
-    weights, norms_low = (
-        lax.all_gather(low_mats, ("dp", "fsdp"), axis=1, tiled=True),
-        lax.all_gather(low_norms, ("dp", "fsdp"), axis=1, tiled=True),
-    )
+    dp, fsdp = lax.axis_size("dp"), lax.axis_size("fsdp")
+    count = dp * fsdp
+    rows = matrices.shape[1]
+    index = device_index()
+    me = index.astype(jnp.int32)[None]
+    ring = dp == 8 and fsdp == 4 and rows % 16 == 0
+    half_w = width // 2
+    if ring:
+        inner, pair, first_bit, second_bit = fsdp, fsdp, 2 * fsdp, 4 * fsdp
+        parts = []
+        for first in (0, 3):
+            for column, order in ((0, (first_bit, second_bit)), (half_w, (second_bit, first_bit))):
+                shard = low_mats[first : first + 3, :, column : column + half_w]
+                parts.append((gather_part(shard, order, inner, pair, count), first, column))
+        weights = place(me, parts, 6, rows, count, width)
+        spread = jnp.zeros((4, width), jnp.bfloat16)
+        spread = lax.dynamic_update_slice(spread, low_norms, (0, index * rows))
+        norms_low = hyper_sum(spread, count)
+    else:
+        weights = lax.all_gather(low_mats, AXES, axis=1, tiled=True)
+        norms_low = lax.all_gather(low_norms, AXES, axis=1, tiled=True)
+    weights_back = weights
     norm_vals = norms_low.astype(jnp.float32)
     segment = segment_ids(lengths[0], row_len)
     live_rows = (segment < set_count).astype(jnp.float32)[:, None]
@@ -124,11 +258,7 @@
     activ, gelu_pull = jax.vjp(gelu_curve, upward)
     activ_low = activ.astype(jnp.bfloat16)
     result = middle + live_rows * jnp.dot(activ_low, weights[5], preferred_element_type=jnp.float32)
-    weights_back, norms_back = (
-        lax.all_gather(low_mats, ("dp", "fsdp"), axis=1, tiled=True),
-        lax.all_gather(low_norms, ("dp", "fsdp"), axis=1, tiled=True),
-    )
-    gains_back = norms_back.astype(jnp.float32)
+    gains_back = norm_vals
     grad_out = cotangent[0].astype(jnp.float32)
     grad_mlp = (live_rows * grad_out).astype(jnp.bfloat16)
     grad_five = jnp.einsum("tf,td->fd", activ_low, grad_mlp, preferred_element_type=jnp.float32)
@@ -189,25 +319,42 @@
     grad_input = grad_middle + norm_back(grad_hone, normed_one, inv_one, gains_back[0])
     attn_mats_local = jnp.concatenate([grad_proj, grad_three[None]], 0)
     attn_norms_local = jnp.stack([gain_one, shift_one])
-    attn_mats, attn_norms = (
-        lax.psum_scatter(attn_mats_local, ("dp", "fsdp"), scatter_dimension=1, tiled=True),
-        lax.psum_scatter(attn_norms_local, ("dp", "fsdp"), scatter_dimension=1, tiled=True),
-    )
-    mlp_mats, mlp_norms = (
-        lax.psum_scatter(mlp_mats_local, ("dp", "fsdp"), scatter_dimension=1, tiled=True),
-        lax.psum_scatter(mlp_norms_local, ("dp", "fsdp"), scatter_dimension=1, tiled=True),
-    )
-    grad_mats = jnp.concatenate([attn_mats, mlp_mats], 0)
-    grad_norms = jnp.concatenate([attn_norms, mlp_norms], 0)
+    norms_local = jnp.concatenate([attn_norms_local, mlp_norms_local], 0)
+    if ring:
+        pieces = []
+        for local in (attn_mats_local[:3], jnp.concatenate([grad_three[None], mlp_mats_local], 0)):
+            low_grads = local.astype(jnp.bfloat16)
+            pieces.append(
+                jnp.concatenate(
+                    [
+                        scatter_part(me, low_grads, column, half_w, order, inner, pair, count)
+                        for column, order in (
+                            (0, (second_bit, first_bit)),
+                            (half_w, (first_bit, second_bit)),
+                        )
+                    ],
+                    -1,
+                )
+            )
+        grad_mats = jnp.concatenate(pieces, 0)
+        grad_norms = lax.dynamic_slice(
+            hyper_sum(norms_local, count), (0, index * rows), (4, rows)
+        )
+    else:
+        mats_local = jnp.concatenate([attn_mats_local, mlp_mats_local], 0)
+        grad_mats = lax.psum_scatter(mats_local, AXES, scatter_dimension=1, tiled=True)
+        grad_norms = lax.psum_scatter(norms_local, AXES, scatter_dimension=1, tiled=True)
     m1_mat, m2_mat, dir_mat, wsq_mat, usq_mat = lamb_parts(
         matrices, grad_mats, moment1_mat, moment2_mat, (1, 2)
     )
     m1_norm, m2_norm, dir_norm, wsq_norm, usq_norm = lamb_parts(
         norm_params, grad_norms, moment1_norm, moment2_norm, (1,)
     )
-    weight_sq, update_sq = lax.psum(
-        (jnp.concatenate([wsq_mat, wsq_norm]), jnp.concatenate([usq_mat, usq_norm])), ("dp", "fsdp")
-    )
+    squares = jnp.stack(
+        [jnp.concatenate([wsq_mat, wsq_norm]), jnp.concatenate([usq_mat, usq_norm])]
+    )
+    squares = hyper_sum(squares, count) if ring else lax.psum(squares, AXES)
+    weight_sq, update_sq = squares[0], squares[1]
     ratios = jnp.sqrt(weight_sq) / jnp.sqrt(update_sq)
     scaled_mats = ratios[:6][:, None, None] * dir_mat
     scaled_norms = ratios[6:][:, None] * dir_norm

time: 977 us -> 1150 us (1.18)
  Pallas kernels: 0 us -> 768 us
  waiting for transfers between devices: 603 us -> 108 us
  blocking collectives: 110 us -> 0 us
  starting transfers between devices: 0.16 us -> 77.2 us
  local copies, waits for them, and re-layouts: 72.6 us -> 36.9 us
  between operations: 14.7 us -> 2.18 us
    pallas_call x0 -> x5, Pallas kernels: none -> 768 us  [the longest x4 386 us: scatter_part(): pl.pallas_call(lambda *refs: split_kernel(rows, masks, column, width, *re...]
    unnamed x7 -> x0, waiting for transfers between devices: 579 us -> none
    ppermute x0 -> x63, waiting for transfers between devices: none -> 108 us  [swap(): return lax.ppermute(value, AXES, [(i, i ^ mask) for i in range(count)])]
    ppermute x0 -> x63, starting transfers between devices: none -> 77.2 us  [swap(): return lax.ppermute(value, AXES, [(i, i ^ mask) for i in range(count)])]
    all_gather x1 -> x0, blocking collectives: 70.4 us -> none  [on_device(): lax.all_gather(low_norms, ('dp', 'fsdp'), axis=1, tiled=True)]
    psum x1 -> x0, blocking collectives: 39.8 us -> none  [on_device(): lax.psum((jnp.concatenate([wsq_mat, wsq_norm]), jnp.concatenate([usq_mat,...]
    all_gather x1 -> x0, waiting for transfers between devices: 23.7 us -> none  [on_device(): lax.all_gather(low_mats, ('dp', 'fsdp'), axis=1, tiled=True)]
    another operation x2, local copies, waits for them, and re-layouts: 16 us -> 0.08 us  [the longest x1 0.08 us: gather_part(): held = jnp.stack(parts)]
  transfers between devices with their start and end apart: 4 -> 63, of which waited for: 4 -> 27; matrix products, arithmetic and copies ran while one was open for 9% -> 6% of each run, Pallas kernels for 0% -> 17%
where the time goes in v1:
time: 1150 us; the launch traced here: 1140 us
  Pallas kernels  768 us (67%)
  waiting for transfers between devices  108 us (9%)
  matrix products  104 us (9%)
  starting transfers between devices  77.2 us (7%)
  other arithmetic  48.6 us (4%)
  local copies, waits for them, and re-layouts  36.9 us (3%)
    pallas_call x4, Pallas kernels, scatter_part(): pl.pallas_call(lambda *refs: split_kernel(rows, masks, column, width, *re...  386 us
    pallas_call x1, Pallas kernels, place(): pl.pallas_call(lambda *refs: place_kernel(rows, layout, *refs), out_shape...  382 us
    ppermute x63, waiting for transfers between devices, swap(): return lax.ppermute(value, AXES, [(i, i ^ mask) for i in range(count)])  108 us
    ppermute x63, starting transfers between devices, swap(): return lax.ppermute(value, AXES, [(i, i ^ mask) for i in range(count)])  77.2 us
  transfers between devices with their start and end apart: 63, of which 27 were waited for; matrix products, arithmetic and copies ran while one was open for 6% of the time, Pallas kernels for 17%

profile of v1, /device:TPU:0, one launch (start us, length us, event | category | flops | bytes accessed | tf_op | source)
XLA Modules:
  0.0 1144.4 jit_solution(6301895208617360977)
XLA Ops:
  2.8 4.1 collective-permute-start.24
  9.0 3.9 collective-permute-start.13
  14.6 2.7 collective-permute-done.12
  17.3 4.5 collective-permute-start.25
  22.4 3.9 collective-permute-start.19
  26.3 3.4 collective-permute-start.5
  29.7 3.8 collective-permute-done.18
  33.5 3.0 collective-permute-start.7
  53.1 6.2 collective-permute-done.8
  67.2 9.0 collective-permute-done.27
  78.3 2.7 collective-permute-done.9
  83.1 7.8 collective-permute-done.15
  96.5 3.1 collective-permute-done.1
  108.4 382.3 %shard_map.176 = bf16[6,1024,1024]{2,1,0:T(8,128)(2,1)} custom-call(s32[1]{0:T(128)} %bitcast.6.refs_0_, bf16[16,3,32,512]{3,2,1,0:T(8,128)(2,1)} %constant_dynamic-update-slice_fusion.5.refs_1_, bf16[16,3,32,512]{3,2,1,0:T(8,128)(2,1)} %collective-permute-done.10.refs_2_, bf16[16,3,32,512]{3,2,1,0:T(8,128)(2,1)} %constant_dynamic-update-slice_fusion.16.refs_3_, ...), custom_call_target="tpu_custom_call" | custom-call | tf_op jit(solution)/shard_map/pallas_call | solution.py:133
  490.6 8.4 fusion.37
  502.2 3.5 copy.63
  505.8 10.3 fusion.89
  516.1 9.0 fusion
  525.2 8.7 fusion.46
  533.9 3.8 fusion.90
  538.1 4.1 fusion.43
  542.3 3.9 fusion.34
  550.8 2.6 multiply_reduce_fusion.1
  556.6 3.0 fusion.45
  559.5 3.2 pad_maximum_fusion.refs_1_
  562.7 96.4 %shard_map.180 = (bf16[16,3,32,512]{3,2,1,0:T(8,128)(2,1)}, bf16[16,3,32,512]{3,2,1,0:T(8,128)(2,1)}) custom-call(s32[1]{0:T(128)} %bitcast.6.refs_0_, bf16[3,1024,1024]{2,1,0:T(8,128)(2,1)} %pad_maximum_fusion.refs_1_), custom_call_target="tpu_custom_call" | custom-call | tf_op jit(solution)/shard_map/pallas_call | solution.py:169
  659.1 96.4 %shard_map.179 = (bf16[16,3,32,512]{3,2,1,0:T(8,128)(2,1)}, bf16[16,3,32,512]{3,2,1,0:T(8,128)(2,1)}) custom-call(s32[1]{0:T(128)} %bitcast.6.refs_0_, bf16[3,1024,1024]{2,1,0:T(8,128)(2,1)} %pad_maximum_fusion.refs_1_), custom_call_target="tpu_custom_call" | custom-call | tf_op jit(solution)/shard_map/pallas_call | solution.py:169
  757.3 10.9 fusion.47
  768.2 12.0 %multiply_reduce_fusion = (f32[8,768]{1,0:T(8,128)S(1)}, f32[8,768,768]{1,2,0:T(8,128)}) fusion(f32[8,768,768]{1,2,0:T(8,128)} %get-tuple-element.125, f32[8,768]{1,0:T(8,128)S(1)} %log_add_fusion, bf16[768,8,128]{0,2,1:T(8,128)(2,1)S(1)} %bitcast.282, bf16[768,1,8,128]{0,3,2,1:T(8,128)(2,1)S(1)} %copy-done.8), kind=kOutput, calls=%fused_computation.1 | convolution fusion | flops 1222109184 | bytes 40943616 | tf_op jit(solution)/shard_map/qhd,khd->hqk/dot_general | solution.py:294
  780.2 13.1 %multiply_convert_fusion = bf16[8,768,768]{1,2,0:T(8,128)(2,1)S(1)} fusion(f32[8,768,768]{1,2,0:T(8,128)} %get-tuple-element.130, f32[8,768,768]{1,2,0:T(8,128)} %get-tuple-element.125, f32[8,768]{1,0:T(8,128)S(1)} %get-tuple-element.129, f32[8,768]{1,0:T(8,128)S(1)} %log_add_fusion), kind=kLoop, calls=%fused_computation | loop fusion | flops 18874368 | bytes 47235072 | tf_op jit(solution)/shard_map/convert_element_type | solution.py:298
  793.3 4.4 multiply_convert_fusion.1
  804.1 2.7 copy.50
  806.8 11.1 fusion.27
  820.1 7.9 convert_bitcast_fusion.refs_1_
  828.0 96.4 %shard_map.178 = (bf16[16,3,32,512]{3,2,1,0:T(8,128)(2,1)}, bf16[16,3,32,512]{3,2,1,0:T(8,128)(2,1)}) custom-call(s32[1]{0:T(128)} %bitcast.6.refs_0_, bf16[3,1024,1024]{2,1,0:T(8,128)(2,1)} %convert_bitcast_fusion.refs_1_), custom_call_target="tpu_custom_call" | custom-call | tf_op jit(solution)/shard_map/pallas_call | solution.py:169
  924.6 3.0 collective-permute-start.54
  927.6 96.4 %shard_map.177 = (bf16[16,3,32,512]{3,2,1,0:T(8,128)(2,1)}, bf16[16,3,32,512]{3,2,1,0:T(8,128)(2,1)}) custom-call(s32[1]{0:T(128)} %bitcast.6.refs_0_, bf16[3,1024,1024]{2,1,0:T(8,128)(2,1)} %convert_bitcast_fusion.refs_1_), custom_call_target="tpu_custom_call" | custom-call | tf_op jit(solution)/shard_map/pallas_call | solution.py:169
  1024.7 2.8 collective-permute-done.55
  1047.7 10.9 collective-permute-done.48
  1063.3 12.1 %collective-permute-done.36 = bf16[8,3,32,512]{3,2,1,0:T(8,128)(2,1)S(1)} collective-permute-done((bf16[8,3,32,512]{3,2,1,0:T(8,128)(2,1)S(1)}, bf16[8,3,32,512]{3,2,1,0:T(8,128)(2,1)S(1)}, u32[]{:S(2)}, u32[]{:S(2)}) %collective-permute-start.36) | collective-permute-done | bytes 786464 | tf_op jit(solution)/shard_map/ppermute | solution.py:81
  1080.2 7.5 collective-permute-done.49
  1096.8 2.6 collective-permute-start.38
  1099.4 5.8 collective-permute-done.51
  1105.3 4.4 collective-permute-start.32
  1112.7 7.2 collective-permute-done.39
  1124.6 3.6 collective-permute-done.58
  1128.3 4.9 fusion.60
  1135.0 3.0 collective-permute-done.61
  (286 shorter events, 126.0 us)
Async XLA Ops:
  2.8 19.6 %collective-permute-start.24 = (bf16[3,32,512]{2,1,0:T(8,128)(2,1)S(1)}, bf16[3,32,512]{2,1,0:T(8,128)(2,1)S(1)}, u32[]{:S(2)}, u32[]{:S(2)}) collective-permute-start(bf16[3,32,512]{2,1,0:T(8,128)(2,1)S(1)} %get-tuple-element.84), channel_id=1, source_target_pairs={{0,2},{1,3},{2,0},{3,1},{4,6},{5,7},{6,4},{7,5},{8,10},{9,11},{10,... | collective-permute-start | bytes 294920 | tf_op jit(solution)/shard_map/ppermute | solution.py:81
  6.9 19.4 %collective-permute-start.23 = (bf16[3,32,512]{2,1,0:T(8,128)(2,1)S(1)}, bf16[3,32,512]{2,1,0:T(8,128)(2,1)S(1)}, u32[]{:S(2)}, u32[]{:S(2)}) collective-permute-start(bf16[3,32,512]{2,1,0:T(8,128)(2,1)S(1)} %get-tuple-element.84), channel_id=1, source_target_pairs={{0,1},{1,0},{2,3},{3,2},{4,5},{5,4},{6,7},{7,6},{8,9},{9,8},{10,11... | collective-permute-start | bytes 294920 | tf_op jit(solution)/shard_map/ppermute | solution.py:81
  8.5 8.8 collective-permute-start.12
  8.8 12.9 %collective-permute-start.11 = (bf16[3,32,512]{2,1,0:T(8,128)(2,1)S(1)}, bf16[3,32,512]{2,1,0:T(8,128)(2,1)S(1)}, u32[]{:S(2)}, u32[]{:S(2)}) collective-permute-start(bf16[3,32,512]{2,1,0:T(8,128)(2,1)S(1)} %get-tuple-element.86), channel_id=1, source_target_pairs={{0,1},{1,0},{2,3},{3,2},{4,5},{5,4},{6,7},{7,6},{8,9},{9,8},{10,11... | collective-permute-start | bytes 294920 | tf_op jit(solution)/shard_map/ppermute | solution.py:81
  9.0 12.8 %collective-permute-start.13 = (bf16[3,32,512]{2,1,0:T(8,128)(2,1)S(1)}, bf16[3,32,512]{2,1,0:T(8,128)(2,1)S(1)}, u32[]{:S(2)}, u32[]{:S(2)}) collective-permute-start(bf16[3,32,512]{2,1,0:T(8,128)(2,1)S(1)} %get-tuple-element.86), channel_id=1, source_target_pairs={{0,3},{1,2},{2,1},{3,0},{4,7},{5,6},{6,5},{7,4},{8,11},{9,10},{10,... | collective-permute-start | bytes 294920 | tf_op jit(solution)/shard_map/ppermute | solution.py:81
  17.3 9.0 collective-permute-start.25
  21.8 11.7 %collective-permute-start.18 = (bf16[3,32,512]{2,1,0:T(8,128)(2,1)S(1)}, bf16[3,32,512]{2,1,0:T(8,128)(2,1)S(1)}, u32[]{:S(2)}, u32[]{:S(2)}) collective-permute-start(bf16[3,32,512]{2,1,0:T(8,128)(2,1)S(1)} %get-tuple-element.85), channel_id=1, source_target_pairs={{0,2},{1,3},{2,0},{3,1},{4,6},{5,7},{6,4},{7,5},{8,10},{9,11},{10,... | collective-permute-start | bytes 294920 | tf_op jit(solution)/shard_map/ppermute | solution.py:81
  21.8 14.7 %collective-permute-start.17 = (bf16[3,32,512]{2,1,0:T(8,128)(2,1)S(1)}, bf16[3,32,512]{2,1,0:T(8,128)(2,1)S(1)}, u32[]{:S(2)}, u32[]{:S(2)}) collective-permute-start(bf16[3,32,512]{2,1,0:T(8,128)(2,1)S(1)} %get-tuple-element.85), channel_id=1, source_target_pairs={{0,1},{1,0},{2,3},{3,2},{4,5},{5,4},{6,7},{7,6},{8,9},{9,8},{10,11... | collective-permute-start | bytes 294920 | tf_op jit(solution)/shard_map/ppermute | solution.py:81
  22.4 14.1 %collective-permute-start.19 = (bf16[3,32,512]{2,1,0:T(8,128)(2,1)S(1)}, bf16[3,32,512]{2,1,0:T(8,128)(2,1)S(1)}, u32[]{:S(2)}, u32[]{:S(2)}) collective-permute-start(bf16[3,32,512]{2,1,0:T(8,128)(2,1)S(1)} %get-tuple-element.85), channel_id=1, source_target_pairs={{0,3},{1,2},{2,1},{3,0},{4,7},{5,6},{6,5},{7,4},{8,11},{9,10},{10,... | collective-permute-start | bytes 294920 | tf_op jit(solution)/shard_map/ppermute | solution.py:81
  26.3 12.5 %collective-permute-start.6 = (bf16[3,32,512]{2,1,0:T(8,128)(2,1)S(1)}, bf16[3,32,512]{2,1,0:T(8,128)(2,1)S(1)}, u32[]{:S(2)}, u32[]{:S(2)}) collective-permute-start(bf16[3,32,512]{2,1,0:T(8,128)(2,1)S(1)} %get-tuple-element.87), channel_id=1, source_target_pairs={{0,2},{1,3},{2,0},{3,1},{4,6},{5,7},{6,4},{7,5},{8,10},{9,11},{10,... | collective-permute-start | bytes 294920 | tf_op jit(solution)/shard_map/ppermute | solution.py:81
  26.3 13.9 %collective-permute-start.5 = (bf16[3,32,512]{2,1,0:T(8,128)(2,1)S(1)}, bf16[3,32,512]{2,1,0:T(8,128)(2,1)S(1)}, u32[]{:S(2)}, u32[]{:S(2)}) collective-permute-start(bf16[3,32,512]{2,1,0:T(8,128)(2,1)S(1)} %get-tuple-element.87), channel_id=1, source_target_pairs={{0,1},{1,0},{2,3},{3,2},{4,5},{5,4},{6,7},{7,6},{8,9},{9,8},{10,11... | collective-permute-start | bytes 294920 | tf_op jit(solution)/shard_map/ppermute | solution.py:81
  36.5 58.2 %collective-permute-start = (bf16[4,1024]{1,0:T(4,128)(2,1)S(1)}, bf16[4,1024]{1,0:T(4,128)(2,1)S(1)}, u32[]{:S(2)}, u32[]{:S(2)}) collective-permute-start(bf16[4,1024]{1,0:T(4,128)(2,1)S(1)} %dynamic_update_slice.5), channel_id=1, source_target_pairs={{0,1},{1,0},{2,3},{3,2},{4,5},{5,4},{6,7},{7,6},{8,9},{9,8},{10,11... | collective-permute-start | bytes 24584 | tf_op jit(solution)/shard_map/ppermute | solution.py:81
  36.5 14.1 %collective-permute-start.26 = (bf16[4,3,32,512]{3,2,1,0:T(8,128)(2,1)S(1)}, bf16[4,3,32,512]{3,2,1,0:T(8,128)(2,1)S(1)}, u32[]{:S(2)}, u32[]{:S(2)}) collective-permute-start(bf16[4,3,32,512]{3,2,1,0:T(8,128)(2,1)S(1)} %pad_maximum_fusion.7), channel_id=1, source_target_pairs={{0,16},{1,17},{2,18},{3,19},{4,20},{5,21},{6,22},{7,23},{8,24},{9,... | collective-permute-start | bytes 1179656 | tf_op jit(solution)/shard_map/ppermute | solution.py:81
  38.8 25.4 %collective-permute-start.20 = (bf16[4,3,32,512]{3,2,1,0:T(8,128)(2,1)S(1)}, bf16[4,3,32,512]{3,2,1,0:T(8,128)(2,1)S(1)}, u32[]{:S(2)}, u32[]{:S(2)}) collective-permute-start(bf16[4,3,32,512]{3,2,1,0:T(8,128)(2,1)S(1)} %pad_maximum_fusion.6), channel_id=1, source_target_pairs={{0,8},{1,9},{2,10},{3,11},{4,12},{5,13},{6,14},{7,15},{8,0},{9,1},... | collective-permute-start | bytes 1179656 | tf_op jit(solution)/shard_map/ppermute | solution.py:81
  40.2 21.5 %collective-permute-start.14 = (bf16[4,3,32,512]{3,2,1,0:T(8,128)(2,1)S(1)}, bf16[4,3,32,512]{3,2,1,0:T(8,128)(2,1)S(1)}, u32[]{:S(2)}, u32[]{:S(2)}) collective-permute-start(bf16[4,3,32,512]{3,2,1,0:T(8,128)(2,1)S(1)} %pad_maximum_fusion.5), channel_id=1, source_target_pairs={{0,16},{1,17},{2,18},{3,19},{4,20},{5,21},{6,22},{7,23},{8,24},{9,... | collective-permute-start | bytes 1179656 | tf_op jit(solution)/shard_map/ppermute | solution.py:81
  41.8 17.4 %collective-permute-start.8 = (bf16[4,3,32,512]{3,2,1,0:T(8,128)(2,1)S(1)}, bf16[4,3,32,512]{3,2,1,0:T(8,128)(2,1)S(1)}, u32[]{:S(2)}, u32[]{:S(2)}) collective-permute-start(bf16[4,3,32,512]{3,2,1,0:T(8,128)(2,1)S(1)} %pad_maximum_fusion.4), channel_id=1, source_target_pairs={{0,8},{1,9},{2,10},{3,11},{4,12},{5,13},{6,14},{7,15},{8,0},{9,1},... | collective-permute-start | bytes 1179656 | tf_op jit(solution)/shard_map/ppermute | solution.py:81
  51.6 24.7 %collective-permute-start.27 = (bf16[8,3,32,512]{3,2,1,0:T(8,128)(2,1)}, bf16[8,3,32,512]{3,2,1,0:T(8,128)(2,1)}, u32[]{:S(2)}, u32[]{:S(2)}) collective-permute-start(bf16[8,3,32,512]{3,2,1,0:T(8,128)(2,1)} %get-tuple-element.70), channel_id=1, source_target_pairs={{0,8},{1,9},{2,10},{3,11},{4,12},{5,13},{6,14},{7,15},{8,0},{9,1},... | collective-permute-start | bytes 2359304 | tf_op jit(solution)/shard_map/ppermute | solution.py:81
  60.2 20.8 %collective-permute-start.9 = (bf16[8,3,32,512]{3,2,1,0:T(8,128)(2,1)}, bf16[8,3,32,512]{3,2,1,0:T(8,128)(2,1)}, u32[]{:S(2)}, u32[]{:S(2)}) collective-permute-start(bf16[8,3,32,512]{3,2,1,0:T(8,128)(2,1)} %get-tuple-element.92), channel_id=1, source_target_pairs={{0,16},{1,17},{2,18},{3,19},{4,20},{5,21},{6,22},{7,23},{8,24},{9,... | collective-permute-start | bytes 2359304 | tf_op jit(solution)/shard_map/ppermute | solution.py:81
  62.7 28.2 %collective-permute-start.15 = (bf16[8,3,32,512]{3,2,1,0:T(8,128)(2,1)}, bf16[8,3,32,512]{3,2,1,0:T(8,128)(2,1)}, u32[]{:S(2)}, u32[]{:S(2)}) collective-permute-start(bf16[8,3,32,512]{3,2,1,0:T(8,128)(2,1)} %get-tuple-element.90), channel_id=1, source_target_pairs={{0,8},{1,9},{2,10},{3,11},{4,12},{5,13},{6,14},{7,15},{8,0},{9,1},... | collective-permute-start | bytes 2359304 | tf_op jit(solution)/shard_map/ppermute | solution.py:81
  65.0 28.0 %collective-permute-start.21 = (bf16[8,3,32,512]{3,2,1,0:T(8,128)(2,1)}, bf16[8,3,32,512]{3,2,1,0:T(8,128)(2,1)}, u32[]{:S(2)}, u32[]{:S(2)}) collective-permute-start(bf16[8,3,32,512]{3,2,1,0:T(8,128)(2,1)} %get-tuple-element.88), channel_id=1, source_target_pairs={{0,16},{1,17},{2,18},{3,19},{4,20},{5,21},{6,22},{7,23},{8,24},{9,... | collective-permute-start | bytes 2359304 | tf_op jit(solution)/shard_map/ppermute | solution.py:81
  78.3 30.0 %collective-permute-start.28 = (bf16[16,3,32,512]{3,2,1,0:T(8,128)(2,1)}, bf16[16,3,32,512]{3,2,1,0:T(8,128)(2,1)}, u32[]{:S(2)}, u32[]{:S(2)}) collective-permute-start(bf16[16,3,32,512]{3,2,1,0:T(8,128)(2,1)} %constant_dynamic-update-slice_fusion.38.refs_7_), channel_id=1, source_target_pairs={{0,4},{1,5},{2,6},{3,7},{4,0},{5,1},{6,2},{7,3},{8,12},{9,13},{10,... | collective-permute-start | bytes 4718600 | tf_op jit(solution)/shard_map/ppermute | solution.py:81
  83.1 25.2 %collective-permute-start.10 = (bf16[16,3,32,512]{3,2,1,0:T(8,128)(2,1)}, bf16[16,3,32,512]{3,2,1,0:T(8,128)(2,1)}, u32[]{:S(2)}, u32[]{:S(2)}) collective-permute-start(bf16[16,3,32,512]{3,2,1,0:T(8,128)(2,1)} %constant_dynamic-update-slice_fusion.5.refs_1_), channel_id=1, source_target_pairs={{0,4},{1,5},{2,6},{3,7},{4,0},{5,1},{6,2},{7,3},{8,12},{9,13},{10,... | collective-permute-start | bytes 4718600 | tf_op jit(solution)/shard_map/ppermute | solution.py:81
  93.0 15.3 %collective-permute-start.16 = (bf16[16,3,32,512]{3,2,1,0:T(8,128)(2,1)}, bf16[16,3,32,512]{3,2,1,0:T(8,128)(2,1)}, u32[]{:S(2)}, u32[]{:S(2)}) collective-permute-start(bf16[16,3,32,512]{3,2,1,0:T(8,128)(2,1)} %constant_dynamic-update-slice_fusion.16.refs_3_), channel_id=1, source_target_pairs={{0,4},{1,5},{2,6},{3,7},{4,0},{5,1},{6,2},{7,3},{8,12},{9,13},{10,... | collective-permute-start | bytes 4718600 | tf_op jit(solution)/shard_map/ppermute | solution.py:81
  94.2 14.1 %collective-permute-start.22 = (bf16[16,3,32,512]{3,2,1,0:T(8,128)(2,1)S(1)}, bf16[16,3,32,512]{3,2,1,0:T(8,128)(2,1)}, u32[]{:S(2)}, u32[]{:S(2)}) collective-permute-start(bf16[16,3,32,512]{3,2,1,0:T(8,128)(2,1)S(1)} %constant_dynamic-update-slice_fusion.27.refs_5_), channel_id=1, source_target_pairs={{0,4},{1,5},{2,6},{3,7},{4,0},{5,1},{6,2},{7,3},{8,12},{9,13},{10,... | collective-permute-start | bytes 4718600 | tf_op jit(solution)/shard_map/ppermute | solution.py:81
  801.9 233.8 %collective-permute-start.47 = (bf16[16,3,32,512]{3,2,1,0:T(8,128)(2,1)}, bf16[16,3,32,512]{3,2,1,0:T(8,128)(2,1)}, u32[]{:S(2)}, u32[]{:S(2)}) collective-permute-start(bf16[16,3,32,512]{3,2,1,0:T(8,128)(2,1)} %get-tuple-element.26), channel_id=1, source_target_pairs={{0,4},{1,5},{2,6},{3,7},{4,0},{5,1},{6,2},{7,3},{8,12},{9,13},{10,... | collective-permute-start | bytes 4718600 | tf_op jit(solution)/shard_map/ppermute | solution.py:81
  801.9 237.7 %collective-permute-start.41 = (bf16[16,3,32,512]{3,2,1,0:T(8,128)(2,1)}, bf16[16,3,32,512]{3,2,1,0:T(8,128)(2,1)}, u32[]{:S(2)}, u32[]{:S(2)}) collective-permute-start(bf16[16,3,32,512]{3,2,1,0:T(8,128)(2,1)} %get-tuple-element.24), channel_id=1, source_target_pairs={{0,4},{1,5},{2,6},{3,7},{4,0},{5,1},{6,2},{7,3},{8,12},{9,13},{10,... | collective-permute-start | bytes 4718600 | tf_op jit(solution)/shard_map/ppermute | solution.py:81
  817.9 106.6 %collective-permute-start.53 = (f32[4,1024]{1,0:T(4,128)S(1)}, f32[4,1024]{1,0:T(4,128)S(1)}, u32[]{:S(2)}, u32[]{:S(2)}) collective-permute-start(f32[4,1024]{1,0:T(4,128)S(1)} %pad_maximum_fusion.8), channel_id=1, source_target_pairs={{0,1},{1,0},{2,3},{3,2},{4,5},{5,4},{6,7},{7,6},{8,9},{9,8},{10,11... | collective-permute-start | bytes 49160 | tf_op jit(solution)/shard_map/ppermute | solution.py:81
  924.4 119.0 %collective-permute-start.35 = (bf16[16,3,32,512]{3,2,1,0:T(8,128)(2,1)}, bf16[16,3,32,512]{3,2,1,0:T(8,128)(2,1)}, u32[]{:S(2)}, u32[]{:S(2)}) collective-permute-start(bf16[16,3,32,512]{3,2,1,0:T(8,128)(2,1)} %get-tuple-element.22), channel_id=1, source_target_pairs={{0,4},{1,5},{2,6},{3,7},{4,0},{5,1},{6,2},{7,3},{8,12},{9,13},{10,... | collective-permute-start | bytes 4718600 | tf_op jit(solution)/shard_map/ppermute | solution.py:81
  924.6 99.7 %collective-permute-start.54 = (f32[4,1024]{1,0:T(4,128)S(1)}, f32[4,1024]{1,0:T(4,128)S(1)}, u32[]{:S(2)}, u32[]{:S(2)}) collective-permute-start(f32[4,1024]{1,0:T(4,128)S(1)} %fusion.78), channel_id=1, source_target_pairs={{0,2},{1,3},{2,0},{3,1},{4,6},{5,7},{6,4},{7,5},{8,10},{9,11},{10,... | collective-permute-start | bytes 49160 | tf_op jit(solution)/shard_map/ppermute | solution.py:81
  1024.0 22.3 %collective-permute-start.29 = (bf16[16,3,32,512]{3,2,1,0:T(8,128)(2,1)}, bf16[16,3,32,512]{3,2,1,0:T(8,128)(2,1)S(1)}, u32[]{:S(2)}, u32[]{:S(2)}) collective-permute-start(bf16[16,3,32,512]{3,2,1,0:T(8,128)(2,1)} %get-tuple-element.20), channel_id=1, source_target_pairs={{0,4},{1,5},{2,6},{3,7},{4,0},{5,1},{6,2},{7,3},{8,12},{9,13},{10,... | collective-permute-start | bytes 4718600 | tf_op jit(solution)/shard_map/ppermute | solution.py:81
  1038.0 20.5 %collective-permute-start.48 = (bf16[8,3,32,512]{3,2,1,0:T(8,128)(2,1)S(1)}, bf16[8,3,32,512]{3,2,1,0:T(8,128)(2,1)S(1)}, u32[]{:S(2)}, u32[]{:S(2)}) collective-permute-start(bf16[8,3,32,512]{3,2,1,0:T(8,128)(2,1)S(1)} %slice.384), channel_id=1, source_target_pairs={{0,8},{1,9},{2,10},{3,11},{4,12},{5,13},{6,14},{7,15},{8,0},{9,1},... | collective-permute-start | bytes 2359304 | tf_op jit(solution)/shard_map/ppermute | solution.py:81
  1041.9 20.5 %collective-permute-start.42 = (bf16[8,3,32,512]{3,2,1,0:T(8,128)(2,1)S(1)}, bf16[8,3,32,512]{3,2,1,0:T(8,128)(2,1)S(1)}, u32[]{:S(2)}, u32[]{:S(2)}) collective-permute-start(bf16[8,3,32,512]{3,2,1,0:T(8,128)(2,1)S(1)} %slice.385), channel_id=1, source_target_pairs={{0,16},{1,17},{2,18},{3,19},{4,20},{5,21},{6,22},{7,23},{8,24},{9,... | collective-permute-start | bytes 2359304 | tf_op jit(solution)/shard_map/ppermute | solution.py:81
  1045.7 29.7 %collective-permute-start.36 = (bf16[8,3,32,512]{3,2,1,0:T(8,128)(2,1)S(1)}, bf16[8,3,32,512]{3,2,1,0:T(8,128)(2,1)S(1)}, u32[]{:S(2)}, u32[]{:S(2)}) collective-permute-start(bf16[8,3,32,512]{3,2,1,0:T(8,128)(2,1)S(1)} %slice.386), channel_id=1, source_target_pairs={{0,8},{1,9},{2,10},{3,11},{4,12},{5,13},{6,14},{7,15},{8,0},{9,1},... | collective-permute-start | bytes 2359304 | tf_op jit(solution)/shard_map/ppermute | solution.py:81
  1047.1 32.2 %collective-permute-start.30 = (bf16[8,3,32,512]{3,2,1,0:T(8,128)(2,1)S(1)}, bf16[8,3,32,512]{3,2,1,0:T(8,128)(2,1)S(1)}, u32[]{:S(2)}, u32[]{:S(2)}) collective-permute-start(bf16[8,3,32,512]{3,2,1,0:T(8,128)(2,1)S(1)} %slice.387), channel_id=1, source_target_pairs={{0,16},{1,17},{2,18},{3,19},{4,20},{5,21},{6,22},{7,23},{8,24},{9,... | collective-permute-start | bytes 2359304 | tf_op jit(solution)/shard_map/ppermute | solution.py:81
  1059.0 28.7 %collective-permute-start.49 = (bf16[4,3,32,512]{3,2,1,0:T(8,128)(2,1)S(1)}, bf16[4,3,32,512]{3,2,1,0:T(8,128)(2,1)S(1)}, u32[]{:S(2)}, u32[]{:S(2)}) collective-permute-start(bf16[4,3,32,512]{3,2,1,0:T(8,128)(2,1)S(1)} %slice.388), channel_id=1, source_target_pairs={{0,16},{1,17},{2,18},{3,19},{4,20},{5,21},{6,22},{7,23},{8,24},{9,... | collective-permute-start | bytes 1179656 | tf_op jit(solution)/shard_map/ppermute | solution.py:81
  1062.7 26.7 %collective-permute-start.43 = (bf16[4,3,32,512]{3,2,1,0:T(8,128)(2,1)S(1)}, bf16[4,3,32,512]{3,2,1,0:T(8,128)(2,1)S(1)}, u32[]{:S(2)}, u32[]{:S(2)}) collective-permute-start(bf16[4,3,32,512]{3,2,1,0:T(8,128)(2,1)S(1)} %slice.389), channel_id=1, source_target_pairs={{0,8},{1,9},{2,10},{3,11},{4,12},{5,13},{6,14},{7,15},{8,0},{9,1},... | collective-permute-start | bytes 1179656 | tf_op jit(solution)/shard_map/ppermute | solution.py:81
  1075.8 16.9 %collective-permute-start.37 = (bf16[4,3,32,512]{3,2,1,0:T(8,128)(2,1)S(1)}, bf16[4,3,32,512]{3,2,1,0:T(8,128)(2,1)S(1)}, u32[]{:S(2)}, u32[]{:S(2)}) collective-permute-start(bf16[4,3,32,512]{3,2,1,0:T(8,128)(2,1)S(1)} %slice.390), channel_id=1, source_target_pairs={{0,16},{1,17},{2,18},{3,19},{4,20},{5,21},{6,22},{7,23},{8,24},{9,... | collective-permute-start | bytes 1179656 | tf_op jit(solution)/shard_map/ppermute | solution.py:81
  1079.6 13.4 %collective-permute-start.31 = (bf16[4,3,32,512]{3,2,1,0:T(8,128)(2,1)S(1)}, bf16[4,3,32,512]{3,2,1,0:T(8,128)(2,1)S(1)}, u32[]{:S(2)}, u32[]{:S(2)}) collective-permute-start(bf16[4,3,32,512]{3,2,1,0:T(8,128)(2,1)S(1)} %slice.391), channel_id=1, source_target_pairs={{0,8},{1,9},{2,10},{3,11},{4,12},{5,13},{6,14},{7,15},{8,0},{9,1},... | collective-permute-start | bytes 1179656 | tf_op jit(solution)/shard_map/ppermute | solution.py:81
  1088.0 8.8 collective-permute-start.52
  1089.4 15.7 %collective-permute-start.51 = (bf16[3,32,512]{2,1,0:T(8,128)(2,1)S(1)}, bf16[3,32,512]{2,1,0:T(8,128)(2,1)S(1)}, u32[]{:S(2)}, u32[]{:S(2)}) collective-permute-start(bf16[3,32,512]{2,1,0:T(8,128)(2,1)S(1)} %get-tuple-element.69), channel_id=1, source_target_pairs={{0,2},{1,3},{2,0},{3,1},{4,6},{5,7},{6,4},{7,5},{8,10},{9,11},{10,... | collective-permute-start | bytes 294920 | tf_op jit(solution)/shard_map/ppermute | solution.py:81
  1092.7 12.5 %collective-permute-start.44 = (bf16[3,32,512]{2,1,0:T(8,128)(2,1)S(1)}, bf16[3,32,512]{2,1,0:T(8,128)(2,1)S(1)}, u32[]{:S(2)}, u32[]{:S(2)}) collective-permute-start(bf16[3,32,512]{2,1,0:T(8,128)(2,1)S(1)} %get-tuple-element.64), channel_id=1, source_target_pairs={{0,1},{1,0},{2,3},{3,2},{4,5},{5,4},{6,7},{7,6},{8,9},{9,8},{10,11... | collective-permute-start | bytes 294920 | tf_op jit(solution)/shard_map/ppermute | solution.py:81
  1093.0 12.3 %collective-permute-start.46 = (bf16[3,32,512]{2,1,0:T(8,128)(2,1)S(1)}, bf16[3,32,512]{2,1,0:T(8,128)(2,1)S(1)}, u32[]{:S(2)}, u32[]{:S(2)}) collective-permute-start(bf16[3,32,512]{2,1,0:T(8,128)(2,1)S(1)} %get-tuple-element.65), channel_id=1, source_target_pairs={{0,3},{1,2},{2,1},{3,0},{4,7},{5,6},{6,5},{7,4},{8,11},{9,10},{10,... | collective-permute-start | bytes 294920 | tf_op jit(solution)/shard_map/ppermute | solution.py:81
  1094.6 15.0 %collective-permute-start.45 = (bf16[3,32,512]{2,1,0:T(8,128)(2,1)S(1)}, bf16[3,32,512]{2,1,0:T(8,128)(2,1)S(1)}, u32[]{:S(2)}, u32[]{:S(2)}) collective-permute-start(bf16[3,32,512]{2,1,0:T(8,128)(2,1)S(1)} %get-tuple-element.66), channel_id=1, source_target_pairs={{0,2},{1,3},{2,0},{3,1},{4,6},{5,7},{6,4},{7,5},{8,10},{9,11},{10,... | collective-permute-start | bytes 294920 | tf_op jit(solution)/shard_map/ppermute | solution.py:81
  1096.8 13.6 %collective-permute-start.38 = (bf16[3,32,512]{2,1,0:T(8,128)(2,1)S(1)}, bf16[3,32,512]{2,1,0:T(8,128)(2,1)S(1)}, u32[]{:S(2)}, u32[]{:S(2)}) collective-permute-start(bf16[3,32,512]{2,1,0:T(8,128)(2,1)S(1)} %get-tuple-element.61), channel_id=1, source_target_pairs={{0,1},{1,0},{2,3},{3,2},{4,5},{5,4},{6,7},{7,6},{8,9},{9,8},{10,11... | collective-permute-start | bytes 294920 | tf_op jit(solution)/shard_map/ppermute | solution.py:81
  1105.2 14.7 %collective-permute-start.39 = (bf16[3,32,512]{2,1,0:T(8,128)(2,1)S(1)}, bf16[3,32,512]{2,1,0:T(8,128)(2,1)S(1)}, u32[]{:S(2)}, u32[]{:S(2)}) collective-permute-start(bf16[3,32,512]{2,1,0:T(8,128)(2,1)S(1)} %get-tuple-element.63), channel_id=1, source_target_pairs={{0,2},{1,3},{2,0},{3,1},{4,6},{5,7},{6,4},{7,5},{8,10},{9,11},{10,... | collective-permute-start | bytes 294920 | tf_op jit(solution)/shard_map/ppermute | solution.py:81
  1105.3 14.6 %collective-permute-start.32 = (bf16[3,32,512]{2,1,0:T(8,128)(2,1)S(1)}, bf16[3,32,512]{2,1,0:T(8,128)(2,1)S(1)}, u32[]{:S(2)}, u32[]{:S(2)}) collective-permute-start(bf16[3,32,512]{2,1,0:T(8,128)(2,1)S(1)} %get-tuple-element.58), channel_id=1, source_target_pairs={{0,1},{1,0},{2,3},{3,2},{4,5},{5,4},{6,7},{7,6},{8,9},{9,8},{10,11... | collective-permute-start | bytes 294920 | tf_op jit(solution)/shard_map/ppermute | solution.py:81
  1109.7 10.3 collective-permute-start.34
  1110.4 12.1 %collective-permute-start.33 = (bf16[3,32,512]{2,1,0:T(8,128)(2,1)S(1)}, bf16[3,32,512]{2,1,0:T(8,128)(2,1)S(1)}, u32[]{:S(2)}, u32[]{:S(2)}) collective-permute-start(bf16[3,32,512]{2,1,0:T(8,128)(2,1)S(1)} %get-tuple-element.60), channel_id=1, source_target_pairs={{0,2},{1,3},{2,0},{3,1},{4,6},{5,7},{6,4},{7,5},{8,10},{9,11},{10,... | collective-permute-start | bytes 294920 | tf_op jit(solution)/shard_map/ppermute | solution.py:81
  (50 other events, 1042.5 us)

commit v2 on v0

v2 whole, which is shorter than its diff:
```python
import functools
import math

import jax
import jax.numpy as jnp
from jax import lax
from jax.experimental import pallas as pl
from jax.experimental.pallas import tpu as pltpu
from jax.sharding import PartitionSpec as P

HEADS = 8
AXES = ("dp", "fsdp")
LANES = 128

ln_eps = 1e-05
beta_one = 0.9
beta_two = 0.999
adam_eps = 1e-06
decay_rate = 0.01
adam_step = 100.0
gelu_coef = 0.7978845608
cubic_coef = 0.044715
mask_depth = -1e30

F32 = jnp.float32
LOW = jnp.bfloat16
NT = (((1,), (1,)), ((), ()))
TN = (((0,), (0,)), ((), ()))
SMEM = pl.BlockSpec(memory_space=pltpu.SMEM)
VMEM = pl.BlockSpec(memory_space=pltpu.VMEM)


def params(mib):
    return pltpu.CompilerParams(vmem_limit_bytes=mib * 2**20)


def shape(dims, kind):
    return jax.ShapeDtypeStruct(dims, kind)


def product(left, right, dims=(((1,), (0,)), ((), ()))):
    return lax.dot_general(left, right, dims, preferred_element_type=F32)


def cost(flops, moved):
    return pl.CostEstimate(flops=int(flops), bytes_accessed=int(moved), transcendentals=0)


def whole(array):
    return pl.BlockSpec(
        array.shape, lambda i: (0,) * len(array.shape), pipeline_mode=pl.Buffered(1)
    )


def rows_of(array, block):
    lead = array.shape[:-2]
    return pl.BlockSpec((*lead, block, array.shape[-1]), lambda i: (*(0,) * len(lead), i, 0))


def swap(value, mask, count):
    return lax.ppermute(value, AXES, [(i, i ^ mask) for i in range(count)])


def swap_all(values, bits, count):
    return [swap(v, b, count) for v, b in zip(values, bits)]


def hyper_sum(value, count):
    mask = 1
    while mask < count:
        value = value + swap(value, mask, count)
        mask *= 2
    return value


def after(value, *others):
    return lax.optimization_barrier((value, others))[0]


def mask_order(order, inner):
    masks = list(range(inner))
    for bit in order:
        masks = masks + [m ^ bit for m in masks]
    return masks


def by_columns(shards, parts):
    mats, rows, columns = shards.shape
    blocks = columns // parts // LANES
    split = shards.reshape(mats, rows, parts, blocks, LANES)
    return split.transpose(2, 0, 3, 1, 4).reshape(parts, mats * blocks * rows, LANES)


def normalize(value):
    centered = value - jnp.mean(value, -1, keepdims=True)
    inv_std = lax.rsqrt(jnp.mean(centered * centered, -1, keepdims=True) + ln_eps)
    return centered * inv_std, inv_std


def norm_back(grad_out, normed, inv_std, gain):
    grad_normed = grad_out * gain
    return inv_std * (
        grad_normed
        - jnp.mean(grad_normed, -1, keepdims=True)
        - normed * jnp.mean(grad_normed * normed, -1, keepdims=True)
    )


def place_all(table_ref, layout, rows, refs, out_ref):
    mats = out_ref.shape[0]
    for (line, start, column, blocks), ref in zip(layout, refs):

        @pl.loop(0, ref.shape[0])
        def _(n, line=line, start=start, column=column, blocks=blocks, ref=ref):
            row = pl.multiple_of(table_ref[line, start + n] * rows, rows)
            for j in range(mats):
                for b in range(blocks):
                    first = (j * blocks + b) * rows
                    lane = column + b * LANES
                    out_ref[j, pl.ds(row, rows), lane : lane + LANES] = ref[
                        n, first : first + rows, :
                    ]


def lane_rows(low, first, number):
    lane = lax.broadcasted_iota(jnp.int32, low, 1)
    return (lane >= first) & (lane < first + number)


def spread_norms(table_ref, layout, first_row, refs, held_ref, norm_ref):
    for (line, start, _, _), ref in zip(layout, refs):
        if line == 0:

            @pl.loop(0, ref.shape[0])
            def _(n, line=line, start=start, ref=ref):
                held_ref[pl.ds(table_ref[line, start + n], 1), :] = ref[
                    n, first_row : first_row + 16, :
                ].astype(F32)[0:1]

    near = LANES // 32
    blocks = held_ref.shape[0] // near
    for i in range(4):
        total = jnp.zeros((blocks, LANES), F32)
        for z in range(near):
            value = held_ref[pl.ds(z, blocks, stride=near), :]
            value = pltpu.roll(value, (32 * (z - i)) % LANES, 1)
            total = total + jnp.where(lane_rows(total.shape, 32 * z, 32), value, 0.0)
        for b in range(blocks):
            norm_ref[i : i + 1, b * LANES : (b + 1) * LANES] = total[b : b + 1]


def pack_norms(norms, held_ref):
    near = LANES // 32
    blocks = held_ref.shape[0] // near
    held = [jnp.zeros((blocks, LANES), F32) for _ in range(near)]
    for i, norm in enumerate(norms):
        stacked = jnp.concatenate(
            [norm[:, b * LANES : (b + 1) * LANES] for b in range(blocks)], 0
        )
        for z in range(near):
            value = pltpu.roll(stacked, (32 * (i - z)) % LANES, 1)
            held[z] = held[z] + jnp.where(lane_rows(value.shape, 32 * i, 32), value, 0.0)
    for z in range(near):
        held_ref[pl.ds(z, blocks, stride=near), :] = held[z]


def project_kernel(layout, rows, norm_row, parts, table_ref, x_ref, *refs):
    chunks = refs[:parts]
    hidden_ref, out_ref, norm_ref, weight_ref, held_ref = refs[-5:]
    mats, width, _ = weight_ref.shape

    @pl.when(pl.program_id(0) == 0)
    def _():
        place_all(table_ref, layout, rows, chunks, weight_ref)
        if norm_row is None:
            norm_ref[...] = refs[parts][...]
        else:
            spread_norms(table_ref, layout, norm_row, chunks, held_ref, norm_ref)

    normed, _ = normalize(x_ref[...].astype(F32))
    hidden = (normed * norm_ref[0:1, :] + norm_ref[1:2, :]).astype(LOW)
    hidden_ref[...] = hidden
    for j in range(mats):
        out_ref[:, j * width : (j + 1) * width] = product(hidden, weight_ref[j]).astype(LOW)


def attend_kernel(group, dim, power, q_ref, k_ref, v_ref, in_ref, out_ref, o_ref, lse_ref):
    for g in range(group):
        span = slice(g * dim, (g + 1) * dim)
        keys = jnp.concatenate([k_ref[:, span], out_ref[...]], 1)
        queries = jnp.concatenate([q_ref[:, span], in_ref[...]], 1)
        scores = product(keys, queries, NT)
        top = jnp.max(scores, 0, keepdims=True)
        weight = jnp.exp2((scores - top) * power)
        total = jnp.sum(weight, 0, keepdims=True)
        probs = (weight * (1.0 / total)).astype(LOW)
        o_ref[:, span] = product(v_ref[:, span].T, probs).T.astype(LOW)
        lse_ref[g] = top * power + jnp.log2(total)


def attend_back_kernel(
    group, dim, power, scale,
    q_ref, k_ref, v_ref, do_ref, o_ref, in_ref, out_ref, lse_ref,
    grad_ref,
):
    for g in range(group):
        span = slice(g * dim, (g + 1) * dim)
        queries, keys, grad = q_ref[:, span], k_ref[:, span], do_ref[:, span]
        both = grad.astype(F32) * o_ref[:, span].astype(F32)
        row_dot = lax.dot_general(
            jnp.ones((8, dim), F32), both, NT,
            preferred_element_type=F32, precision=lax.Precision.HIGHEST,
        )[0:1]
        scores = product(
            jnp.concatenate([keys, out_ref[...]], 1),
            jnp.concatenate([queries, in_ref[...]], 1),
            NT,
        )
        probs = jnp.exp2(scores * power - lse_ref[g])
        grad_probs = product(v_ref[:, span], grad, NT)
        grad_scores = (probs * (grad_probs - row_dot)).astype(LOW)
        grad_ref[2, :, span] = product(probs.astype(LOW), grad).astype(LOW)
        grad_ref[1, :, span] = (product(grad_scores, queries) * scale).astype(LOW)
        grad_ref[0, :, span] = (product(keys.T, grad_scores).T * scale).astype(LOW)


def middle_kernel(layout, rows, atts, table_ref, x_ref, dz_ref, live_ref, norm_ref, *refs):
    att_refs, chunks = refs[:atts], refs[atts:-10]
    dnorm_ref, result_ref, dmid_ref, dmlp_ref, hidden_ref = refs[-10:-5]
    dup_ref, act_ref, dbranch_ref, datt_ref, weight_ref = refs[-5:]

    @pl.when(pl.program_id(0) == 0)
    def _():
        place_all(table_ref, layout, rows, chunks, weight_ref)
        dnorm_ref[...] = jnp.zeros_like(dnorm_ref)

    gain, shift = norm_ref[2:3, :], norm_ref[3:4, :]
    live = live_ref[...]
    branch, first = None, 0
    for ref in att_refs:
        part = product(ref[...], weight_ref[0, first : first + ref.shape[1], :])
        branch = part if branch is None else branch + part
        first += ref.shape[1]
    middle = x_ref[...].astype(F32) + live * branch
    normed, inv_std = normalize(middle)
    hidden = (normed * gain + shift).astype(LOW)
    hidden_ref[...] = hidden
    upward = product(hidden, weight_ref[1])
    square = upward * upward
    bend = jnp.tanh(gelu_coef * (upward + cubic_coef * square * upward))
    half = 0.5 * (1.0 + bend)
    active = (upward * half).astype(LOW)
    act_ref[...] = active
    slope = half + (0.5 * gelu_coef) * upward * (1.0 - bend * bend) * (
        1.0 + (3.0 * cubic_coef) * square
    )
    result_ref[...] = (middle + live * product(active, weight_ref[2])).astype(LOW)
    grad = dz_ref[...].astype(F32)
    dmlp = (live * grad).astype(LOW)
    dmlp_ref[...] = dmlp
    dup = (product(dmlp, weight_ref[2], NT) * slope).astype(LOW)
    dup_ref[...] = dup
    dhidden = product(dup, weight_ref[1], NT)
    dnorm_ref[0:1, :] += jnp.sum(dhidden * normed, 0, keepdims=True)
    dnorm_ref[1:2, :] += jnp.sum(dhidden, 0, keepdims=True)
    dmid = grad + norm_back(dhidden, normed, inv_std, gain)
    dmid_ref[...] = dmid
    dbranch = (live * dmid).astype(LOW)
    dbranch_ref[...] = dbranch
    datt_ref[...] = product(dbranch, weight_ref[0], NT).astype(LOW)


def last_kernel(layout, rows, parts, table_ref, x_ref, dmid_ref, norm_ref, *refs):
    chunks, grads = refs[:parts], refs[parts:-3]
    out_ref, dnorm_ref, weight_ref = refs[-3:]
    mats = weight_ref.shape[0]

    @pl.when(pl.program_id(0) == 0)
    def _():
        place_all(table_ref, layout, rows, chunks, weight_ref)
        dnorm_ref[...] = jnp.zeros_like(dnorm_ref)

    total, column = None, 0
    for ref in grads:
        wide = ref.shape[2]
        for j in range(mats):
            part = product(ref[j], weight_ref[j, :, column : column + wide], NT)
            total = part if total is None else total + part
        column += wide
    normed, inv_std = normalize(x_ref[...].astype(F32))
    dnorm_ref[0:1, :] += jnp.sum(total * normed, 0, keepdims=True)
    dnorm_ref[1:2, :] += jnp.sum(total, 0, keepdims=True)
    out_ref[...] = (
        dmid_ref[...] + norm_back(total, normed, inv_std, norm_ref[0:1, :])
    ).astype(LOW)


def weight_grad_kernel(pieces, rights, norms, rows, table_ref, *refs):
    lefts = refs[: sum(pieces)]
    right_refs = refs[len(lefts) : len(lefts) + len(rights)]
    norm_refs = refs[len(lefts) + len(rights) : len(lefts) + len(rights) + norms]
    outs, (held_ref, pack_ref) = refs[len(lefts) + len(rights) + norms : -2], refs[-2:]
    mats = len(pieces)
    parts = outs[0].shape[0]
    blocks = held_ref.shape[1] // LANES // parts
    first = 0
    for j in range(mats):
        start = 0
        for left in lefts[first : first + pieces[j]]:
            step = min(256, left.shape[1])
            for c in range(0, left.shape[1], step):
                column = 0
                for (mat, entry), ref in zip(rights, right_refs):
                    if mat == j or mat is None:
                        right = ref[...] if entry is None else ref[j]
                        wide = right.shape[1]
                        held_ref[start : start + step, column : column + wide] = product(
                            left[:, c : c + step], right, TN
                        ).astype(LOW)
                        column += wide
                start += step
        first += pieces[j]
        for h in range(parts):
            for side, ref in enumerate(outs):
                number = ref.shape[1]

                @pl.loop(0, number)
                def _(n, ref=ref, side=side, number=number, j=j, h=h):
                    row = pl.multiple_of(table_ref[h, side * number + n] * rows, rows)
                    for b in range(blocks):
                        lane = (h * blocks + b) * LANES
                        at = (j * blocks + b) * rows
                        ref[h, n, at : at + rows, :] = held_ref[
                            pl.ds(row, rows), lane : lane + LANES
                        ]

    if norms:
        pack_norms(
            [ref[i : i + 1, :] for ref in norm_refs for i in range(ref.shape[0])], pack_ref
        )
        at = mats * blocks * rows
        for h in range(parts):
            for side, ref in enumerate(outs):
                number = ref.shape[1]

                @pl.loop(0, number)
                def _(n, ref=ref, side=side, number=number, h=h):
                    row = pack_ref[pl.ds(table_ref[h, side * number + n], 1), :]
                    ref[h, n, at : at + 16, :] = jnp.broadcast_to(row, (16, LANES)).astype(LOW)


def weight_grads(table, lefts, rights, norms, rows, chunks, parts, sides):
    mats = len(lefts)
    pieces = [len(p) for p in lefts]
    flat = [a for p in lefts for a in p]
    length = flat[0].shape[0]
    width = sum(p.shape[1] for p in lefts[0])
    wide = sum(a.shape[-1] for m, _, a in rights if m in (0, None))
    size = mats * wide // parts // LANES * rows + (16 if norms else 0)
    return pl.pallas_call(
        functools.partial(
            weight_grad_kernel, pieces, [r[:2] for r in rights], len(norms), rows
        ),
        out_shape=[shape((parts, chunks // sides, size, LANES), LOW)] * sides,
        in_specs=[SMEM] + [VMEM] * (len(flat) + len(rights) + len(norms)),
        out_specs=[VMEM] * sides,
        scratch_shapes=[pltpu.VMEM((width, wide), LOW), pltpu.VMEM((32, LANES), F32)],
        compiler_params=params(28),
        cost_estimate=cost(2 * mats * length * width * wide, 4 * mats * width * wide),
    )(table, *flat, *[a for _, _, a in rights], *norms)


def sum_kernel(plans, *refs):
    ins, outs = refs[: -len(plans)], refs[-len(plans) :]
    for plan, out in zip(plans, outs):
        for at, terms in plan:
            total = None
            for number, entry in terms:
                value = ins[number][entry].astype(F32)
                total = value if total is None else total + value
            out[at] = total.astype(out.dtype)


def stage_sums(inputs, plans, outs):
    return pl.pallas_call(
        functools.partial(sum_kernel, plans),
        out_shape=outs,
        in_specs=[VMEM] * len(inputs),
        out_specs=[VMEM] * len(outs),
        compiler_params=params(24),
        cost_estimate=cost(0, 2**22),
    )(*inputs)


def far_sums(keep, taken, earlier):
    parts, chunks, size, _ = keep.shape
    half = chunks // 2 ** (len(earlier) + 1)
    plans = [
        [
            (n, [(0, (h, half + n)), (1, (h, half + n))]
             + [(2 + parts * e + h, half + n) for e in range(len(earlier))])
            for n in range(half)
        ]
        for h in range(parts)
    ]
    outs = [shape((half, size, LANES), LOW)] * parts
    return stage_sums([keep, taken, *[t for e in earlier for t in e]], plans, outs)


def near_sums(keep, taken, earlier, inner):
    parts, _, size, _ = keep.shape
    plans = [
        [
            (h, [(0, (h, k)), (1, (h, k))] + [(2 + parts * e + h, k) for e in range(len(earlier))])
            for h in range(parts)
        ]
        for k in range(inner)
    ]
    outs = [shape((parts, size, LANES), F32 if k == 0 else LOW) for k in range(inner)]
    return stage_sums([keep, taken, *[t for e in earlier for t in e]], plans, outs)


def lamb_values(weight, grad, first, second):
    m_one = beta_one * first + (1.0 - beta_one) * grad
    m_two = beta_two * second + (1.0 - beta_two) * grad * grad
    step_dir = (
        m_one
        / (1.0 - beta_one**adam_step)
        / (jnp.sqrt(m_two / (1.0 - beta_two**adam_step)) + adam_eps)
        + decay_rate * weight
    )
    return m_one, m_two, step_dir


def whole_sum(value):
    return jnp.sum(jnp.sum(value, 0, keepdims=True), 1, keepdims=True)


def lamb_kernel(first, parts, terms, norm_ends, prior, *refs):
    weight_ref, one_ref, two_ref = refs[:3]
    norm_refs = refs[3:6] if norm_ends else ()
    base = 3 + len(norm_refs)
    term_refs = refs[base : base + terms]
    prior_refs = refs[base + terms : base + terms + prior]
    outs = refs[base + terms + prior :]
    mats, rows = 3, weight_ref.shape[1]
    lane = lax.broadcasted_iota(jnp.int32, (8, LANES), 1)
    line = lax.broadcasted_iota(jnp.int32, (8, LANES), 0)
    squares = jnp.zeros((8, LANES), F32)
    weight_sq = [jnp.zeros((1, LANES), F32)] * mats
    update_sq = [jnp.zeros((1, LANES), F32)] * mats
    for column, blocks, used, entry in parts:
        for j in range(mats):
            for b in range(blocks):
                at = (j * blocks + b) * rows
                grad = None
                for t in used:
                    value = term_refs[t][entry, at : at + rows, :].astype(F32)
                    grad = value if grad is None else grad + value
                span = slice(column + b * LANES, column + (b + 1) * LANES)
                weight = weight_ref[first + j, :, span]
                m_one, m_two, step = lamb_values(
                    weight, grad, one_ref[first + j, :, span], two_ref[first + j, :, span]
                )
                for ref, value in zip(outs, (grad, m_one, m_two, step)):
                    ref[j, :, span] = value
                weight_sq[j] += jnp.sum(weight * weight, 0, keepdims=True)
                update_sq[j] += jnp.sum(step * step, 0, keepdims=True)
    for j in range(mats):
        spot = lane == first + j
        squares += jnp.where(spot & (line == 0), jnp.sum(weight_sq[j], 1, keepdims=True), 0.0)
        squares += jnp.where(spot & (line == 1), jnp.sum(update_sq[j], 1, keepdims=True), 0.0)
    if prior:
        for ref, old in zip(outs[:4], prior_refs[:4]):
            ref[mats:] = old[...]
        squares += prior_refs[4][...]
    if norm_ends:
        used, entry, at = norm_ends
        row = None
        for t in used:
            value = term_refs[t][entry, at : at + 16, :].astype(F32)[0:1]
            row = value if row is None else row + value
        for i in range(4):
            span = slice(i * rows, (i + 1) * rows)
            weight = norm_refs[0][i : i + 1, :]
            grad = row[:, span]
            m_one, m_two, step = lamb_values(
                weight, grad, norm_refs[1][i : i + 1, :], norm_refs[2][i : i + 1, :]
            )
            for ref, value in zip(outs[5:], (grad, m_one, m_two, step)):
                ref[i : i + 1, :] = value
            spot = lane == 6 + i
            squares += jnp.where(spot & (line == 0), whole_sum(weight * weight), 0.0)
            squares += jnp.where(spot & (line == 1), whole_sum(step * step), 0.0)
    outs[4][...] = squares


def lamb_call(first, parts, terms, state, norm_state, norm_ends, prior):
    mats, rows, width = state[0].shape
    outs = [shape((mats if prior else 3, rows, width), F32)] * 4 + [shape((8, LANES), F32)]
    if norm_ends:
        outs += [shape(norm_state[0].shape, F32)] * 4
    inputs = [*state, *norm_state, *terms, *prior]
    return pl.pallas_call(
        functools.partial(lamb_kernel, first, parts, len(terms), norm_ends, len(prior)),
        out_shape=outs,
        in_specs=[VMEM] * len(inputs),
        out_specs=[VMEM] * len(outs),
        compiler_params=params(24),
        cost_estimate=cost(0, 2**22),
    )(*inputs)


def on_device(
    latents,
    lengths,
    cotangent,
    matrices,
    norm_params,
    moment1_mat,
    moment2_mat,
    moment1_norm,
    moment2_norm,
):
    _, length, width = latents.shape
    dim = width // HEADS
    scale = 1.0 / math.sqrt(dim)
    power = scale * math.log2(math.e)
    dp, fsdp = lax.axis_size("dp"), lax.axis_size("fsdp")
    count = dp * fsdp
    rows = matrices.shape[1]
    index = lax.axis_index("dp") * fsdp + lax.axis_index("fsdp")
    ring = dp == 8 and fsdp == 4 and rows == 32
    inner, pair = fsdp, fsdp
    block = 256 if length % 256 == 0 else length
    low_mats = matrices.astype(LOW)
    low_norms = norm_params.astype(LOW)

    if ring:
        firsts, seconds = (2 * fsdp, 4 * fsdp), (4 * fsdp, 2 * fsdp)
        half_blocks = width // 2 // LANES
        norm_row = 3 * half_blocks * rows
        masks = jnp.array(
            [
                [m ^ side for side in (0, pair) for m in mask_order(o, inner)]
                for o in zip(firsts, seconds)
            ],
            jnp.int32,
        )
        table = jnp.bitwise_xor(masks, index.astype(jnp.int32))
        norm_rows = jnp.pad(low_norms.reshape(1, 1, 4 * rows), ((0, 1), (0, 15), (0, 0)))
        shards = [
            jnp.concatenate([by_columns(low_mats[:3], 2), norm_rows], 1),
            by_columns(low_mats[3:], 2),
        ]
        quarter = count // 4
        layout = tuple(
            (h, side * count // 2 + part * quarter, h * width // 2, half_blocks)
            for h in range(2)
            for side in range(2)
            for part in range(2)
        )

        def near_of(shard):
            return [shard] + [swap(shard, k, count) for k in range(1, inner)]

        def halves_of(near):
            return [jnp.stack([n[h] for n in near]) for h in range(2)]

        def grow(held, taken):
            return [jnp.concatenate(both) for both in zip(held, taken)]

        def with_pairs(held, taken, early):
            late = swap_all(taken, [pair, pair], count)
            return [a for h in range(2) for a in (held[h], taken[h], early[h], late[h])]

        near = near_of(shards[0])
        held = halves_of(near)
        taken = swap_all(held, firsts, count)
        later = near_of(after(shards[1], *held))
        held = grow(held, taken)
        taken = swap_all(held, seconds, count)
        early = swap_all(held, [pair, pair], count)
        later = halves_of(after(later, *held))
        parts_in = with_pairs(held, taken, early)
        norm_vals = []
    else:
        weights = lax.all_gather(low_mats, AXES, axis=1, tiled=True)
        norm_vals = [lax.all_gather(low_norms, AXES, axis=1, tiled=True).astype(F32)]
        table = jnp.zeros((1, 1), jnp.int32)
        rows = width
        parts_in, parts_out = by_columns(weights[:3], 1), by_columns(weights[3:], 1)
        parts_in, parts_out = [parts_in], [parts_out]
        layout = ((0, 0, 0, width // LANES),)
        norm_row = None

    ends = jnp.cumsum(lengths[0, :-1])
    sets = ends.shape[0]
    segment = jnp.sum(
        (jnp.arange(length, dtype=jnp.int32)[:, None] >= ends[None, :]).astype(jnp.int32), axis=1
    )
    live = (segment < sets).astype(F32)[:, None]
    lanes = jnp.arange(LANES, dtype=jnp.int32)[None, :]
    same = segment[:, None] == lanes
    mark_in = same.astype(LOW)
    mark_out = jnp.where(same | (lanes > sets), 0.0, mask_depth).astype(LOW)

    x, dz = latents[0], cotangent[0]
    steps = (length // block,)
    if ring:
        taken = swap_all(later, firsts, count)
        x = after(x, *later)
    held_rows = pl.BlockSpec((4, width), lambda i: (0, 0))
    two_rows = pl.BlockSpec((2, width), lambda i: (0, 0))
    weight_scratch = pltpu.VMEM((3, width, width), LOW)
    hidden_one, qkv, norm_vals = pl.pallas_call(
        functools.partial(project_kernel, layout, rows, norm_row, len(parts_in)),
        grid=steps,
        out_shape=[
            shape((length, width), LOW),
            shape((length, 3 * width), LOW),
            shape((4, width), F32),
        ],
        in_specs=[SMEM, rows_of(x, block)]
        + [whole(a) for a in parts_in]
        + [held_rows] * len(norm_vals),
        out_specs=[
            pl.BlockSpec((block, width), lambda i: (i, 0)),
            pl.BlockSpec((block, 3 * width), lambda i: (i, 0)),
            held_rows,
        ],
        scratch_shapes=[weight_scratch, pltpu.VMEM((32, LANES), F32)],
        compiler_params=params(28),
        cost_estimate=cost(6 * length * width * width, 12 * width * width),
    )(table, x, *parts_in, *norm_vals)
    x = latents[0]

    group = 2
    marks = [pl.BlockSpec((length, LANES), lambda h: (0, 0))] * 2

    def heads_at(first):
        return pl.BlockSpec((length, dim * group), lambda h: (0, first // group + h))

    def sums_at(first):
        return pl.BlockSpec((group, 1, length), lambda h: (first // group + h, 0, 0))

    def attend(first, number, qkv):
        return pl.pallas_call(
            functools.partial(attend_kernel, group, dim, power),
            grid=(number // group,),
            in_specs=[heads_at(first + i * HEADS) for i in range(3)] + marks,
            out_specs=[heads_at(0), sums_at(0)],
            out_shape=[shape((length, number * dim), LOW), shape((number, 1, length), F32)],
            compiler_params=params(28),
            cost_estimate=cost(8 * length * length * number * dim, 8 * length * number * dim),
        )(qkv, qkv, qkv, mark_in, mark_out)

    ahead = HEADS // 2
    if ring:
        later = grow(later, after(taken, hidden_one))
        taken = swap_all(later, seconds, count)
        early = swap_all(later, [pair, pair], count)
        attended, log_sums = zip(*[attend(f, ahead, after(qkv, *later)) for f in (0, ahead)])
        taken = after(taken, *attended)
        parts_out = with_pairs(later, taken, early)
    else:
        attended, log_sums = zip(*[attend(f, ahead, qkv) for f in (0, ahead)])

    row_block = pl.BlockSpec((block, width), lambda i: (i, 0))
    (dnorm_two, result, dmid, dmlp, hidden_two, dup, active, dbranch, dattended) = pl.pallas_call(
        functools.partial(middle_kernel, layout, rows, len(attended)),
        grid=steps,
        out_shape=[
            shape((2, width), F32),
            shape((length, width), LOW),
            shape((length, width), F32),
            *[shape((length, width), LOW)] * 6,
        ],
        in_specs=[SMEM, row_block, row_block, rows_of(live, block), held_rows]
        + [rows_of(a, block) for a in attended]
        + [whole(a) for a in parts_out],
        out_specs=[two_rows] + [row_block] * 8,
        scratch_shapes=[weight_scratch],
        compiler_params=params(36),
        cost_estimate=cost(12 * length * width * width, 12 * width * width),
    )(table, x, dz, live, norm_vals, *attended, *parts_out)

    def attend_back(first, number, dattended):
        side = first // ahead
        inside = first - side * ahead
        return pl.pallas_call(
            functools.partial(attend_back_kernel, group, dim, power, scale),
            grid=(number // group,),
            in_specs=[heads_at(first + i * HEADS) for i in range(3)]
            + [heads_at(first), heads_at(inside), *marks, sums_at(inside)],
            out_specs=pl.BlockSpec((3, length, dim * group), lambda h: (0, 0, h)),
            out_shape=shape((3, length, number * dim), LOW),
            compiler_params=params(28),
            cost_estimate=cost(20 * length * length * number * dim, 16 * length * number * dim),
        )(qkv, qkv, qkv, dattended, attended[side], mark_in, mark_out, log_sums[side])

    def last(dmid, grads):
        return pl.pallas_call(
            functools.partial(last_kernel, layout, rows, len(parts_in)),
            grid=steps,
            out_shape=[shape((length, width), LOW), shape((2, width), F32)],
            in_specs=[SMEM, row_block, row_block, held_rows]
            + [whole(a) for a in parts_in]
            + [rows_of(g, block) for g in grads],
            out_specs=[row_block, two_rows],
            scratch_shapes=[weight_scratch],
            compiler_params=params(36),
            cost_estimate=cost(6 * length * width * width, 6 * width * width),
        )(table, x, dmid, norm_vals, *parts_in, *grads)

    out_lefts = [list(attended), [hidden_two], [active]]
    out_rights = [(0, None, dbranch), (1, None, dup), (2, None, dmlp)]
    in_lefts = [[hidden_one]] * 3
    state, norm_state = (matrices, moment1_mat, moment2_mat), (norm_params, moment1_norm, moment2_norm)
    if ring:
        keep, send = weight_grads(table, out_lefts, out_rights, [], rows, count, 2, 2)
        taken = swap(send, pair, count)
        grads = [attend_back(0, 2, after(dattended, keep))]
        grads.append(attend_back(2, 2, after(dattended, grads[0])))
        sums = far_sums(keep, after(taken, grads[1]), [])
        far_one = swap_all(sums, seconds, count)
        grads.append(attend_back(4, 2, after(dattended, *sums)))
        keep_a, send_a = weight_grads(
            table, in_lefts, [(None, 0, g) for g in grads], [], rows, count, 2, 2
        )
        taken_a = swap(send_a, pair, count)
        grads.append(attend_back(6, 2, after(dattended, keep_a)))
        sums_a = far_sums(keep_a, after(taken_a, grads[3]), [])
        far_one_a = swap_all(sums_a, seconds, count)
        sums = far_sums(keep, taken, [after(far_one, *sums_a)])
        far_two = swap_all(sums, firsts, count)
        grad_latents, dnorm_one = last(after(dmid, *sums), grads)
        keep_b, send_b = weight_grads(
            table,
            in_lefts,
            [(None, 0, grads[3])],
            [dnorm_one, dnorm_two],
            rows,
            count,
            2,
            2,
        )
        taken_b = swap(send_b, pair, count)
        sums_a = far_sums(keep_a, taken_a, [after(far_one_a, keep_b)])
        far_two_a = swap_all(sums_a, firsts, count)
        near = near_sums(keep, taken, [far_one, after(far_two, *sums_a)], inner)
        sums_b = far_sums(keep_b, after(taken_b, *near), [])
        far_one_b = swap_all(sums_b, seconds, count)
        near = [near[0]] + swap_all(near[1:], range(1, inner), count)
        near_a = near_sums(keep_a, taken_a, [far_one_a, after(far_two_a, *sums_b)], inner)
        near_a = [near_a[0]] + swap_all(near_a[1:], range(1, inner), count)
        sums_b = far_sums(keep_b, taken_b, [after(far_one_b, near_a[0])])
        far_two_b = swap_all(sums_b, firsts, count)
        parts = [(h * width // 2, half_blocks, range(inner), h) for h in range(2)]
        prior = lamb_call(3, parts, after(near, *sums_b), state, (), None, ())
        near_b = near_sums(keep_b, taken_b, [far_one_b, after(far_two_b, prior[4])], inner)
        near_b = [near_b[0]] + swap_all(near_b[1:], range(1, inner), count)
        a_blocks, b_blocks = 3 * group * dim // 2 // LANES, group * dim // 2 // LANES
        parts = [(h * a_blocks * LANES, a_blocks, range(inner), h) for h in range(2)] + [
            ((2 * a_blocks + h * b_blocks) * LANES, b_blocks, range(inner, 2 * inner), h)
            for h in range(2)
        ]
        norm_ends = (range(inner, 2 * inner), 0, 3 * b_blocks * rows)
        found = lamb_call(0, parts, [*near_a, *near_b], state, norm_state, norm_ends, prior)
        grad_mats, m1_mat, m2_mat, dir_mat, squares, grad_norms, m1_norm, m2_norm, dir_norm = found
        squares = hyper_sum(squares, count)[:2, :10]
    else:
        (out_grads,) = weight_grads(table, out_lefts, out_rights, [], rows, 1, 1, 1)
        grads = [attend_back(f, ahead, dattended) for f in (0, ahead)]
        (in_grads,) = weight_grads(
            table, in_lefts, [(None, 0, g) for g in grads], [], rows, 1, 1, 1
        )
        grad_latents, dnorm_one = last(dmid, grads)
        norms_local = jnp.concatenate([dnorm_one, dnorm_two], 0)
        mats_local = jnp.concatenate([in_grads[0, 0], out_grads[0, 0]], 0).astype(F32)
        mats_local = mats_local.reshape(6, width // LANES, width, LANES)
        mats_local = mats_local.transpose(0, 2, 1, 3).reshape(6, width, width)
        grad_mats = lax.psum_scatter(mats_local, AXES, scatter_dimension=1, tiled=True)
        grad_norms = lax.psum_scatter(norms_local, AXES, scatter_dimension=1, tiled=True)
        m1_mat, m2_mat, dir_mat = lamb_values(matrices, grad_mats, moment1_mat, moment2_mat)
        m1_norm, m2_norm, dir_norm = lamb_values(norm_params, grad_norms, moment1_norm, moment2_norm)
        squares = jnp.stack(
            [
                jnp.concatenate([jnp.sum(m * m, (1, 2)), jnp.sum(n * n, 1)])
                for m, n in ((matrices, norm_params), (dir_mat, dir_norm))
            ]
        )
        squares = lax.psum(squares, AXES)
    ratios = jnp.sqrt(squares[0]) / jnp.sqrt(squares[1])
    scaled_mats = ratios[:6][:, None, None] * dir_mat
    scaled_norms = ratios[6:][:, None] * dir_norm
    return (
        result[None],
        grad_latents[None],
        grad_mats,
        grad_norms,
        scaled_mats,
        scaled_norms,
        m1_mat,
        m2_mat,
        m1_norm,
        m2_norm,
        ratios,
    )


def solution(mesh):
    return jax.shard_map(
        on_device,
        mesh=mesh,
        in_specs=(
            P(("dp", "fsdp"), None, None),
            P(("dp", "fsdp"), None),
            P(("dp", "fsdp"), None, None),
            P(None, ("dp", "fsdp"), None),
            P(None, ("dp", "fsdp")),
            P(None, ("dp", "fsdp"), None),
            P(None, ("dp", "fsdp"), None),
            P(None, ("dp", "fsdp")),
            P(None, ("dp", "fsdp")),
        ),
        out_specs=(
            P(("dp", "fsdp"), None, None),
            P(("dp", "fsdp"), None, None),
            P(None, ("dp", "fsdp"), None),
            P(None, ("dp", "fsdp")),
            P(None, ("dp", "fsdp"), None),
            P(None, ("dp", "fsdp")),
            P(None, ("dp", "fsdp"), None),
            P(None, ("dp", "fsdp"), None),
            P(None, ("dp", "fsdp")),
            P(None, ("dp", "fsdp")),
            P(),
        ),
        check_vma=False,
    )
```

time: 977 us -> 280 us (0.29)
  waiting for transfers between devices: 603 us -> 111 us
  matrix products: 111 us -> 0 us
  blocking collectives: 110 us -> 0 us
  Pallas kernels: 0 us -> 89.8 us
  local copies, waits for them, and re-layouts: 72.6 us -> 12.5 us
  starting transfers between devices: 0.16 us -> 57.4 us
  other arithmetic: 55.1 us -> 4.96 us
  between operations: 14.7 us -> 1.69 us
    unnamed x7 -> x0, waiting for transfers between devices: 579 us -> none
    dot_general x18 -> x0, matrix products: 111 us -> none  [the longest x1 11.9 us: on_device(): jnp.einsum('qhd,khd->hqk', grad_attn, values, preferred_element_type=jnp....]
    ppermute x0 -> x51, waiting for transfers between devices: none -> 111 us  [swap(): return lax.ppermute(value, AXES, [(i, i ^ mask) for i in range(count)])]
    pallas_call x0 -> x23, Pallas kernels: none -> 89.8 us  [the longest x3 21.5 us: weight_grads(): pl.pallas_call(functools.partial(weight_grad_kernel, pieces, [r[:2] for r...]
    all_gather x1 -> x0, blocking collectives: 70.4 us -> none  [on_device(): lax.all_gather(low_norms, ('dp', 'fsdp'), axis=1, tiled=True)]
    ppermute x0 -> x51, starting transfers between devices: none -> 57.4 us  [swap(): return lax.ppermute(value, AXES, [(i, i ^ mask) for i in range(count)])]
    psum x1 -> x0, blocking collectives: 39.8 us -> none  [on_device(): lax.psum((jnp.concatenate([wsq_mat, wsq_norm]), jnp.concatenate([usq_mat,...]
    all_gather x1 -> x0, waiting for transfers between devices: 23.7 us -> none  [on_device(): lax.all_gather(low_mats, ('dp', 'fsdp'), axis=1, tiled=True)]
  transfers between devices with their start and end apart: 4 -> 51, of which waited for: 4 -> 27; matrix products, arithmetic and copies ran while one was open for 9% -> 1% of each run, Pallas kernels for 0% -> 12%
where the time goes in v2:
time: 280 us; the launch traced here: 277 us
  waiting for transfers between devices  111 us (40%)
  Pallas kernels  89.8 us (32%)
  starting transfers between devices  57.4 us (20%)
  local copies, waits for them, and re-layouts  12.5 us (4%)
  other arithmetic  4.96 us (2%)
    ppermute x51, waiting for transfers between devices, swap(): return lax.ppermute(value, AXES, [(i, i ^ mask) for i in range(count)])  111 us
    ppermute x51, starting transfers between devices, swap(): return lax.ppermute(value, AXES, [(i, i ^ mask) for i in range(count)])  57.4 us
    pallas_call x3, Pallas kernels, weight_grads(): pl.pallas_call(functools.partial(weight_grad_kernel, pieces, [r[:2] for r...  21.5 us
    pallas_call x1, Pallas kernels, on_device(): pl.pallas_call(functools.partial(middle_kernel, layout, rows, len(attende...  17.4 us
    pallas_call x4, Pallas kernels, attend_back(): pl.pallas_call(functools.partial(attend_back_kernel, group, dim, power, s...  15.6 us
    unnamed x100, local copies, waits for them, and re-layouts  11.6 us
    pallas_call x1, Pallas kernels, last(): pl.pallas_call(functools.partial(last_kernel, layout, rows, len(parts_in)...  11 us
    pallas_call x2, Pallas kernels, attend(): pl.pallas_call(functools.partial(attend_kernel, group, dim, power), grid=...  10 us
  transfers between devices with their start and end apart: 51, of which 27 were waited for; matrix products, arithmetic and copies ran while one was open for 1% of the time, Pallas kernels for 12%

profile of v2, /device:TPU:0, one launch (start us, length us, event | category | flops | bytes accessed | tf_op | source)
XLA Modules:
  0.0 277.0 jit_solution(2101661330209676289)
XLA Ops:
  2.8 5.1 %collective-permute-start.2 = (bf16[2,400,128]{2,1,0:T(8,128)(2,1)S(1)}, bf16[2,400,128]{2,1,0:T(8,128)(2,1)S(1)}, u32[]{:S(2)}, u32[]{:S(2)}) collective-permute-start(bf16[2,400,128]{2,1,0:T(8,128)(2,1)S(1)} %fusion.3), channel_id=1, source_target_pairs={{0,3},{1,2},{2,1},{3,0},{4,7},{5,6},{6,5},{7,4},{8,11},{9,10},{10,... | collective-permute-start | bytes 614408 | tf_op jit(solution)/shard_map/ppermute | solution.py:61
  8.6 12.5 %collective-permute-done = bf16[2,400,128]{2,1,0:T(8,128)(2,1)S(1)} collective-permute-done((bf16[2,400,128]{2,1,0:T(8,128)(2,1)S(1)}, bf16[2,400,128]{2,1,0:T(8,128)(2,1)S(1)}, u32[]{:S(2)}, u32[]{:S(2)}) %collective-permute-start) | collective-permute-done | bytes 204832 | tf_op jit(solution)/shard_map/ppermute | solution.py:61
  21.2 4.1 %collective-permute-done.1 = bf16[2,400,128]{2,1,0:T(8,128)(2,1)S(1)} collective-permute-done((bf16[2,400,128]{2,1,0:T(8,128)(2,1)S(1)}, bf16[2,400,128]{2,1,0:T(8,128)(2,1)S(1)}, u32[]{:S(2)}, u32[]{:S(2)}) %collective-permute-start.1) | collective-permute-done | bytes 204832 | tf_op jit(solution)/shard_map/ppermute | solution.py:61
  25.6 1.6 collective-permute-start.7
  27.2 1.6 collective-permute-start.6
  28.8 7.4 %collective-permute-done.7 = bf16[4,400,128]{2,1,0:T(8,128)(2,1)S(1)} collective-permute-done((bf16[4,400,128]{2,1,0:T(8,128)(2,1)S(1)}, bf16[4,400,128]{2,1,0:T(8,128)(2,1)S(1)}, u32[]{:S(2)}, u32[]{:S(2)}) %collective-permute-start.7) | collective-permute-done | bytes 409632 | tf_op jit(solution)/shard_map/ppermute | solution.py:61
  36.2 1.6 collective-permute-start.11
  37.9 1.5 collective-permute-start.8
  40.0 2.4 collective-permute-start.5
  42.4 2.1 collective-permute-start.3
  44.5 5.2 %collective-permute-done.5 = bf16[2,384,128]{2,1,0:T(8,128)(2,1)S(1)} collective-permute-done((bf16[2,384,128]{2,1,0:T(8,128)(2,1)S(1)}, bf16[2,384,128]{2,1,0:T(8,128)(2,1)S(1)}, u32[]{:S(2)}, u32[]{:S(2)}) %collective-permute-start.5) | collective-permute-done | bytes 196640 | tf_op jit(solution)/shard_map/ppermute | solution.py:61
  49.8 7.2 %collective-permute-done.4 = bf16[2,384,128]{2,1,0:T(8,128)(2,1)S(1)} collective-permute-done((bf16[2,384,128]{2,1,0:T(8,128)(2,1)S(1)}, bf16[2,384,128]{2,1,0:T(8,128)(2,1)S(1)}, u32[]{:S(2)}, u32[]{:S(2)}) %collective-permute-start.4) | collective-permute-done | bytes 196640 | tf_op jit(solution)/shard_map/ppermute | solution.py:61
  61.8 9.7 %shard_map.185 = (bf16[768,1024]{1,0:T(8,128)(2,1)S(1)}, bf16[768,3072]{1,0:T(8,128)(2,1)S(1)}, f32[4,1024]{1,0:T(4,128)S(1)}) custom-call(s32[2,32]{1,0:T(2,128)S(1)} %broadcast_xor_fusion.table_ref, bf16[768,1024]{1,0:T(8,128)(2,1)S(1)} %bitcast.20, bf16[8,400,128]{2,1,0:T(8,128)(2,1)S(1)} %constant_dynamic-update-slice_fusion.refs_0_, ...), custom_call_target="tpu_custom_call" | custom-call | flops 4831838208 | bytes 12582912 | tf_op jit(solution)/shard_map/pallas_call | solution.py:616
  74.3 5.0 %shard_map.187 = (bf16[768,512]{1,0:T(8,128)(2,1)S(1)}, f32[4,1,768]{2,1,0:T(1,128)S(1)}) custom-call(bf16[768,3072]{1,0:T(8,128)(2,1)S(1)} %get-tuple-element.119.q_ref.k_ref.v_ref, bf16[768,3072]{1,0:T(8,128)(2,1)S(1)} %get-tuple-element.119.q_ref.k_ref.v_ref, bf16[768,3072]{1,0:T(8,128)(2,1)S(1)} %get-tuple-element.119.q_ref.k_ref.v_ref, ...), custom_call_target="tpu_custom_call" | custom-call | flops 2415919104 | bytes 3145728 | tf_op jit(solution)/shard_map/pallas_call | solution.py:648
  79.3 5.0 %shard_map.186 = (bf16[768,512]{1,0:T(8,128)(2,1)S(1)}, f32[4,1,768]{2,1,0:T(1,128)S(1)}) custom-call(bf16[768,3072]{1,0:T(8,128)(2,1)S(1)} %get-tuple-element.119.q_ref.k_ref.v_ref, bf16[768,3072]{1,0:T(8,128)(2,1)S(1)} %get-tuple-element.119.q_ref.k_ref.v_ref, bf16[768,3072]{1,0:T(8,128)(2,1)S(1)} %get-tuple-element.119.q_ref.k_ref.v_ref, ...), custom_call_target="tpu_custom_call" | custom-call | flops 2415919104 | bytes 3145728 | tf_op jit(solution)/shard_map/pallas_call | solution.py:648
  84.4 6.9 %collective-permute-done.17.refs_7_ = bf16[8,384,128]{2,1,0:T(8,128)(2,1)S(1)} collective-permute-done((bf16[8,384,128]{2,1,0:T(8,128)(2,1)S(1)}, bf16[8,384,128]{2,1,0:T(8,128)(2,1)S(1)}, u32[]{:S(2)}, u32[]{:S(2)}) %collective-permute-start.17) | collective-permute-done | bytes 786464 | tf_op jit(solution)/shard_map/ppermute | solution.py:61
  92.4 1.6 collective-permute-done.19.refs_5_
  95.1 17.4 %shard_map.188 = (f32[2,1024]{1,0:T(2,128)S(1)}, bf16[768,1024]{1,0:T(8,128)(2,1)}, f32[768,1024]{1,0:T(8,128)}, bf16[768,1024]{1,0:T(8,128)(2,1)S(1)}, bf16[768...) custom-call(s32[2,32]{1,0:T(2,128)S(1)} %broadcast_xor_fusion.table_, ...), custom_call_target="tpu_custom_call" | custom-call | flops 9663676416 | bytes 12582912 | tf_op jit(solution)/shard_map/pallas_call | solution.py:670
  113.6 1.4 copy-done.43
  115.0 9.0 %shard_map.189 = (bf16[2,16,384,128]{3,2,1,0:T(8,128)(2,1)S(1)}, bf16[2,16,384,128]{3,2,1,0:T(8,128)(2,1)S(1)}) custom-call(s32[2,32]{1,0:T(2,128)S(1)} %broadcast_xor_fusion.table_ref, bf16[768,512]{1,0:T(8,128)(2,1)S(1)} %get-tuple-element.120.refs_0_.o_ref, bf16[768,512]{1,0:T(8,128)(2,1)S(1)} %get-tuple-element.121.refs_1_.o_ref, ...), custom_call_target="tpu_custom_call" | custom-call | flops 4831838208 | bytes 12582912 | tf_op jit(solution)/shard_map/pallas_call | solution.py:360
  125.3 3.9 %shard_map.190.refs_3_.refs_8_ = bf16[3,768,256]{2,1,0:T(8,128)(2,1)S(1)} custom-call(bf16[768,3072]{1,0:T(8,128)(2,1)S(1)} %get-tuple-element.119.q_ref.k_ref.v_ref, bf16[768,3072]{1,0:T(8,128)(2,1)S(1)} %get-tuple-element.119.q_ref.k_ref.v_ref, bf16[768,3072]{1,0:T(8,128)(2,1)S(1)} %get-tuple-element.119.q_ref.k_ref.v_ref, ...), custom_call_target="tpu_custom_call" | custom-call | flops 3019898880 | bytes 3145728 | tf_op jit(solution)/shard_map/pallas_call | solution.py:691
  129.2 3.9 %shard_map.191.refs_4_.refs_9_ = bf16[3,768,256]{2,1,0:T(8,128)(2,1)S(1)} custom-call(bf16[768,3072]{1,0:T(8,128)(2,1)S(1)} %get-tuple-element.119.q_ref.k_ref.v_ref, bf16[768,3072]{1,0:T(8,128)(2,1)S(1)} %get-tuple-element.119.q_ref.k_ref.v_ref, bf16[768,3072]{1,0:T(8,128)(2,1)S(1)} %get-tuple-element.119.q_ref.k_ref.v_ref, ...), custom_call_target="tpu_custom_call" | custom-call | flops 3019898880 | bytes 3145728 | tf_op jit(solution)/shard_map/pallas_call | solution.py:691
  134.7 3.9 %shard_map.193.refs_5_.refs_10_ = bf16[3,768,256]{2,1,0:T(8,128)(2,1)S(1)} custom-call(bf16[768,3072]{1,0:T(8,128)(2,1)S(1)} %get-tuple-element.119.q_ref.k_ref.v_ref, bf16[768,3072]{1,0:T(8,128)(2,1)S(1)} %get-tuple-element.119.q_ref.k_ref.v_ref, bf16[768,3072]{1,0:T(8,128)(2,1)S(1)} %get-tuple-element.119.q_ref.k_ref.v_ref, ...), custom_call_target="tpu_custom_call" | custom-call | flops 3019898880 | bytes 3145728 | tf_op jit(solution)/shard_map/pallas_call | solution.py:691
  138.6 7.9 %shard_map.194 = (bf16[2,16,288,128]{3,2,1,0:T(8,128)(2,1)S(1)}, bf16[2,16,288,128]{3,2,1,0:T(8,128)(2,1)S(1)}) custom-call(s32[2,32]{1,0:T(2,128)S(1)} %broadcast_xor_fusion.table_ref, bf16[768,1024]{1,0:T(8,128)(2,1)S(1)} %copy-done.5, bf16[768,1024]{1,0:T(8,128)(2,1)S(1)} %copy-done.5, bf16[768,1024]{1,0:T(8,128)(2,1)S(1)} %copy-done.5, ...), custom_call_target="tpu_custom_call" | custom-call | flops 3623878656 | bytes 9437184 | tf_op jit(solution)/shard_map/pallas_call | solution.py:360
  149.0 3.9 %shard_map.195.refs_11_.refs_3_ = bf16[3,768,256]{2,1,0:T(8,128)(2,1)S(1)} custom-call(bf16[768,3072]{1,0:T(8,128)(2,1)S(1)} %get-tuple-element.119.q_ref.k_ref.v_ref, bf16[768,3072]{1,0:T(8,128)(2,1)S(1)} %get-tuple-element.119.q_ref.k_ref.v_ref, bf16[768,3072]{1,0:T(8,128)(2,1)S(1)} %get-tuple-element.119.q_ref.k_ref.v_ref, ...), custom_call_target="tpu_custom_call" | custom-call | flops 3019898880 | bytes 3145728 | tf_op jit(solution)/shard_map/pallas_call | solution.py:691
  154.4 12.2 %collective-permute-done.23.refs_2_ = bf16[8,384,128]{2,1,0:T(8,128)(2,1)S(1)} collective-permute-done((bf16[8,384,128]{2,1,0:T(8,128)(2,1)S(1)}, bf16[8,384,128]{2,1,0:T(8,128)(2,1)S(1)}, u32[]{:S(2)}, u32[]{:S(2)}) %collective-permute-start.23) | collective-permute-done | bytes 786464 | tf_op jit(solution)/shard_map/ppermute | solution.py:61
  170.9 1.9 copy-done.41
  172.8 11.0 %shard_map.198 = (bf16[768,1024]{1,0:T(8,128)(2,1)}, f32[2,1024]{1,0:T(2,128)S(1)}) custom-call(s32[2,32]{1,0:T(2,128)S(1)} %broadcast_xor_fusion.table_ref, bf16[768,1024]{1,0:T(8,128)(2,1)S(1)} %bitcast.21, f32[768,1024]{1,0:T(8,128)S(1)} %copy-done.41, f32[4,1024]{1,0:T(4,128)S(1)} %get-tuple-element.114.norm_ref, bf16[8,400,128]{2,1,0:T(8,128)(2,1)S(1)} %copy-done.27, ...), custom_call_target="tpu_custom_call" | custom-call | flops 4831838208 | bytes 6291456 | tf_op jit(solution)/shard_map/pallas_call | solution.py:703
  183.8 4.7 %shard_map.199 = (bf16[2,16,112,128]{3,2,1,0:T(8,128)(2,1)S(1)}, bf16[2,16,112,128]{3,2,1,0:T(8,128)(2,1)S(1)}) custom-call(s32[2,32]{1,0:T(2,128)S(1)} %broadcast_xor_fusion.table_ref, bf16[768,1024]{1,0:T(8,128)(2,1)S(1)} %copy-done.6, bf16[768,1024]{1,0:T(8,128)(2,1)S(1)} %copy-done.6, bf16[768,1024]{1,0:T(8,128)(2,1)S(1)} %copy-done.6, ...), custom_call_target="tpu_custom_call" | custom-call | flops 1207959552 | bytes 3145728 | tf_op jit(solution)/shard_map/pallas_call | solution.py:360
  189.5 1.5 collective-permute-start.27
  192.7 12.1 %collective-permute-done.26.refs_2_ = bf16[8,288,128]{2,1,0:T(8,128)(2,1)S(1)} collective-permute-done((bf16[8,288,128]{2,1,0:T(8,128)(2,1)S(1)}, bf16[8,288,128]{2,1,0:T(8,128)(2,1)S(1)}, u32[]{:S(2)}, u32[]{:S(2)}) %collective-permute-start.26) | collective-permute-done | bytes 589856 | tf_op jit(solution)/shard_map/ppermute | solution.py:61
  205.9 1.6 collective-permute-start.28
  208.0 6.1 %collective-permute-done.31.refs_4_ = bf16[4,384,128]{2,1,0:T(8,128)(2,1)S(1)} collective-permute-done((bf16[4,384,128]{2,1,0:T(8,128)(2,1)S(1)}, bf16[4,384,128]{2,1,0:T(8,128)(2,1)S(1)}, u32[]{:S(2)}, u32[]{:S(2)}) %collective-permute-start.31) | collective-permute-done | bytes 393248 | tf_op jit(solution)/shard_map/ppermute | solution.py:61
  216.8 3.6 %collective-permute-done.28.refs_4_ = bf16[4,288,128]{2,1,0:T(8,128)(2,1)S(1)} collective-permute-done((bf16[4,288,128]{2,1,0:T(8,128)(2,1)S(1)}, bf16[4,288,128]{2,1,0:T(8,128)(2,1)S(1)}, u32[]{:S(2)}, u32[]{:S(2)}) %collective-permute-start.28) | collective-permute-done | bytes 294944 | tf_op jit(solution)/shard_map/ppermute | solution.py:61
  220.4 2.0 collective-permute-start.42
  224.6 1.6 collective-permute-start.38
  226.8 8.5 %collective-permute-done.41.refs_5_ = bf16[2,384,128]{2,1,0:T(8,128)(2,1)S(1)} collective-permute-done((bf16[2,384,128]{2,1,0:T(8,128)(2,1)S(1)}, bf16[2,384,128]{2,1,0:T(8,128)(2,1)S(1)}, u32[]{:S(2)}, u32[]{:S(2)}) %collective-permute-start.41) | collective-permute-done | bytes 196640 | tf_op jit(solution)/shard_map/ppermute | solution.py:61
  235.3 1.7 collective-permute-start.35
  237.8 10.3 %collective-permute-start.43 = (bf16[2,112,128]{2,1,0:T(8,128)(2,1)S(1)}, bf16[2,112,128]{2,1,0:T(8,128)(2,1)S(1)}, u32[]{:S(2)}, u32[]{:S(2)}) collective-permute-start(bf16[2,112,128]{2,1,0:T(8,128)(2,1)S(1)} %get-tuple-element.189), channel_id=1, source_target_pairs={{0,1},{1,0},{2,3},{3,2},{4,5},{5,4},{6,7},{7,6},{8,9},{9,8},{10,11... | collective-permute-start | bytes 172040 | tf_op jit(solution)/shard_map/ppermute | solution.py:61
  248.8 1.7 collective-permute-start.45
  250.5 5.4 %collective-permute-done.44.refs_12_ = bf16[2,112,128]{2,1,0:T(8,128)(2,1)S(1)} collective-permute-done((bf16[2,112,128]{2,1,0:T(8,128)(2,1)S(1)}, bf16[2,112,128]{2,1,0:T(8,128)(2,1)S(1)}, u32[]{:S(2)}, u32[]{:S(2)}) %collective-permute-start.44) | collective-permute-done | bytes 57376 | tf_op jit(solution)/shard_map/ppermute | solution.py:61
  256.0 1.9 shard_map.207
  259.1 2.4 collective-permute-done.46
  261.5 1.6 collective-permute-start.47
  263.1 2.9 %collective-permute-done.47 = f32[8,128]{1,0:T(8,128)S(1)} collective-permute-done((f32[8,128]{1,0:T(8,128)S(1)}, f32[8,128]{1,0:T(8,128)S(1)}, u32[]{:S(2)}, u32[]{:S(2)}) %collective-permute-start.47) | collective-permute-done | bytes 4128 | tf_op jit(solution)/shard_map/ppermute | solution.py:61
  267.2 1.5 collective-permute-start.49
  268.7 2.1 collective-permute-done.49
  272.1 2.3 collective-permute-done.50
  (214 shorter events, 43.1 us)
Async XLA Ops:
  2.8 22.6 %collective-permute-start.2 = (bf16[2,400,128]{2,1,0:T(8,128)(2,1)S(1)}, bf16[2,400,128]{2,1,0:T(8,128)(2,1)S(1)}, u32[]{:S(2)}, u32[]{:S(2)}) collective-permute-start(bf16[2,400,128]{2,1,0:T(8,128)(2,1)S(1)} %fusion.3), channel_id=1, source_target_pairs={{0,3},{1,2},{2,1},{3,0},{4,7},{5,6},{6,5},{7,4},{8,11},{9,10},{10,... | collective-permute-start | bytes 614408 | tf_op jit(solution)/shard_map/ppermute | solution.py:61
  7.9 17.4 %collective-permute-start.1 = (bf16[2,400,128]{2,1,0:T(8,128)(2,1)S(1)}, bf16[2,400,128]{2,1,0:T(8,128)(2,1)S(1)}, u32[]{:S(2)}, u32[]{:S(2)}) collective-permute-start(bf16[2,400,128]{2,1,0:T(8,128)(2,1)S(1)} %fusion.3), channel_id=1, source_target_pairs={{0,2},{1,3},{2,0},{3,1},{4,6},{5,7},{6,4},{7,5},{8,10},{9,11},{10,... | collective-permute-start | bytes 614408 | tf_op jit(solution)/shard_map/ppermute | solution.py:61
  7.9 13.2 %collective-permute-start = (bf16[2,400,128]{2,1,0:T(8,128)(2,1)S(1)}, bf16[2,400,128]{2,1,0:T(8,128)(2,1)S(1)}, u32[]{:S(2)}, u32[]{:S(2)}) collective-permute-start(bf16[2,400,128]{2,1,0:T(8,128)(2,1)S(1)} %fusion.3), channel_id=1, source_target_pairs={{0,1},{1,0},{2,3},{3,2},{4,5},{5,4},{6,7},{7,6},{8,9},{9,8},{10,11... | collective-permute-start | bytes 614408 | tf_op jit(solution)/shard_map/ppermute | solution.py:61
  25.6 10.6 %collective-permute-start.7 = (bf16[4,400,128]{2,1,0:T(8,128)(2,1)S(1)}, bf16[4,400,128]{2,1,0:T(8,128)(2,1)S(1)}, u32[]{:S(2)}, u32[]{:S(2)}) collective-permute-start(bf16[4,400,128]{2,1,0:T(8,128)(2,1)S(1)} %pad_maximum_fusion.1), channel_id=1, source_target_pairs={{0,16},{1,17},{2,18},{3,19},{4,20},{5,21},{6,22},{7,23},{8,24},{9,... | collective-permute-start | bytes 1228808 | tf_op jit(solution)/shard_map/ppermute | solution.py:61
  27.2 10.6 %collective-permute-start.6 = (bf16[4,400,128]{2,1,0:T(8,128)(2,1)S(1)}, bf16[4,400,128]{2,1,0:T(8,128)(2,1)S(1)}, u32[]{:S(2)}, u32[]{:S(2)}) collective-permute-start(bf16[4,400,128]{2,1,0:T(8,128)(2,1)S(1)} %pad_maximum_fusion), channel_id=1, source_target_pairs={{0,8},{1,9},{2,10},{3,11},{4,12},{5,13},{6,14},{7,15},{8,0},{9,1},... | collective-permute-start | bytes 1228808 | tf_op jit(solution)/shard_map/ppermute | solution.py:61
  36.2 20.8 %collective-permute-start.11 = (bf16[8,400,128]{2,1,0:T(8,128)(2,1)S(1)}, bf16[8,400,128]{2,1,0:T(8,128)(2,1)}, u32[]{:S(2)}, u32[]{:S(2)}) collective-permute-start(bf16[8,400,128]{2,1,0:T(8,128)(2,1)S(1)} %constant_dynamic-update-slice_fusion.5.refs_4_), channel_id=1, source_target_pairs={{0,8},{1,9},{2,10},{3,11},{4,12},{5,13},{6,14},{7,15},{8,0},{9,1},... | collective-permute-start | bytes 2457608 | tf_op jit(solution)/shard_map/ppermute | solution.py:61
  37.9 19.6 %collective-permute-start.8 = (bf16[8,400,128]{2,1,0:T(8,128)(2,1)S(1)}, bf16[8,400,128]{2,1,0:T(8,128)(2,1)}, u32[]{:S(2)}, u32[]{:S(2)}) collective-permute-start(bf16[8,400,128]{2,1,0:T(8,128)(2,1)S(1)} %constant_dynamic-update-slice_fusion.refs_0_), channel_id=1, source_target_pairs={{0,16},{1,17},{2,18},{3,19},{4,20},{5,21},{6,22},{7,23},{8,24},{9,... | collective-permute-start | bytes 2457608 | tf_op jit(solution)/shard_map/ppermute | solution.py:61
  40.0 9.7 %collective-permute-start.5 = (bf16[2,384,128]{2,1,0:T(8,128)(2,1)S(1)}, bf16[2,384,128]{2,1,0:T(8,128)(2,1)S(1)}, u32[]{:S(2)}, u32[]{:S(2)}) collective-permute-start(bf16[2,384,128]{2,1,0:T(8,128)(2,1)S(1)} %bitcast.23), channel_id=1, source_target_pairs={{0,3},{1,2},{2,1},{3,0},{4,7},{5,6},{6,5},{7,4},{8,11},{9,10},{10,... | collective-permute-start | bytes 589832 | tf_op jit(solution)/shard_map/ppermute | solution.py:61
  42.4 14.5 %collective-permute-start.4 = (bf16[2,384,128]{2,1,0:T(8,128)(2,1)S(1)}, bf16[2,384,128]{2,1,0:T(8,128)(2,1)S(1)}, u32[]{:S(2)}, u32[]{:S(2)}) collective-permute-start(bf16[2,384,128]{2,1,0:T(8,128)(2,1)S(1)} %bitcast.24), channel_id=1, source_target_pairs={{0,2},{1,3},{2,0},{3,1},{4,6},{5,7},{6,4},{7,5},{8,10},{9,11},{10,... | collective-permute-start | bytes 589832 | tf_op jit(solution)/shard_map/ppermute | solution.py:61
  42.4 14.5 %collective-permute-start.3 = (bf16[2,384,128]{2,1,0:T(8,128)(2,1)S(1)}, bf16[2,384,128]{2,1,0:T(8,128)(2,1)S(1)}, u32[]{:S(2)}, u32[]{:S(2)}) collective-permute-start(bf16[2,384,128]{2,1,0:T(8,128)(2,1)S(1)} %bitcast.25), channel_id=1, source_target_pairs={{0,1},{1,0},{2,3},{3,2},{4,5},{5,4},{6,7},{7,6},{8,9},{9,8},{10,11... | collective-permute-start | bytes 589832 | tf_op jit(solution)/shard_map/ppermute | solution.py:61
  49.8 8.8 %collective-permute-start.12 = (bf16[8,400,128]{2,1,0:T(8,128)(2,1)S(1)}, bf16[8,400,128]{2,1,0:T(8,128)(2,1)S(1)}, u32[]{:S(2)}, u32[]{:S(2)}) collective-permute-start(bf16[8,400,128]{2,1,0:T(8,128)(2,1)S(1)} %constant_dynamic-update-slice_fusion.5.refs_4_), channel_id=1, source_target_pairs={{0,4},{1,5},{2,6},{3,7},{4,0},{5,1},{6,2},{7,3},{8,12},{9,13},{10,... | collective-permute-start | bytes 2457608 | tf_op jit(solution)/shard_map/ppermute | solution.py:61
  57.0 3.6 %collective-permute-start.13 = (bf16[8,400,128]{2,1,0:T(8,128)(2,1)}, bf16[8,400,128]{2,1,0:T(8,128)(2,1)S(1)}, u32[]{:S(2)}, u32[]{:S(2)}) collective-permute-start(bf16[8,400,128]{2,1,0:T(8,128)(2,1)} %collective-permute-done.11.refs_5_), channel_id=1, source_target_pairs={{0,4},{1,5},{2,6},{3,7},{4,0},{5,1},{6,2},{7,3},{8,12},{9,13},{10,... | collective-permute-start | bytes 2457608 | tf_op jit(solution)/shard_map/ppermute | solution.py:61
  57.6 4.2 %collective-permute-start.10 = (bf16[8,400,128]{2,1,0:T(8,128)(2,1)}, bf16[8,400,128]{2,1,0:T(8,128)(2,1)S(1)}, u32[]{:S(2)}, u32[]{:S(2)}) collective-permute-start(bf16[8,400,128]{2,1,0:T(8,128)(2,1)} %collective-permute-done.8.refs_1_), channel_id=1, source_target_pairs={{0,4},{1,5},{2,6},{3,7},{4,0},{5,1},{6,2},{7,3},{8,12},{9,13},{10,... | collective-permute-start | bytes 2457608 | tf_op jit(solution)/shard_map/ppermute | solution.py:61
  57.9 13.6 %collective-permute-start.14 = (bf16[4,384,128]{2,1,0:T(8,128)(2,1)S(1)}, bf16[4,384,128]{2,1,0:T(8,128)(2,1)S(1)}, u32[]{:S(2)}, u32[]{:S(2)}) collective-permute-start(bf16[4,384,128]{2,1,0:T(8,128)(2,1)S(1)} %pad_maximum_fusion.2), channel_id=1, source_target_pairs={{0,8},{1,9},{2,10},{3,11},{4,12},{5,13},{6,14},{7,15},{8,0},{9,1},... | collective-permute-start | bytes 1179656 | tf_op jit(solution)/shard_map/ppermute | solution.py:61
  58.6 13.0 %collective-permute-start.15 = (bf16[4,384,128]{2,1,0:T(8,128)(2,1)S(1)}, bf16[4,384,128]{2,1,0:T(8,128)(2,1)S(1)}, u32[]{:S(2)}, u32[]{:S(2)}) collective-permute-start(bf16[4,384,128]{2,1,0:T(8,128)(2,1)S(1)} %pad_maximum_fusion.3), channel_id=1, source_target_pairs={{0,16},{1,17},{2,18},{3,19},{4,20},{5,21},{6,22},{7,23},{8,24},{9,... | collective-permute-start | bytes 1179656 | tf_op jit(solution)/shard_map/ppermute | solution.py:61
  71.6 19.6 %collective-permute-start.17 = (bf16[8,384,128]{2,1,0:T(8,128)(2,1)S(1)}, bf16[8,384,128]{2,1,0:T(8,128)(2,1)S(1)}, u32[]{:S(2)}, u32[]{:S(2)}) collective-permute-start(bf16[8,384,128]{2,1,0:T(8,128)(2,1)S(1)} %constant_dynamic-update-slice_fusion.15.refs_6_), channel_id=1, source_target_pairs={{0,8},{1,9},{2,10},{3,11},{4,12},{5,13},{6,14},{7,15},{8,0},{9,1},... | collective-permute-start | bytes 2359304 | tf_op jit(solution)/shard_map/ppermute | solution.py:61
  72.3 19.4 %collective-permute-start.16 = (bf16[8,384,128]{2,1,0:T(8,128)(2,1)S(1)}, bf16[8,384,128]{2,1,0:T(8,128)(2,1)S(1)}, u32[]{:S(2)}, u32[]{:S(2)}) collective-permute-start(bf16[8,384,128]{2,1,0:T(8,128)(2,1)S(1)} %constant_dynamic-update-slice_fusion.10.refs_2_), channel_id=1, source_target_pairs={{0,16},{1,17},{2,18},{3,19},{4,20},{5,21},{6,22},{7,23},{8,24},{9,... | collective-permute-start | bytes 2359304 | tf_op jit(solution)/shard_map/ppermute | solution.py:61
  73.7 18.6 %collective-permute-start.20 = (bf16[8,384,128]{2,1,0:T(8,128)(2,1)S(1)}, bf16[8,384,128]{2,1,0:T(8,128)(2,1)S(1)}, u32[]{:S(2)}, u32[]{:S(2)}) collective-permute-start(bf16[8,384,128]{2,1,0:T(8,128)(2,1)S(1)} %constant_dynamic-update-slice_fusion.15.refs_6_), channel_id=1, source_target_pairs={{0,4},{1,5},{2,6},{3,7},{4,0},{5,1},{6,2},{7,3},{8,12},{9,13},{10,... | collective-permute-start | bytes 2359304 | tf_op jit(solution)/shard_map/ppermute | solution.py:61
  73.8 18.5 %collective-permute-start.18 = (bf16[8,384,128]{2,1,0:T(8,128)(2,1)S(1)}, bf16[8,384,128]{2,1,0:T(8,128)(2,1)S(1)}, u32[]{:S(2)}, u32[]{:S(2)}) collective-permute-start(bf16[8,384,128]{2,1,0:T(8,128)(2,1)S(1)} %constant_dynamic-update-slice_fusion.10.refs_2_), channel_id=1, source_target_pairs={{0,4},{1,5},{2,6},{3,7},{4,0},{5,1},{6,2},{7,3},{8,12},{9,13},{10,... | collective-permute-start | bytes 2359304 | tf_op jit(solution)/shard_map/ppermute | solution.py:61
  91.7 3.4 %collective-permute-start.21 = (bf16[8,384,128]{2,1,0:T(8,128)(2,1)S(1)}, bf16[8,384,128]{2,1,0:T(8,128)(2,1)S(1)}, u32[]{:S(2)}, u32[]{:S(2)}) collective-permute-start(bf16[8,384,128]{2,1,0:T(8,128)(2,1)S(1)} %collective-permute-done.17.refs_7_), channel_id=1, source_target_pairs={{0,4},{1,5},{2,6},{3,7},{4,0},{5,1},{6,2},{7,3},{8,12},{9,13},{10,... | collective-permute-start | bytes 2359304 | tf_op jit(solution)/shard_map/ppermute | solution.py:61
  124.0 9.2 %collective-permute-start.22 = (bf16[2,16,384,128]{3,2,1,0:T(8,128)(2,1)S(1)}, bf16[2,16,384,128]{3,2,1,0:T(8,128)(2,1)S(1)}, u32[]{:S(2)}, u32[]{:S(2)}) collective-permute-start(bf16[2,16,384,128]{3,2,1,0:T(8,128)(2,1)S(1)} %get-tuple-element.132), channel_id=1, source_target_pairs={{0,4},{1,5},{2,6},{3,7},{4,0},{5,1},{6,2},{7,3},{8,12},{9,13},{10,... | collective-permute-start | bytes 9437192 | tf_op jit(solution)/shard_map/ppermute | solution.py:61
  146.6 6.3 %collective-permute-start.25 = (bf16[2,16,288,128]{3,2,1,0:T(8,128)(2,1)S(1)}, bf16[2,16,288,128]{3,2,1,0:T(8,128)(2,1)S(1)}, u32[]{:S(2)}, u32[]{:S(2)}) collective-permute-start(bf16[2,16,288,128]{3,2,1,0:T(8,128)(2,1)S(1)} %get-tuple-element.143), channel_id=1, source_target_pairs={{0,4},{1,5},{2,6},{3,7},{4,0},{5,1},{6,2},{7,3},{8,12},{9,13},{10,... | collective-permute-start | bytes 7077896 | tf_op jit(solution)/shard_map/ppermute | solution.py:61
  147.0 19.6 %collective-permute-start.23 = (bf16[8,384,128]{2,1,0:T(8,128)(2,1)S(1)}, bf16[8,384,128]{2,1,0:T(8,128)(2,1)S(1)}, u32[]{:S(2)}, u32[]{:S(2)}) collective-permute-start(bf16[8,384,128]{2,1,0:T(8,128)(2,1)S(1)} %get-tuple-element.138), channel_id=1, source_target_pairs={{0,16},{1,17},{2,18},{3,19},{4,20},{5,21},{6,22},{7,23},{8,24},{9,... | collective-permute-start | bytes 2359304 | tf_op jit(solution)/shard_map/ppermute | solution.py:61
  148.2 19.3 %collective-permute-start.24 = (bf16[8,384,128]{2,1,0:T(8,128)(2,1)S(1)}, bf16[8,384,128]{2,1,0:T(8,128)(2,1)S(1)}, u32[]{:S(2)}, u32[]{:S(2)}) collective-permute-start(bf16[8,384,128]{2,1,0:T(8,128)(2,1)S(1)} %get-tuple-element.139), channel_id=1, source_target_pairs={{0,8},{1,9},{2,10},{3,11},{4,12},{5,13},{6,14},{7,15},{8,0},{9,1},... | collective-permute-start | bytes 2359304 | tf_op jit(solution)/shard_map/ppermute | solution.py:61
  188.5 26.0 %collective-permute-start.30 = (bf16[2,16,112,128]{3,2,1,0:T(8,128)(2,1)S(1)}, bf16[2,16,112,128]{3,2,1,0:T(8,128)(2,1)S(1)}, u32[]{:S(2)}, u32[]{:S(2)}) collective-permute-start(bf16[2,16,112,128]{3,2,1,0:T(8,128)(2,1)S(1)} %get-tuple-element.161), channel_id=1, source_target_pairs={{0,4},{1,5},{2,6},{3,7},{4,0},{5,1},{6,2},{7,3},{8,12},{9,13},{10,... | collective-permute-start | bytes 2752520 | tf_op jit(solution)/shard_map/ppermute | solution.py:61
  188.6 16.2 %collective-permute-start.26 = (bf16[8,288,128]{2,1,0:T(8,128)(2,1)S(1)}, bf16[8,288,128]{2,1,0:T(8,128)(2,1)S(1)}, u32[]{:S(2)}, u32[]{:S(2)}) collective-permute-start(bf16[8,288,128]{2,1,0:T(8,128)(2,1)S(1)} %get-tuple-element.146), channel_id=1, source_target_pairs={{0,16},{1,17},{2,18},{3,19},{4,20},{5,21},{6,22},{7,23},{8,24},{9,... | collective-permute-start | bytes 1769480 | tf_op jit(solution)/shard_map/ppermute | solution.py:61
  189.5 16.2 %collective-permute-start.27 = (bf16[8,288,128]{2,1,0:T(8,128)(2,1)S(1)}, bf16[8,288,128]{2,1,0:T(8,128)(2,1)S(1)}, u32[]{:S(2)}, u32[]{:S(2)}) collective-permute-start(bf16[8,288,128]{2,1,0:T(8,128)(2,1)S(1)} %get-tuple-element.147), channel_id=1, source_target_pairs={{0,8},{1,9},{2,10},{3,11},{4,12},{5,13},{6,14},{7,15},{8,0},{9,1},... | collective-permute-start | bytes 1769480 | tf_op jit(solution)/shard_map/ppermute | solution.py:61
  191.0 23.1 %collective-permute-start.31 = (bf16[4,384,128]{2,1,0:T(8,128)(2,1)S(1)}, bf16[4,384,128]{2,1,0:T(8,128)(2,1)S(1)}, u32[]{:S(2)}, u32[]{:S(2)}) collective-permute-start(bf16[4,384,128]{2,1,0:T(8,128)(2,1)S(1)} %get-tuple-element.150), channel_id=1, source_target_pairs={{0,8},{1,9},{2,10},{3,11},{4,12},{5,13},{6,14},{7,15},{8,0},{9,1},... | collective-permute-start | bytes 1179656 | tf_op jit(solution)/shard_map/ppermute | solution.py:61
  191.5 22.6 %collective-permute-start.32 = (bf16[4,384,128]{2,1,0:T(8,128)(2,1)S(1)}, bf16[4,384,128]{2,1,0:T(8,128)(2,1)S(1)}, u32[]{:S(2)}, u32[]{:S(2)}) collective-permute-start(bf16[4,384,128]{2,1,0:T(8,128)(2,1)S(1)} %get-tuple-element.151), channel_id=1, source_target_pairs={{0,16},{1,17},{2,18},{3,19},{4,20},{5,21},{6,22},{7,23},{8,24},{9,... | collective-permute-start | bytes 1179656 | tf_op jit(solution)/shard_map/ppermute | solution.py:61
  205.9 14.5 %collective-permute-start.28 = (bf16[4,288,128]{2,1,0:T(8,128)(2,1)S(1)}, bf16[4,288,128]{2,1,0:T(8,128)(2,1)S(1)}, u32[]{:S(2)}, u32[]{:S(2)}) collective-permute-start(bf16[4,288,128]{2,1,0:T(8,128)(2,1)S(1)} %get-tuple-element.159), channel_id=1, source_target_pairs={{0,8},{1,9},{2,10},{3,11},{4,12},{5,13},{6,14},{7,15},{8,0},{9,1},... | collective-permute-start | bytes 884744 | tf_op jit(solution)/shard_map/ppermute | solution.py:61
  207.5 12.9 %collective-permute-start.29 = (bf16[4,288,128]{2,1,0:T(8,128)(2,1)S(1)}, bf16[4,288,128]{2,1,0:T(8,128)(2,1)S(1)}, u32[]{:S(2)}, u32[]{:S(2)}) collective-permute-start(bf16[4,288,128]{2,1,0:T(8,128)(2,1)S(1)} %get-tuple-element.160), channel_id=1, source_target_pairs={{0,16},{1,17},{2,18},{3,19},{4,20},{5,21},{6,22},{7,23},{8,24},{9,... | collective-permute-start | bytes 884744 | tf_op jit(solution)/shard_map/ppermute | solution.py:61
  214.6 9.4 %collective-permute-start.36 = (bf16[8,112,128]{2,1,0:T(8,128)(2,1)S(1)}, bf16[8,112,128]{2,1,0:T(8,128)(2,1)S(1)}, u32[]{:S(2)}, u32[]{:S(2)}) collective-permute-start(bf16[8,112,128]{2,1,0:T(8,128)(2,1)S(1)} %get-tuple-element.169), channel_id=1, source_target_pairs={{0,16},{1,17},{2,18},{3,19},{4,20},{5,21},{6,22},{7,23},{8,24},{9,... | collective-permute-start | bytes 688136 | tf_op jit(solution)/shard_map/ppermute | solution.py:61
  215.9 8.6 %collective-permute-start.37 = (bf16[8,112,128]{2,1,0:T(8,128)(2,1)S(1)}, bf16[8,112,128]{2,1,0:T(8,128)(2,1)S(1)}, u32[]{:S(2)}, u32[]{:S(2)}) collective-permute-start(bf16[8,112,128]{2,1,0:T(8,128)(2,1)S(1)} %get-tuple-element.170), channel_id=1, source_target_pairs={{0,8},{1,9},{2,10},{3,11},{4,12},{5,13},{6,14},{7,15},{8,0},{9,1},... | collective-permute-start | bytes 688136 | tf_op jit(solution)/shard_map/ppermute | solution.py:61
  216.8 9.4 %collective-permute-start.40 = (bf16[2,384,128]{2,1,0:T(8,128)(2,1)S(1)}, bf16[2,384,128]{2,1,0:T(8,128)(2,1)S(1)}, u32[]{:S(2)}, u32[]{:S(2)}) collective-permute-start(bf16[2,384,128]{2,1,0:T(8,128)(2,1)S(1)} %get-tuple-element.165), channel_id=1, source_target_pairs={{0,1},{1,0},{2,3},{3,2},{4,5},{5,4},{6,7},{7,6},{8,9},{9,8},{10,11... | collective-permute-start | bytes 589832 | tf_op jit(solution)/shard_map/ppermute | solution.py:61
  220.4 14.9 %collective-permute-start.41 = (bf16[2,384,128]{2,1,0:T(8,128)(2,1)S(1)}, bf16[2,384,128]{2,1,0:T(8,128)(2,1)S(1)}, u32[]{:S(2)}, u32[]{:S(2)}) collective-permute-start(bf16[2,384,128]{2,1,0:T(8,128)(2,1)S(1)} %get-tuple-element.166), channel_id=1, source_target_pairs={{0,2},{1,3},{2,0},{3,1},{4,6},{5,7},{6,4},{7,5},{8,10},{9,11},{10,... | collective-permute-start | bytes 589832 | tf_op jit(solution)/shard_map/ppermute | solution.py:61
  220.4 14.9 %collective-permute-start.42 = (bf16[2,384,128]{2,1,0:T(8,128)(2,1)S(1)}, bf16[2,384,128]{2,1,0:T(8,128)(2,1)S(1)}, u32[]{:S(2)}, u32[]{:S(2)}) collective-permute-start(bf16[2,384,128]{2,1,0:T(8,128)(2,1)S(1)} %get-tuple-element.167), channel_id=1, source_target_pairs={{0,3},{1,2},{2,1},{3,0},{4,7},{5,6},{6,5},{7,4},{8,11},{9,10},{10,... | collective-permute-start | bytes 589832 | tf_op jit(solution)/shard_map/ppermute | solution.py:61
  224.0 24.8 %collective-permute-start.33 = (bf16[2,288,128]{2,1,0:T(8,128)(2,1)S(1)}, bf16[2,288,128]{2,1,0:T(8,128)(2,1)S(1)}, u32[]{:S(2)}, u32[]{:S(2)}) collective-permute-start(bf16[2,288,128]{2,1,0:T(8,128)(2,1)S(1)} %get-tuple-element.174), channel_id=1, source_target_pairs={{0,1},{1,0},{2,3},{3,2},{4,5},{5,4},{6,7},{7,6},{8,9},{9,8},{10,11... | collective-permute-start | bytes 442376 | tf_op jit(solution)/shard_map/ppermute | solution.py:61
  224.6 13.1 %collective-permute-start.38 = (bf16[4,112,128]{2,1,0:T(8,128)(2,1)S(1)}, bf16[4,112,128]{2,1,0:T(8,128)(2,1)S(1)}, u32[]{:S(2)}, u32[]{:S(2)}) collective-permute-start(bf16[4,112,128]{2,1,0:T(8,128)(2,1)S(1)} %get-tuple-element.179), channel_id=1, source_target_pairs={{0,8},{1,9},{2,10},{3,11},{4,12},{5,13},{6,14},{7,15},{8,0},{9,1},... | collective-permute-start | bytes 344072 | tf_op jit(solution)/shard_map/ppermute | solution.py:61
  226.2 11.5 %collective-permute-start.39 = (bf16[4,112,128]{2,1,0:T(8,128)(2,1)S(1)}, bf16[4,112,128]{2,1,0:T(8,128)(2,1)S(1)}, u32[]{:S(2)}, u32[]{:S(2)}) collective-permute-start(bf16[4,112,128]{2,1,0:T(8,128)(2,1)S(1)} %get-tuple-element.180), channel_id=1, source_target_pairs={{0,16},{1,17},{2,18},{3,19},{4,20},{5,21},{6,22},{7,23},{8,24},{9,... | collective-permute-start | bytes 344072 | tf_op jit(solution)/shard_map/ppermute | solution.py:61
  235.3 15.3 %collective-permute-start.34 = (bf16[2,288,128]{2,1,0:T(8,128)(2,1)S(1)}, bf16[2,288,128]{2,1,0:T(8,128)(2,1)S(1)}, u32[]{:S(2)}, u32[]{:S(2)}) collective-permute-start(bf16[2,288,128]{2,1,0:T(8,128)(2,1)S(1)} %get-tuple-element.175), channel_id=1, source_target_pairs={{0,2},{1,3},{2,0},{3,1},{4,6},{5,7},{6,4},{7,5},{8,10},{9,11},{10,... | collective-permute-start | bytes 442376 | tf_op jit(solution)/shard_map/ppermute | solution.py:61
  235.3 15.3 %collective-permute-start.35 = (bf16[2,288,128]{2,1,0:T(8,128)(2,1)S(1)}, bf16[2,288,128]{2,1,0:T(8,128)(2,1)S(1)}, u32[]{:S(2)}, u32[]{:S(2)}) collective-permute-start(bf16[2,288,128]{2,1,0:T(8,128)(2,1)S(1)} %get-tuple-element.176), channel_id=1, source_target_pairs={{0,3},{1,2},{2,1},{3,0},{4,7},{5,6},{6,5},{7,4},{8,11},{9,10},{10,... | collective-permute-start | bytes 442376 | tf_op jit(solution)/shard_map/ppermute | solution.py:61
  237.8 12.7 %collective-permute-start.43 = (bf16[2,112,128]{2,1,0:T(8,128)(2,1)S(1)}, bf16[2,112,128]{2,1,0:T(8,128)(2,1)S(1)}, u32[]{:S(2)}, u32[]{:S(2)}) collective-permute-start(bf16[2,112,128]{2,1,0:T(8,128)(2,1)S(1)} %get-tuple-element.189), channel_id=1, source_target_pairs={{0,1},{1,0},{2,3},{3,2},{4,5},{5,4},{6,7},{7,6},{8,9},{9,8},{10,11... | collective-permute-start | bytes 172040 | tf_op jit(solution)/shard_map/ppermute | solution.py:61
  248.1 7.9 %collective-permute-start.44 = (bf16[2,112,128]{2,1,0:T(8,128)(2,1)S(1)}, bf16[2,112,128]{2,1,0:T(8,128)(2,1)S(1)}, u32[]{:S(2)}, u32[]{:S(2)}) collective-permute-start(bf16[2,112,128]{2,1,0:T(8,128)(2,1)S(1)} %get-tuple-element.190), channel_id=1, source_target_pairs={{0,2},{1,3},{2,0},{3,1},{4,6},{5,7},{6,4},{7,5},{8,10},{9,11},{10,... | collective-permute-start | bytes 172040 | tf_op jit(solution)/shard_map/ppermute | solution.py:61
  248.8 7.2 %collective-permute-start.45 = (bf16[2,112,128]{2,1,0:T(8,128)(2,1)S(1)}, bf16[2,112,128]{2,1,0:T(8,128)(2,1)S(1)}, u32[]{:S(2)}, u32[]{:S(2)}) collective-permute-start(bf16[2,112,128]{2,1,0:T(8,128)(2,1)S(1)} %get-tuple-element.191), channel_id=1, source_target_pairs={{0,3},{1,2},{2,1},{3,0},{4,7},{5,6},{6,5},{7,4},{8,11},{9,10},{10,... | collective-permute-start | bytes 172040 | tf_op jit(solution)/shard_map/ppermute | solution.py:61
  257.9 3.6 %collective-permute-start.46 = (f32[8,128]{1,0:T(8,128)S(1)}, f32[8,128]{1,0:T(8,128)S(1)}, u32[]{:S(2)}, u32[]{:S(2)}) collective-permute-start(f32[8,128]{1,0:T(8,128)S(1)} %get-tuple-element.198), channel_id=1, source_target_pairs={{0,1},{1,0},{2,3},{3,2},{4,5},{5,4},{6,7},{7,6},{8,9},{9,8},{10,11... | collective-permute-start | bytes 12296 | tf_op jit(solution)/shard_map/ppermute | solution.py:61
  261.5 4.5 %collective-permute-start.47 = (f32[8,128]{1,0:T(8,128)S(1)}, f32[8,128]{1,0:T(8,128)S(1)}, u32[]{:S(2)}, u32[]{:S(2)}) collective-permute-start(f32[8,128]{1,0:T(8,128)S(1)} %add.21), channel_id=1, source_target_pairs={{0,2},{1,3},{2,0},{3,1},{4,6},{5,7},{6,4},{7,5},{8,10},{9,11},{10,... | collective-permute-start | bytes 12296 | tf_op jit(solution)/shard_map/ppermute | solution.py:61
  267.2 3.6 %collective-permute-start.49 = (f32[8,128]{1,0:T(8,128)S(1)}, f32[8,128]{1,0:T(8,128)S(1)}, u32[]{:S(2)}, u32[]{:S(2)}) collective-permute-start(f32[8,128]{1,0:T(8,128)S(1)} %add.23), channel_id=1, source_target_pairs={{0,8},{1,9},{2,10},{3,11},{4,12},{5,13},{6,14},{7,15},{8,0},{9,1},... | collective-permute-start | bytes 12296 | tf_op jit(solution)/shard_map/ppermute | solution.py:61
  270.8 3.6 %collective-permute-start.50 = (f32[8,128]{1,0:T(8,128)S(1)}, f32[8,128]{1,0:T(8,128)S(1)}, u32[]{:S(2)}, u32[]{:S(2)}) collective-permute-start(f32[8,128]{1,0:T(8,128)S(1)} %add.24), channel_id=1, source_target_pairs={{0,16},{1,17},{2,18},{3,19},{4,20},{5,21},{6,22},{7,23},{8,24},{9,... | collective-permute-start | bytes 12296 | tf_op jit(solution)/shard_map/ppermute | solution.py:61
  (49 other events, 485.3 us)

commit v3 on v2

--- a/solution.py
+++ b/solution.py
@@ -224,17 +224,9 @@
         grad_ref[0, :, span] = (product(keys.T, grad_scores).T * scale).astype(LOW)
 
 
-def middle_kernel(layout, rows, atts, table_ref, x_ref, dz_ref, live_ref, norm_ref, *refs):
-    att_refs, chunks = refs[:atts], refs[atts:-10]
-    dnorm_ref, result_ref, dmid_ref, dmlp_ref, hidden_ref = refs[-10:-5]
-    dup_ref, act_ref, dbranch_ref, datt_ref, weight_ref = refs[-5:]
-
-    @pl.when(pl.program_id(0) == 0)
-    def _():
-        place_all(table_ref, layout, rows, chunks, weight_ref)
-        dnorm_ref[...] = jnp.zeros_like(dnorm_ref)
-
-    gain, shift = norm_ref[2:3, :], norm_ref[3:4, :]
+def middle_kernel(atts, x_ref, dz_ref, live_ref, norm_ref, weight_ref, *refs):
+    att_refs = refs[:atts]
+    result_ref, middle_ref, dmlp_ref, hidden_ref, dup_ref, act_ref = refs[atts:]
     live = live_ref[...]
     branch, first = None, 0
     for ref in att_refs:
@@ -242,8 +234,9 @@
         branch = part if branch is None else branch + part
         first += ref.shape[1]
     middle = x_ref[...].astype(F32) + live * branch
-    normed, inv_std = normalize(middle)
-    hidden = (normed * gain + shift).astype(LOW)
+    middle_ref[...] = middle
+    normed, _ = normalize(middle)
+    hidden = (normed * norm_ref[2:3, :] + norm_ref[3:4, :]).astype(LOW)
     hidden_ref[...] = hidden
     upward = product(hidden, weight_ref[1])
     square = upward * upward
@@ -255,24 +248,34 @@
         1.0 + (3.0 * cubic_coef) * square
     )
     result_ref[...] = (middle + live * product(active, weight_ref[2])).astype(LOW)
-    grad = dz_ref[...].astype(F32)
-    dmlp = (live * grad).astype(LOW)
+    dmlp = (live * dz_ref[...].astype(F32)).astype(LOW)
     dmlp_ref[...] = dmlp
-    dup = (product(dmlp, weight_ref[2], NT) * slope).astype(LOW)
-    dup_ref[...] = dup
-    dhidden = product(dup, weight_ref[1], NT)
+    dup_ref[...] = (product(dmlp, weight_ref[2], NT) * slope).astype(LOW)
+
+
+def middle_back_kernel(
+    middle_ref, dup_ref, dz_ref, live_ref, norm_ref, weight_ref,
+    dmid_ref, dbranch_ref, datt_ref, dnorm_ref,
+):
+    @pl.when(pl.program_id(0) == 0)
+    def _():
+        dnorm_ref[...] = jnp.zeros_like(dnorm_ref)
+
+    normed, inv_std = normalize(middle_ref[...])
+    dhidden = product(dup_ref[...], weight_ref[1], NT)
     dnorm_ref[0:1, :] += jnp.sum(dhidden * normed, 0, keepdims=True)
     dnorm_ref[1:2, :] += jnp.sum(dhidden, 0, keepdims=True)
-    dmid = grad + norm_back(dhidden, normed, inv_std, gain)
+    dmid = dz_ref[...].astype(F32) + norm_back(dhidden, normed, inv_std, norm_ref[2:3, :])
     dmid_ref[...] = dmid
-    dbranch = (live * dmid).astype(LOW)
+    dbranch = (live_ref[...] * dmid).astype(LOW)
     dbranch_ref[...] = dbranch
     datt_ref[...] = product(dbranch, weight_ref[0], NT).astype(LOW)
 
 
-def last_kernel(layout, rows, parts, table_ref, x_ref, dmid_ref, norm_ref, *refs):
-    chunks, grads = refs[:parts], refs[parts:-3]
-    out_ref, dnorm_ref, weight_ref = refs[-3:]
+def last_kernel(layout, rows, parts, sides, table_ref, x_ref, dmid_ref, norm_ref, other_ref, *refs):
+    chunks, grads = refs[:parts], refs[parts : -4 - sides]
+    out_ref, dnorm_ref = refs[-4 - sides : -2 - sides]
+    packs, (weight_ref, held_ref) = refs[-2 - sides : -2], refs[-2:]
     mats = weight_ref.shape[0]
 
     @pl.when(pl.program_id(0) == 0)
@@ -294,91 +297,95 @@
         dmid_ref[...] + norm_back(total, normed, inv_std, norm_ref[0:1, :])
     ).astype(LOW)
 
-
-def weight_grad_kernel(pieces, rights, norms, rows, table_ref, *refs):
-    lefts = refs[: sum(pieces)]
-    right_refs = refs[len(lefts) : len(lefts) + len(rights)]
-    norm_refs = refs[len(lefts) + len(rights) : len(lefts) + len(rights) + norms]
-    outs, (held_ref, pack_ref) = refs[len(lefts) + len(rights) + norms : -2], refs[-2:]
-    mats = len(pieces)
+    @pl.when((pl.program_id(0) == pl.num_programs(0) - 1) & (sides > 0))
+    def _():
+        norms = [ref[i : i + 1, :] for ref in (dnorm_ref, other_ref) for i in range(2)]
+        if packs:
+            pack_norms(norms, held_ref)
+        for side, ref in enumerate(packs):
+
+            @pl.loop(0, ref.shape[0])
+            def _(n, ref=ref, side=side):
+                row = held_ref[pl.ds(table_ref[0, side * ref.shape[0] + n], 1), :]
+                ref[n] = jnp.broadcast_to(row, (16, LANES)).astype(LOW)
+
+
+def weight_grad_kernel(jobs, rows, lefts, extra, table_ref, *refs):
+    rights = 1 + max(right for _, right, _ in jobs)
+    outs, held_ref = refs[lefts + rights : -1], refs[-1]
     parts = outs[0].shape[0]
-    blocks = held_ref.shape[1] // LANES // parts
-    first = 0
-    for j in range(mats):
+    at = 0
+    for pieces, right, entry in jobs:
+        value = refs[lefts + right][...] if entry is None else refs[lefts + right][entry]
+        wide = value.shape[1]
+        blocks = wide // LANES // parts
         start = 0
-        for left in lefts[first : first + pieces[j]]:
+        for piece in pieces:
+            left = refs[piece]
             step = min(256, left.shape[1])
             for c in range(0, left.shape[1], step):
-                column = 0
-                for (mat, entry), ref in zip(rights, right_refs):
-                    if mat == j or mat is None:
-                        right = ref[...] if entry is None else ref[j]
-                        wide = right.shape[1]
-                        held_ref[start : start + step, column : column + wide] = product(
-                            left[:, c : c + step], right, TN
-                        ).astype(LOW)
-                        column += wide
+                held_ref[start : start + step, :wide] = product(
+                    left[:, c : c + step], value, TN
+                ).astype(LOW)
                 start += step
-        first += pieces[j]
         for h in range(parts):
             for side, ref in enumerate(outs):
                 number = ref.shape[1]
 
                 @pl.loop(0, number)
-                def _(n, ref=ref, side=side, number=number, j=j, h=h):
+                def _(n, ref=ref, side=side, number=number, h=h, at=at, blocks=blocks):
                     row = pl.multiple_of(table_ref[h, side * number + n] * rows, rows)
                     for b in range(blocks):
                         lane = (h * blocks + b) * LANES
-                        at = (j * blocks + b) * rows
-                        ref[h, n, at : at + rows, :] = held_ref[
+                        first = at + b * rows
+                        ref[h, n, first : first + rows, :] = held_ref[
                             pl.ds(row, rows), lane : lane + LANES
                         ]
 
-    if norms:
-        pack_norms(
-            [ref[i : i + 1, :] for ref in norm_refs for i in range(ref.shape[0])], pack_ref
-        )
-        at = mats * blocks * rows
+        at += blocks * rows
+    if extra:
+        for ref in outs:
+            ref[:, :, at : at + extra, :] = jnp.zeros((*ref.shape[:2], extra, LANES), LOW)
+
+
+def weight_grads(table, lefts, rights, jobs, rows, chunks, parts, sides, extra=0):
+    length = lefts[0].shape[0]
+    width = rows * chunks
+    wides = [rights[right].shape[-1] for _, right, _ in jobs]
+    size = sum(wides) // parts // LANES * rows + extra
+    return pl.pallas_call(
+        functools.partial(weight_grad_kernel, jobs, rows, len(lefts), extra),
+        out_shape=[shape((parts, chunks // sides, size, LANES), LOW)] * sides,
+        in_specs=[SMEM] + [VMEM] * (len(lefts) + len(rights)),
+        out_specs=[VMEM] * sides,
+        scratch_shapes=[pltpu.VMEM((width, max(wides)), LOW)],
+        compiler_params=params(28),
+        cost_estimate=cost(2 * length * width * sum(wides), 4 * width * sum(wides)),
+    )(table, *lefts, *rights)
+
+
+def slots_of(jobs, rows, parts):
+    slots = [[] for _ in range(parts)]
+    at = 0
+    for matrix, column, wide in jobs:
+        blocks = wide // LANES // parts
         for h in range(parts):
-            for side, ref in enumerate(outs):
-                number = ref.shape[1]
-
-                @pl.loop(0, number)
-                def _(n, ref=ref, side=side, number=number, h=h):
-                    row = pack_ref[pl.ds(table_ref[h, side * number + n], 1), :]
-                    ref[h, n, at : at + 16, :] = jnp.broadcast_to(row, (16, LANES)).astype(LOW)
-
-
-def weight_grads(table, lefts, rights, norms, rows, chunks, parts, sides):
-    mats = len(lefts)
-    pieces = [len(p) for p in lefts]
-    flat = [a for p in lefts for a in p]
-    length = flat[0].shape[0]
-    width = sum(p.shape[1] for p in lefts[0])
-    wide = sum(a.shape[-1] for m, _, a in rights if m in (0, None))
-    size = mats * wide // parts // LANES * rows + (16 if norms else 0)
-    return pl.pallas_call(
-        functools.partial(
-            weight_grad_kernel, pieces, [r[:2] for r in rights], len(norms), rows
-        ),
-        out_shape=[shape((parts, chunks // sides, size, LANES), LOW)] * sides,
-        in_specs=[SMEM] + [VMEM] * (len(flat) + len(rights) + len(norms)),
-        out_specs=[VMEM] * sides,
-        scratch_shapes=[pltpu.VMEM((width, wide), LOW), pltpu.VMEM((32, LANES), F32)],
-        compiler_params=params(28),
-        cost_estimate=cost(2 * mats * length * width * wide, 4 * mats * width * wide),
-    )(table, *flat, *[a for _, _, a in rights], *norms)
+            for b in range(blocks):
+                slots[h].append((matrix, column + (h * blocks + b) * LANES, at + b * rows))
+        at += blocks * rows
+    return slots
 
 
 def sum_kernel(plans, *refs):
     ins, outs = refs[: -len(plans)], refs[-len(plans) :]
     for plan, out in zip(plans, outs):
-        for at, terms in plan:
-            total = None
-            for number, entry in terms:
-                value = ins[number][entry].astype(F32)
-                total = value if total is None else total + value
+        for at, terms, ends in plan:
+            total = sum(ins[number][entry].astype(F32) for number, entry in terms)
             out[at] = total.astype(out.dtype)
+            if ends:
+                size = ins[ends[0][0]].shape[1]
+                last = total[-size:] + sum(ins[n][entry].astype(F32) for n, entry in ends)
+                out[at, -size:, :] = last.astype(out.dtype)
 
 
 def stage_sums(inputs, plans, outs):
@@ -392,32 +399,47 @@
     )(*inputs)
 
 
-def far_sums(keep, taken, earlier):
+def terms_of(parts, earlier, h, entry):
+    return [(0, (h, entry)), (1, (h, entry))] + [
+        (2 + parts * e + h, entry) for e in range(earlier)
+    ]
+
+
+def far_sums(keep, taken, earlier, ends=()):
     parts, chunks, size, _ = keep.shape
     half = chunks // 2 ** (len(earlier) + 1)
+    base = 2 + parts * len(earlier)
     plans = [
         [
-            (n, [(0, (h, half + n)), (1, (h, half + n))]
-             + [(2 + parts * e + h, half + n) for e in range(len(earlier))])
+            (
+                n,
+                terms_of(parts, len(earlier), h, half + n),
+                [(base + e, half + n) for e in range(len(ends))] if h == 0 else [],
+            )
             for n in range(half)
         ]
         for h in range(parts)
     ]
     outs = [shape((half, size, LANES), LOW)] * parts
-    return stage_sums([keep, taken, *[t for e in earlier for t in e]], plans, outs)
-
-
-def near_sums(keep, taken, earlier, inner):
+    return stage_sums([keep, taken, *[t for e in earlier for t in e], *ends], plans, outs)
+
+
+def near_sums(keep, taken, earlier, inner, ends=()):
     parts, _, size, _ = keep.shape
+    base = 2 + parts * len(earlier)
     plans = [
         [
-            (h, [(0, (h, k)), (1, (h, k))] + [(2 + parts * e + h, k) for e in range(len(earlier))])
+            (
+                h,
+                terms_of(parts, len(earlier), h, k),
+                [(base + e, k) for e in range(len(ends))] if h == 0 else [],
+            )
             for h in range(parts)
         ]
         for k in range(inner)
     ]
     outs = [shape((parts, size, LANES), F32 if k == 0 else LOW) for k in range(inner)]
-    return stage_sums([keep, taken, *[t for e in earlier for t in e]], plans, outs)
+    return stage_sums([keep, taken, *[t for e in earlier for t in e], *ends], plans, outs)
 
 
 def lamb_values(weight, grad, first, second):
@@ -436,38 +458,34 @@
     return jnp.sum(jnp.sum(value, 0, keepdims=True), 1, keepdims=True)
 
 
-def lamb_kernel(first, parts, terms, norm_ends, prior, *refs):
+def lamb_kernel(base, mats, groups, terms, norm_ends, prior, *refs):
     weight_ref, one_ref, two_ref = refs[:3]
     norm_refs = refs[3:6] if norm_ends else ()
-    base = 3 + len(norm_refs)
-    term_refs = refs[base : base + terms]
-    prior_refs = refs[base + terms : base + terms + prior]
-    outs = refs[base + terms + prior :]
-    mats, rows = 3, weight_ref.shape[1]
+    first = 3 + len(norm_refs)
+    term_refs = refs[first : first + terms]
+    prior_refs = refs[first + terms : first + terms + prior]
+    outs = refs[first + terms + prior :]
+    rows = weight_ref.shape[1]
     lane = lax.broadcasted_iota(jnp.int32, (8, LANES), 1)
     line = lax.broadcasted_iota(jnp.int32, (8, LANES), 0)
     squares = jnp.zeros((8, LANES), F32)
     weight_sq = [jnp.zeros((1, LANES), F32)] * mats
     update_sq = [jnp.zeros((1, LANES), F32)] * mats
-    for column, blocks, used, entry in parts:
-        for j in range(mats):
-            for b in range(blocks):
-                at = (j * blocks + b) * rows
-                grad = None
-                for t in used:
-                    value = term_refs[t][entry, at : at + rows, :].astype(F32)
-                    grad = value if grad is None else grad + value
-                span = slice(column + b * LANES, column + (b + 1) * LANES)
-                weight = weight_ref[first + j, :, span]
-                m_one, m_two, step = lamb_values(
-                    weight, grad, one_ref[first + j, :, span], two_ref[first + j, :, span]
-                )
-                for ref, value in zip(outs, (grad, m_one, m_two, step)):
-                    ref[j, :, span] = value
-                weight_sq[j] += jnp.sum(weight * weight, 0, keepdims=True)
-                update_sq[j] += jnp.sum(step * step, 0, keepdims=True)
+    for used, entry, slots in groups:
+        for matrix, column, at in slots:
+            grad = sum(term_refs[t][entry, at : at + rows, :].astype(F32) for t in used)
+            span = slice(column, column + LANES)
+            weight = weight_ref[matrix, :, span]
+            m_one, m_two, step = lamb_values(
+                weight, grad, one_ref[matrix, :, span], two_ref[matrix, :, span]
+            )
+            j = matrix - base
+            for ref, value in zip(outs, (grad, m_one, m_two, step)):
+                ref[j, :, span] = value
+            weight_sq[j] += jnp.sum(weight * weight, 0, keepdims=True)
+            update_sq[j] += jnp.sum(step * step, 0, keepdims=True)
     for j in range(mats):
-        spot = lane == first + j
+        spot = lane == base + j
         squares += jnp.where(spot & (line == 0), jnp.sum(weight_sq[j], 1, keepdims=True), 0.0)
         squares += jnp.where(spot & (line == 1), jnp.sum(update_sq[j], 1, keepdims=True), 0.0)
     if prior:
@@ -476,14 +494,10 @@
         squares += prior_refs[4][...]
     if norm_ends:
         used, entry, at = norm_ends
-        row = None
-        for t in used:
-            value = term_refs[t][entry, at : at + 16, :].astype(F32)[0:1]
-            row = value if row is None else row + value
+        row = sum(term_refs[t][entry, at : at + 16, :].astype(F32)[0:1] for t in used)
         for i in range(4):
-            span = slice(i * rows, (i + 1) * rows)
             weight = norm_refs[0][i : i + 1, :]
-            grad = row[:, span]
+            grad = row[:, i * rows : (i + 1) * rows]
             m_one, m_two, step = lamb_values(
                 weight, grad, norm_refs[1][i : i + 1, :], norm_refs[2][i : i + 1, :]
             )
@@ -495,14 +509,14 @@
     outs[4][...] = squares
 
 
-def lamb_call(first, parts, terms, state, norm_state, norm_ends, prior):
-    mats, rows, width = state[0].shape
-    outs = [shape((mats if prior else 3, rows, width), F32)] * 4 + [shape((8, LANES), F32)]
+def lamb_call(base, mats, groups, terms, state, norm_state=(), norm_ends=None, prior=()):
+    total, rows, width = state[0].shape
+    outs = [shape((total if prior else mats, rows, width), F32)] * 4 + [shape((8, LANES), F32)]
     if norm_ends:
         outs += [shape(norm_state[0].shape, F32)] * 4
     inputs = [*state, *norm_state, *terms, *prior]
     return pl.pallas_call(
-        functools.partial(lamb_kernel, first, parts, len(terms), norm_ends, len(prior)),
+        functools.partial(lamb_kernel, base, mats, groups, len(terms), norm_ends, len(prior)),
         out_shape=outs,
         in_specs=[VMEM] * len(inputs),
         out_specs=[VMEM] * len(outs),
@@ -549,10 +563,7 @@
         )
         table = jnp.bitwise_xor(masks, index.astype(jnp.int32))
         norm_rows = jnp.pad(low_norms.reshape(1, 1, 4 * rows), ((0, 1), (0, 15), (0, 0)))
-        shards = [
-            jnp.concatenate([by_columns(low_mats[:3], 2), norm_rows], 1),
-            by_columns(low_mats[3:], 2),
-        ]
+        shard = jnp.concatenate([by_columns(low_mats[:3], 2), norm_rows], 1)
         quarter = count // 4
         layout = tuple(
             (h, side * count // 2 + part * quarter, h * width // 2, half_blocks)
@@ -561,36 +572,25 @@
             for part in range(2)
         )
 
-        def near_of(shard):
-            return [shard] + [swap(shard, k, count) for k in range(1, inner)]
-
-        def halves_of(near):
-            return [jnp.stack([n[h] for n in near]) for h in range(2)]
-
         def grow(held, taken):
             return [jnp.concatenate(both) for both in zip(held, taken)]
 
-        def with_pairs(held, taken, early):
-            late = swap_all(taken, [pair, pair], count)
-            return [a for h in range(2) for a in (held[h], taken[h], early[h], late[h])]
-
-        near = near_of(shards[0])
-        held = halves_of(near)
-        taken = swap_all(held, firsts, count)
-        later = near_of(after(shards[1], *held))
-        held = grow(held, taken)
+        near = [shard] + [swap(shard, k, count) for k in range(1, inner)]
+        held = [jnp.stack([n[h] for n in near]) for h in range(2)]
+        held = grow(held, swap_all(held, firsts, count))
         taken = swap_all(held, seconds, count)
         early = swap_all(held, [pair, pair], count)
-        later = halves_of(after(later, *held))
-        parts_in = with_pairs(held, taken, early)
+        late = swap_all(taken, [pair, pair], count)
+        parts_in = [a for h in range(2) for a in (held[h], taken[h], early[h], late[h])]
+        weights_out = lax.all_gather(low_mats[3:], AXES, axis=1, tiled=True)
         norm_vals = []
     else:
-        weights = lax.all_gather(low_mats, AXES, axis=1, tiled=True)
+        weights_in = lax.all_gather(low_mats[:3], AXES, axis=1, tiled=True)
+        weights_out = lax.all_gather(low_mats[3:], AXES, axis=1, tiled=True)
         norm_vals = [lax.all_gather(low_norms, AXES, axis=1, tiled=True).astype(F32)]
         table = jnp.zeros((1, 1), jnp.int32)
         rows = width
-        parts_in, parts_out = by_columns(weights[:3], 1), by_columns(weights[3:], 1)
-        parts_in, parts_out = [parts_in], [parts_out]
+        parts_in = [by_columns(weights_in, 1)]
         layout = ((0, 0, 0, width // LANES),)
         norm_row = None
 
@@ -607,9 +607,6 @@
 
     x, dz = latents[0], cotangent[0]
     steps = (length // block,)
-    if ring:
-        taken = swap_all(later, firsts, count)
-        x = after(x, *later)
     held_rows = pl.BlockSpec((4, width), lambda i: (0, 0))
     two_rows = pl.BlockSpec((2, width), lambda i: (0, 0))
     weight_scratch = pltpu.VMEM((3, width, width), LOW)
@@ -633,7 +630,6 @@
         compiler_params=params(28),
         cost_estimate=cost(6 * length * width * width, 12 * width * width),
     )(table, x, *parts_in, *norm_vals)
-    x = latents[0]
 
     group = 2
     marks = [pl.BlockSpec((length, LANES), lambda h: (0, 0))] * 2
@@ -656,34 +652,32 @@
         )(qkv, qkv, qkv, mark_in, mark_out)
 
     ahead = HEADS // 2
-    if ring:
-        later = grow(later, after(taken, hidden_one))
-        taken = swap_all(later, seconds, count)
-        early = swap_all(later, [pair, pair], count)
-        attended, log_sums = zip(*[attend(f, ahead, after(qkv, *later)) for f in (0, ahead)])
-        taken = after(taken, *attended)
-        parts_out = with_pairs(later, taken, early)
-    else:
-        attended, log_sums = zip(*[attend(f, ahead, qkv) for f in (0, ahead)])
+    attended, log_sums = zip(*[attend(f, ahead, qkv) for f in (0, ahead)])
 
     row_block = pl.BlockSpec((block, width), lambda i: (i, 0))
-    (dnorm_two, result, dmid, dmlp, hidden_two, dup, active, dbranch, dattended) = pl.pallas_call(
-        functools.partial(middle_kernel, layout, rows, len(attended)),
+    low_rows = shape((length, width), LOW)
+    result, middle, dmlp, hidden_two, dup, active = pl.pallas_call(
+        functools.partial(middle_kernel, len(attended)),
         grid=steps,
-        out_shape=[
-            shape((2, width), F32),
-            shape((length, width), LOW),
-            shape((length, width), F32),
-            *[shape((length, width), LOW)] * 6,
-        ],
-        in_specs=[SMEM, row_block, row_block, rows_of(live, block), held_rows]
-        + [rows_of(a, block) for a in attended]
-        + [whole(a) for a in parts_out],
-        out_specs=[two_rows] + [row_block] * 8,
-        scratch_shapes=[weight_scratch],
-        compiler_params=params(36),
-        cost_estimate=cost(12 * length * width * width, 12 * width * width),
-    )(table, x, dz, live, norm_vals, *attended, *parts_out)
+        out_shape=[low_rows, shape((length, width), F32), *[low_rows] * 4],
+        in_specs=[row_block, row_block, rows_of(live, block), held_rows, whole(weights_out)]
+        + [rows_of(a, block) for a in attended],
+        out_specs=[row_block] * 6,
+        compiler_params=params(32),
+        cost_estimate=cost(8 * length * width * width, 12 * width * width),
+    )(x, dz, live, norm_vals, weights_out, *attended)
+
+    def middle_back(dup):
+        return pl.pallas_call(
+            middle_back_kernel,
+            grid=steps,
+            out_shape=[shape((length, width), F32), low_rows, low_rows, shape((2, width), F32)],
+            in_specs=[row_block, row_block, row_block, rows_of(live, block), held_rows]
+            + [whole(weights_out)],
+            out_specs=[row_block] * 3 + [two_rows],
+            compiler_params=params(28),
+            cost_estimate=cost(4 * length * width * width, 12 * width * width),
+        )(middle, dup, dz, live, norm_vals, weights_out)
 
     def attend_back(first, number, dattended):
         side = first // ahead
@@ -699,88 +693,121 @@
             cost_estimate=cost(20 * length * length * number * dim, 16 * length * number * dim),
         )(qkv, qkv, qkv, dattended, attended[side], mark_in, mark_out, log_sums[side])
 
-    def last(dmid, grads):
+    def last(dmid, grads, sides):
+        packs = [shape((count // max(sides, 1), 16, LANES), LOW)] * sides
         return pl.pallas_call(
-            functools.partial(last_kernel, layout, rows, len(parts_in)),
+            functools.partial(last_kernel, layout, rows, len(parts_in), sides),
             grid=steps,
-            out_shape=[shape((length, width), LOW), shape((2, width), F32)],
-            in_specs=[SMEM, row_block, row_block, held_rows]
+            out_shape=[low_rows, shape((2, width), F32), *packs],
+            in_specs=[SMEM, row_block, row_block, held_rows, two_rows]
             + [whole(a) for a in parts_in]
             + [rows_of(g, block) for g in grads],
-            out_specs=[row_block, two_rows],
-            scratch_shapes=[weight_scratch],
+            out_specs=[row_block, two_rows]
+            + [pl.BlockSpec(p.shape, lambda i: (0, 0, 0)) for p in packs],
+            scratch_shapes=[weight_scratch, pltpu.VMEM((32, LANES), F32)],
             compiler_params=params(36),
             cost_estimate=cost(6 * length * width * width, 6 * width * width),
-        )(table, x, dmid, norm_vals, *parts_in, *grads)
-
-    out_lefts = [list(attended), [hidden_two], [active]]
-    out_rights = [(0, None, dbranch), (1, None, dup), (2, None, dmlp)]
-    in_lefts = [[hidden_one]] * 3
+        )(table, x, dmid, norm_vals, dnorm_two, *parts_in, *grads)
+
     state, norm_state = (matrices, moment1_mat, moment2_mat), (norm_params, moment1_norm, moment2_norm)
+    in_jobs = [((0,), n, j) for n in range(2) for j in range(3)]
+    mlp = ([hidden_two, active], [dup, dmlp], [((0,), 0, None), ((1,), 1, None)])
     if ring:
-        keep, send = weight_grads(table, out_lefts, out_rights, [], rows, count, 2, 2)
+        pairs = range(1, inner)
+
+        def slots(jobs):
+            return slots_of(jobs, rows, 2)
+
+        slots_mlp = slots([(4, 0, width), (5, 0, width)])
+        heads_w = group * dim
+        slots_one = slots(
+            [(3, 0, width)] + [(j, n * heads_w, heads_w) for n in range(2) for j in range(3)]
+        )
+        slots_two = slots([(j, n * heads_w, heads_w) for n in (2, 3) for j in range(3)])
+
+        keep, send = weight_grads(table, *mlp, rows, count, 2, 2)
         taken = swap(send, pair, count)
-        grads = [attend_back(0, 2, after(dattended, keep))]
+        dmid, dbranch, dattended, dnorm_two = middle_back(after(dup, keep))
+
+        sent = far_sums(keep, after(taken, dattended), [])
+        far = [swap_all(sent, seconds, count)]
+        grads = [attend_back(0, 2, after(dattended, *sent))]
         grads.append(attend_back(2, 2, after(dattended, grads[0])))
-        sums = far_sums(keep, after(taken, grads[1]), [])
-        far_one = swap_all(sums, seconds, count)
-        grads.append(attend_back(4, 2, after(dattended, *sums)))
-        keep_a, send_a = weight_grads(
-            table, in_lefts, [(None, 0, g) for g in grads], [], rows, count, 2, 2
-        )
-        taken_a = swap(send_a, pair, count)
-        grads.append(attend_back(6, 2, after(dattended, keep_a)))
-        sums_a = far_sums(keep_a, after(taken_a, grads[3]), [])
-        far_one_a = swap_all(sums_a, seconds, count)
-        sums = far_sums(keep, taken, [after(far_one, *sums_a)])
-        far_two = swap_all(sums, firsts, count)
-        grad_latents, dnorm_one = last(after(dmid, *sums), grads)
-        keep_b, send_b = weight_grads(
+        keep_one, send_one = weight_grads(
             table,
-            in_lefts,
-            [(None, 0, grads[3])],
-            [dnorm_one, dnorm_two],
+            [*attended, hidden_one],
+            [dbranch, *grads],
+            [((0, 1), 0, None)] + [((2,), 1 + n, j) for _, n, j in in_jobs],
             rows,
             count,
             2,
             2,
         )
-        taken_b = swap(send_b, pair, count)
-        sums_a = far_sums(keep_a, taken_a, [after(far_one_a, keep_b)])
-        far_two_a = swap_all(sums_a, firsts, count)
-        near = near_sums(keep, taken, [far_one, after(far_two, *sums_a)], inner)
-        sums_b = far_sums(keep_b, after(taken_b, *near), [])
-        far_one_b = swap_all(sums_b, seconds, count)
-        near = [near[0]] + swap_all(near[1:], range(1, inner), count)
-        near_a = near_sums(keep_a, taken_a, [far_one_a, after(far_two_a, *sums_b)], inner)
-        near_a = [near_a[0]] + swap_all(near_a[1:], range(1, inner), count)
-        sums_b = far_sums(keep_b, taken_b, [after(far_one_b, near_a[0])])
-        far_two_b = swap_all(sums_b, firsts, count)
-        parts = [(h * width // 2, half_blocks, range(inner), h) for h in range(2)]
-        prior = lamb_call(3, parts, after(near, *sums_b), state, (), None, ())
-        near_b = near_sums(keep_b, taken_b, [far_one_b, after(far_two_b, prior[4])], inner)
-        near_b = [near_b[0]] + swap_all(near_b[1:], range(1, inner), count)
-        a_blocks, b_blocks = 3 * group * dim // 2 // LANES, group * dim // 2 // LANES
-        parts = [(h * a_blocks * LANES, a_blocks, range(inner), h) for h in range(2)] + [
-            ((2 * a_blocks + h * b_blocks) * LANES, b_blocks, range(inner, 2 * inner), h)
-            for h in range(2)
-        ]
-        norm_ends = (range(inner, 2 * inner), 0, 3 * b_blocks * rows)
-        found = lamb_call(0, parts, [*near_a, *near_b], state, norm_state, norm_ends, prior)
+
+        sent = far_sums(keep, taken, after(far, keep_one))
+        far.append(swap_all(sent, firsts, count))
+        taken_one = swap(after(send_one, *sent), pair, count)
+        grads.append(attend_back(4, 2, after(dattended, *sent, keep_one)))
+
+        near = near_sums(keep, taken, [far[0], after(far[1], grads[2])], inner)
+        sent_one = far_sums(keep_one, after(taken_one, grads[2]), [])
+        far_one = [swap_all(sent_one, seconds, count)]
+        near = [near[0]] + swap_all(near[1:], pairs, count)
+        grads.append(attend_back(6, 2, after(dattended, *sent_one, near[0])))
+        keep_two, send_two = weight_grads(
+            table, [hidden_one], grads[2:], in_jobs, rows, count, 2, 2, 16
+        )
+
+        sent_one = far_sums(keep_one, taken_one, after(far_one, keep_two, *near))
+        far_one.append(swap_all(sent_one, firsts, count))
+        taken_two = swap(after(send_two, *sent_one), pair, count)
+        grad_latents, dnorm_one, *packs = last(after(dmid, *sent_one), grads, 2)
+
+        near_one = near_sums(
+            keep_one, taken_one, [far_one[0], after(far_one[1], grad_latents)], inner
+        )
+        near_one = [near_one[0]] + swap_all(near_one[1:], pairs, count)
+        ends = [packs[0], swap(after(packs[1], near_one[0]), pair, count)]
+        groups = [(range(inner), h, slots_mlp[h]) for h in range(2)]
+        prior = lamb_call(4, 2, groups, near, state)
+
+        taken_two, ends[1] = after((taken_two, ends[1]), prior[4])
+        sent_two = far_sums(keep_two, taken_two, [], ends)
+        far_two = [swap_all(sent_two, seconds, count)]
+        sent_two = far_sums(keep_two, taken_two, far_two, ends)
+        far_two.append(swap_all(sent_two, firsts, count))
+        near_one = [near_one[0], *after(near_one[1:], *sent_two)]
+        near_two = near_sums(keep_two, taken_two, far_two, inner, ends)
+        near_two = [near_two[0]] + swap_all(near_two[1:], pairs, count)
+        groups = [(range(inner), h, slots_one[h]) for h in range(2)]
+        groups += [(range(inner, 2 * inner), h, slots_two[h]) for h in range(2)]
+        norm_ends = (range(inner, 2 * inner), 0, near_two[0].shape[1] - 16)
+        found = lamb_call(
+            0, 4, groups, [*near_one, *near_two], state, norm_state, norm_ends, prior
+        )
         grad_mats, m1_mat, m2_mat, dir_mat, squares, grad_norms, m1_norm, m2_norm, dir_norm = found
         squares = hyper_sum(squares, count)[:2, :10]
     else:
-        (out_grads,) = weight_grads(table, out_lefts, out_rights, [], rows, 1, 1, 1)
+        dmid, dbranch, dattended, dnorm_two = middle_back(dup)
         grads = [attend_back(f, ahead, dattended) for f in (0, ahead)]
+        (mlp_grads,) = weight_grads(table, *mlp, rows, 1, 1, 1)
         (in_grads,) = weight_grads(
-            table, in_lefts, [(None, 0, g) for g in grads], [], rows, 1, 1, 1
-        )
-        grad_latents, dnorm_one = last(dmid, grads)
+            table,
+            [*attended, hidden_one],
+            [dbranch, *grads],
+            [((0, 1), 0, None)] + [((2,), 1 + n, j) for j in range(3) for n in range(2)],
+            rows,
+            1,
+            1,
+            1,
+        )
+        grad_latents, dnorm_one = last(dmid, grads, 0)
         norms_local = jnp.concatenate([dnorm_one, dnorm_two], 0)
-        mats_local = jnp.concatenate([in_grads[0, 0], out_grads[0, 0]], 0).astype(F32)
-        mats_local = mats_local.reshape(6, width // LANES, width, LANES)
-        mats_local = mats_local.transpose(0, 2, 1, 3).reshape(6, width, width)
-        grad_mats = lax.psum_scatter(mats_local, AXES, scatter_dimension=1, tiled=True)
+        local = jnp.concatenate([in_grads[0, 0], mlp_grads[0, 0]], 0).astype(F32)
+        local = local.reshape(6, width // LANES, width, LANES)
+        local = local.transpose(0, 2, 1, 3).reshape(6, width, width)
+        local = jnp.concatenate([local[1:4], local[:1], local[4:]], 0)
+        grad_mats = lax.psum_scatter(local, AXES, scatter_dimension=1, tiled=True)
         grad_norms = lax.psum_scatter(norms_local, AXES, scatter_dimension=1, tiled=True)
         m1_mat, m2_mat, dir_mat = lamb_values(matrices, grad_mats, moment1_mat, moment2_mat)
         m1_norm, m2_norm, dir_norm = lamb_values(norm_params, grad_norms, moment1_norm, moment2_norm)

time: 280 us -> 274 us (0.979)
  waiting for transfers between devices: 111 us -> 94.8 us
  between operations: 1.69 us -> 15 us
  starting transfers between devices: 57.4 us -> 47.2 us
  local copies, waits for them, and re-layouts: 12.5 us -> 16.9 us
  Pallas kernels: 89.8 us -> 93.4 us
    ppermute x51 -> x41, waiting for transfers between devices: 111 us -> 94.7 us  [swap(): return lax.ppermute(value, AXES, [(i, i ^ mask) for i in range(count)])]
    ppermute x51 -> x41, starting transfers between devices: 57.4 us -> 47.2 us  [swap(): return lax.ppermute(value, AXES, [(i, i ^ mask) for i in range(count)])]
    unnamed x100 -> x74, local copies, waits for them, and re-layouts: 11.6 us -> 15.4 us
    pallas_call x6 -> x7, Pallas kernels: 41.4 us -> 42.7 us  [the longest x3 26.1 us: weight_grads(): pl.pallas_call(functools.partial(weight_grad_kernel, jobs, rows, len(left...]
  transfers between devices with their start and end apart: 51 -> 42, of which waited for: 27 -> 20; matrix products, arithmetic and copies ran while one was open for 1% -> 1% of each run, Pallas kernels for 12% -> 28%
where the time goes in v3:
time: 274 us; the launch traced here: 271 us
  waiting for transfers between devices  94.8 us (35%)
  Pallas kernels  93.4 us (34%)
  starting transfers between devices  47.2 us (17%)
  local copies, waits for them, and re-layouts  16.9 us (6%)
  between operations  15 us (5%)
  other arithmetic  4.15 us (2%)
    ppermute x41, waiting for transfers between devices, swap(): return lax.ppermute(value, AXES, [(i, i ^ mask) for i in range(count)])  94.7 us
    ppermute x41, starting transfers between devices, swap(): return lax.ppermute(value, AXES, [(i, i ^ mask) for i in range(count)])  47.2 us
    pallas_call x3, Pallas kernels, weight_grads(): pl.pallas_call(functools.partial(weight_grad_kernel, jobs, rows, len(left...  26.1 us
    pallas_call x4, Pallas kernels, attend_back(): pl.pallas_call(functools.partial(attend_back_kernel, group, dim, power, s...  15.6 us
    unnamed x74, local copies, waits for them, and re-layouts  15.4 us
    pallas_call x1, Pallas kernels, last(): pl.pallas_call(functools.partial(last_kernel, layout, rows, len(parts_in)...  12.2 us
    pallas_call x1, Pallas kernels, on_device(): pl.pallas_call(functools.partial(project_kernel, layout, rows, norm_row,...  10.7 us
    pallas_call x2, Pallas kernels, attend(): pl.pallas_call(functools.partial(attend_kernel, group, dim, power), grid=...  10 us
  transfers between devices with their start and end apart: 42, of which 20 were waited for; matrix products, arithmetic and copies ran while one was open for 1% of the time, Pallas kernels for 28%

profile of v3, /device:TPU:0, one launch (start us, length us, event | category | flops | bytes accessed | tf_op | source)
XLA Modules:
  0.0 271.4 jit_solution(5305013656932882380)
XLA Ops:
  9.4 5.1 %collective-permute-start.2 = (bf16[2,400,128]{2,1,0:T(8,128)(2,1)S(1)}, bf16[2,400,128]{2,1,0:T(8,128)(2,1)S(1)}, u32[]{:S(2)}, u32[]{:S(2)}) collective-permute-start(bf16[2,400,128]{2,1,0:T(8,128)(2,1)S(1)} %fusion.3), channel_id=1, source_target_pairs={{0,3},{1,2},{2,1},{3,0},{4,7},{5,6},{6,5},{7,4},{8,11},{9,10},{10,... | collective-permute-start | bytes 614408 | tf_op jit(solution)/shard_map/ppermute | solution.py:61
  15.3 15.4 %collective-permute-done = bf16[2,400,128]{2,1,0:T(8,128)(2,1)S(1)} collective-permute-done((bf16[2,400,128]{2,1,0:T(8,128)(2,1)S(1)}, bf16[2,400,128]{2,1,0:T(8,128)(2,1)S(1)}, u32[]{:S(2)}, u32[]{:S(2)}) %collective-permute-start) | collective-permute-done | bytes 204832 | tf_op jit(solution)/shard_map/ppermute | solution.py:61
  30.7 5.3 %collective-permute-done.1 = bf16[2,400,128]{2,1,0:T(8,128)(2,1)S(1)} collective-permute-done((bf16[2,400,128]{2,1,0:T(8,128)(2,1)S(1)}, bf16[2,400,128]{2,1,0:T(8,128)(2,1)S(1)}, u32[]{:S(2)}, u32[]{:S(2)}) %collective-permute-start.1) | collective-permute-done | bytes 204832 | tf_op jit(solution)/shard_map/ppermute | solution.py:61
  36.2 1.6 collective-permute-start.7
  37.9 1.6 collective-permute-start.3
  39.5 9.4 %collective-permute-done.7 = bf16[4,400,128]{2,1,0:T(8,128)(2,1)S(1)} collective-permute-done((bf16[4,400,128]{2,1,0:T(8,128)(2,1)S(1)}, bf16[4,400,128]{2,1,0:T(8,128)(2,1)S(1)}, u32[]{:S(2)}, u32[]{:S(2)}) %collective-permute-start.7) | collective-permute-done | bytes 409632 | tf_op jit(solution)/shard_map/ppermute | solution.py:61
  49.0 1.8 collective-permute-start.8
  50.7 4.7 %collective-permute-done.3 = bf16[4,400,128]{2,1,0:T(8,128)(2,1)S(1)} collective-permute-done((bf16[4,400,128]{2,1,0:T(8,128)(2,1)S(1)}, bf16[4,400,128]{2,1,0:T(8,128)(2,1)S(1)}, u32[]{:S(2)}, u32[]{:S(2)}) %collective-permute-start.3) | collective-permute-done | bytes 409632 | tf_op jit(solution)/shard_map/ppermute | solution.py:61
  56.4 21.5 %collective-permute-done.8.refs_5_ = bf16[8,400,128]{2,1,0:T(8,128)(2,1)} collective-permute-done((bf16[8,400,128]{2,1,0:T(8,128)(2,1)S(1)}, bf16[8,400,128]{2,1,0:T(8,128)(2,1)}, u32[]{:S(2)}, u32[]{:S(2)}) %collective-permute-start.8) | collective-permute-done | bytes 819232 | tf_op jit(solution)/shard_map/ppermute | solution.py:61
  79.1 1.6 collective-permute-done.10.refs_7_
  84.4 10.7 %shard_map.185 = (bf16[768,1024]{1,0:T(8,128)(2,1)S(1)}, bf16[768,3072]{1,0:T(8,128)(2,1)S(1)}, f32[4,1024]{1,0:T(4,128)S(1)}) custom-call(s32[2,32]{1,0:T(2,128)S(1)} %broadcast_xor_fusion.table_ref, bf16[768,1024]{1,0:T(8,128)(2,1)S(1)} %bitcast.20, bf16[8,400,128]{2,1,0:T(8,128)(2,1)S(1)} %constant_dynamic-update-slice_fusion.refs_0_, ...), custom_call_target="tpu_custom_call" | custom-call | flops 4831838208 | bytes 12582912 | tf_op jit(solution)/shard_map/pallas_call | solution.py:613
  95.2 5.0 %shard_map.187 = (bf16[768,512]{1,0:T(8,128)(2,1)S(1)}, f32[4,1,768]{2,1,0:T(1,128)S(1)}) custom-call(bf16[768,3072]{1,0:T(8,128)(2,1)S(1)} %get-tuple-element.100.q_ref.k_ref.v_ref, bf16[768,3072]{1,0:T(8,128)(2,1)S(1)} %get-tuple-element.100.q_ref.k_ref.v_ref, bf16[768,3072]{1,0:T(8,128)(2,1)S(1)} %get-tuple-element.100.q_ref.k_ref.v_ref, ...), custom_call_target="tpu_custom_call" | custom-call | flops 2415919104 | bytes 3145728 | tf_op jit(solution)/shard_map/pallas_call | solution.py:644
  100.2 5.0 %shard_map.186 = (bf16[768,512]{1,0:T(8,128)(2,1)S(1)}, f32[4,1,768]{2,1,0:T(1,128)S(1)}) custom-call(bf16[768,3072]{1,0:T(8,128)(2,1)S(1)} %get-tuple-element.100.q_ref.k_ref.v_ref, bf16[768,3072]{1,0:T(8,128)(2,1)S(1)} %get-tuple-element.100.q_ref.k_ref.v_ref, bf16[768,3072]{1,0:T(8,128)(2,1)S(1)} %get-tuple-element.100.q_ref.k_ref.v_ref, ...), custom_call_target="tpu_custom_call" | custom-call | flops 2415919104 | bytes 3145728 | tf_op jit(solution)/shard_map/pallas_call | solution.py:644
  105.3 2.8 %copy-done.2 = bf16[3,1024,1024]{2,1,0:T(8,128)(2,1)S(1)} copy-done((bf16[3,1024,1024]{2,1,0:T(8,128)(2,1)S(1)}, bf16[3,1024,1024]{2,1,0:T(8,128)(2,1)}, u32[]{:S(2)}) %copy-start.2) | copy-done | bytes 6291480
  110.9 8.8 %shard_map.188 = (bf16[768,1024]{1,0:T(8,128)(2,1)}, f32[768,1024]{1,0:T(8,128)S(1)}, bf16[768,1024]{1,0:T(8,128)(2,1)S(1)}, bf16[768,1024]{1,0:T(8,128)(2,1)S(1...) custom-call(bf16[768,1024]{1,0:T(8,128)(2,1)S(1)} %bitcast.21, bf16[768,1024]{1,0:T(8,128)(2,1)S(1)} %bitcast.18, ...), custom_call_target="tpu_custom_call" | custom-call | flops 6442450944 | bytes 12582912 | tf_op jit(solution)/shard_map/pallas_call | solution.py:659
  119.6 6.6 %shard_map.189 = (bf16[2,16,256,128]{3,2,1,0:T(8,128)(2,1)S(1)}, bf16[2,16,256,128]{3,2,1,0:T(8,128)(2,1)S(1)}) custom-call(s32[2,32]{1,0:T(2,128)S(1)} %broadcast_xor_fusion.table_ref, bf16[768,1024]{1,0:T(8,128)(2,1)S(1)} %get-tuple-element.106.refs_0_, bf16[768,1024]{1,0:T(8,128)(2,1)S(1)} %get-tuple-element.107.refs_1_, ...), custom_call_target="tpu_custom_call" | custom-call | flops 3221225472 | bytes 8388608 | tf_op jit(solution)/shard_map/pallas_call | solution.py:356
  126.3 2.9 %copy-done.3 = bf16[3,1024,1024]{2,1,0:T(8,128)(2,1)S(1)} copy-done((bf16[3,1024,1024]{2,1,0:T(8,128)(2,1)S(1)}, bf16[3,1024,1024]{2,1,0:T(8,128)(2,1)}, u32[]{:S(2)}) %copy-start.3) | copy-done | bytes 6291480
  129.3 1.5 copy-done.9
  130.8 5.4 %shard_map.190 = (f32[768,1024]{1,0:T(8,128)S(1)}, bf16[768,1024]{1,0:T(8,128)(2,1)S(1)}, bf16[768,1024]{1,0:T(8,128)(2,1)S(1)}, f32[2,1024]{1,0:T(2,128)S(1)}) custom-call(f32[768,1024]{1,0:T(8,128)S(1)} %get-tuple-element.104.middle_ref, bf16[768,1024]{1,0:T(8,128)(2,1)S(1)} %copy-done.9, bf16[768,1024]{1,0:T(8,128)(2,1)S(1)} %bitcast.19, ...), custom_call_target="tpu_custom_call" | custom-call | flops 3221225472 | bytes 12582912 | tf_op jit(solution)/shard_map/pallas_call | solution.py:671
  137.9 2.9 %collective-permute-start.13 = (bf16[8,256,128]{2,1,0:T(8,128)(2,1)S(1)}, bf16[8,256,128]{2,1,0:T(8,128)(2,1)S(1)}, u32[]{:S(2)}, u32[]{:S(2)}) collective-permute-start(bf16[8,256,128]{2,1,0:T(8,128)(2,1)S(1)} %get-tuple-element.118), channel_id=1, source_target_pairs={{0,8},{1,9},{2,10},{3,11},{4,12},{5,13},{6,14},{7,15},{8,0},{9,1},... | collective-permute-start | bytes 1572872 | tf_op jit(solution)/shard_map/ppermute | solution.py:61
  140.7 3.9 %shard_map.192.refs_4_.refs_8_ = bf16[3,768,256]{2,1,0:T(8,128)(2,1)S(1)} custom-call(bf16[768,3072]{1,0:T(8,128)(2,1)S(1)} %bitcast.17, bf16[768,3072]{1,0:T(8,128)(2,1)S(1)} %bitcast.17, bf16[768,3072]{1,0:T(8,128)(2,1)S(1)} %bitcast.17, bf16[768,1024]{1,0:T(8,128)(2,1)S(1)} %get-tuple-element.137.do_ref, ...), custom_call_target="tpu_custom_call" | custom-call | flops 3019898880 | bytes 3145728 | tf_op jit(solution)/shard_map/pallas_call | solution.py:685
  144.7 3.9 %shard_map.193.refs_5_.refs_9_ = bf16[3,768,256]{2,1,0:T(8,128)(2,1)S(1)} custom-call(bf16[768,3072]{1,0:T(8,128)(2,1)S(1)} %bitcast.17, bf16[768,3072]{1,0:T(8,128)(2,1)S(1)} %bitcast.17, bf16[768,3072]{1,0:T(8,128)(2,1)S(1)} %bitcast.17, bf16[768,1024]{1,0:T(8,128)(2,1)S(1)} %get-tuple-element.137.do_ref, ...), custom_call_target="tpu_custom_call" | custom-call | flops 3019898880 | bytes 3145728 | tf_op jit(solution)/shard_map/pallas_call | solution.py:685
  148.6 10.9 %shard_map.194 = (bf16[2,16,320,128]{3,2,1,0:T(8,128)(2,1)S(1)}, bf16[2,16,320,128]{3,2,1,0:T(8,128)(2,1)S(1)}) custom-call(s32[2,32]{1,0:T(2,128)S(1)} %broadcast_xor_fusion.table_ref, bf16[768,512]{1,0:T(8,128)(2,1)S(1)} %get-tuple-element.101.refs_0_.o_ref, bf16[768,512]{1,0:T(8,128)(2,1)S(1)} %get-tuple-element.102.refs_1_.o_ref, ...), custom_call_target="tpu_custom_call" | custom-call | flops 4026531840 | bytes 10485760 | tf_op jit(solution)/shard_map/pallas_call | solution.py:356
  160.2 1.7 collective-permute-start.18
  162.0 3.9 %shard_map.196.refs_1_.refs_10_ = bf16[3,768,256]{2,1,0:T(8,128)(2,1)S(1)} custom-call(bf16[768,3072]{1,0:T(8,128)(2,1)S(1)} %bitcast.17, bf16[768,3072]{1,0:T(8,128)(2,1)S(1)} %bitcast.17, bf16[768,3072]{1,0:T(8,128)(2,1)S(1)} %bitcast.17, bf16[768,1024]{1,0:T(8,128)(2,1)S(1)} %get-tuple-element.137.do_ref, ...), custom_call_target="tpu_custom_call" | custom-call | flops 3019898880 | bytes 3145728 | tf_op jit(solution)/shard_map/pallas_call | solution.py:685
  169.1 1.9 collective-permute-start.20
  171.0 2.5 collective-permute-start.21
  173.5 3.9 %shard_map.199.refs_2_.refs_11_ = bf16[3,768,256]{2,1,0:T(8,128)(2,1)S(1)} custom-call(bf16[768,3072]{1,0:T(8,128)(2,1)S(1)} %bitcast.17, bf16[768,3072]{1,0:T(8,128)(2,1)S(1)} %bitcast.17, bf16[768,3072]{1,0:T(8,128)(2,1)S(1)} %bitcast.17, bf16[768,1024]{1,0:T(8,128)(2,1)S(1)} %get-tuple-element.137.do_ref, ...), custom_call_target="tpu_custom_call" | custom-call | flops 3019898880 | bytes 3145728 | tf_op jit(solution)/shard_map/pallas_call | solution.py:685
  177.4 8.6 %shard_map.200 = (bf16[2,16,208,128]{3,2,1,0:T(8,128)(2,1)S(1)}, bf16[2,16,208,128]{3,2,1,0:T(8,128)(2,1)}) custom-call(s32[2,32]{1,0:T(2,128)S(1)} %broadcast_xor_fusion.table_ref, bf16[768,1024]{1,0:T(8,128)(2,1)S(1)} %copy-done.32, bf16[3,768,256]{2,1,0:T(8,128)(2,1)S(1)} %shard_map.196.refs_1_.refs_10_, bf16[3,768,256]{2,1,0:T(8,128)(2,1)S(1)} %shard_map.199.refs_2_.refs_11_), custom_call_target="tpu_custom_call" | custom-call | flops 2415919104 | bytes 6291456 | tf_op jit(solution)/shard_map/pallas_call | solution.py:356
  186.5 1.9 collective-permute-start.22
  188.3 2.5 collective-permute-start.23
  190.9 12.2 %shard_map.202 = (bf16[768,1024]{1,0:T(8,128)(2,1)}, f32[2,1024]{1,0:T(2,128)}, bf16[16,16,128]{2,1,0:T(8,128)(2,1)S(1)}, bf16[16,16,128]{2,1,0:T(8,128)(2,1)S(1)}) custom-call(s32[2,32]{1,0:T(2,128)S(1)} %broadcast_xor_fusion.table_ref, bf16[768,1024]{1,0:T(8,128)(2,1)S(1)} %bitcast.22, f32[768,1024]{1,0:T(8,128)S(1)} %copy-done.27, ...), custom_call_target="tpu_custom_call" | custom-call | flops 4831838208 | bytes 6291456 | tf_op jit(solution)/shard_map/pallas_call | solution.py:698
  205.7 2.0 collective-permute-start.30
  207.7 9.3 %collective-permute-done.29.refs_2_ = bf16[8,208,128]{2,1,0:T(8,128)(2,1)S(1)} collective-permute-done((bf16[8,208,128]{2,1,0:T(8,128)(2,1)S(1)}, bf16[8,208,128]{2,1,0:T(8,128)(2,1)S(1)}, u32[]{:S(2)}, u32[]{:S(2)}) %collective-permute-start.29) | collective-permute-done | bytes 426016 | tf_op jit(solution)/shard_map/ppermute | solution.py:61
  217.4 1.8 collective-permute-start.31
  219.5 1.9 collective-permute-start.25
  221.4 2.5 collective-permute-start.26
  225.3 1.9 collective-permute-start.34
  227.5 2.2 collective-permute-start.35
  229.7 8.8 %collective-permute-done.25.refs_8_ = bf16[2,320,128]{2,1,0:T(8,128)(2,1)S(1)} collective-permute-done((bf16[2,320,128]{2,1,0:T(8,128)(2,1)S(1)}, bf16[2,320,128]{2,1,0:T(8,128)(2,1)S(1)}, u32[]{:S(2)}, u32[]{:S(2)}) %collective-permute-start.25) | collective-permute-done | bytes 163872 | tf_op jit(solution)/shard_map/ppermute | solution.py:61
  238.5 5.0 %collective-permute-done.34.refs_12_ = bf16[2,208,128]{2,1,0:T(8,128)(2,1)S(1)} collective-permute-done((bf16[2,208,128]{2,1,0:T(8,128)(2,1)S(1)}, bf16[2,208,128]{2,1,0:T(8,128)(2,1)S(1)}, u32[]{:S(2)}, u32[]{:S(2)}) %collective-permute-start.34) | collective-permute-done | bytes 106528 | tf_op jit(solution)/shard_map/ppermute | solution.py:61
  243.5 2.1 shard_map.208
  245.5 1.7 collective-permute-start.36
  247.2 1.9 collective-permute-done.36
  249.2 1.7 collective-permute-start.37
  250.8 2.8 %collective-permute-done.37 = f32[8,128]{1,0:T(8,128)S(1)} collective-permute-done((f32[8,128]{1,0:T(8,128)S(1)}, f32[8,128]{1,0:T(8,128)S(1)}, u32[]{:S(2)}, u32[]{:S(2)}) %collective-permute-start.37) | collective-permute-done | bytes 4128 | tf_op jit(solution)/shard_map/ppermute | solution.py:61
  256.1 2.3 collective-permute-done.39
  259.8 2.3 collective-permute-done.40
  (171 shorter events, 29.0 us)
Async XLA Ops:
  7.2 98.1 %all-gather.2.cloned.1.call-start = ((), (), s32[]{:S(2)}) async-start(), calls=%async_computation | async-start | bytes 6488064 | tf_op jit(solution)/shard_map/all_gather | solution.py:585
  9.4 26.6 %collective-permute-start.2 = (bf16[2,400,128]{2,1,0:T(8,128)(2,1)S(1)}, bf16[2,400,128]{2,1,0:T(8,128)(2,1)S(1)}, u32[]{:S(2)}, u32[]{:S(2)}) collective-permute-start(bf16[2,400,128]{2,1,0:T(8,128)(2,1)S(1)} %fusion.3), channel_id=1, source_target_pairs={{0,3},{1,2},{2,1},{3,0},{4,7},{5,6},{6,5},{7,4},{8,11},{9,10},{10,... | collective-permute-start | bytes 614408 | tf_op jit(solution)/shard_map/ppermute | solution.py:61
  14.6 21.4 %collective-permute-start.1 = (bf16[2,400,128]{2,1,0:T(8,128)(2,1)S(1)}, bf16[2,400,128]{2,1,0:T(8,128)(2,1)S(1)}, u32[]{:S(2)}, u32[]{:S(2)}) collective-permute-start(bf16[2,400,128]{2,1,0:T(8,128)(2,1)S(1)} %fusion.3), channel_id=1, source_target_pairs={{0,2},{1,3},{2,0},{3,1},{4,6},{5,7},{6,4},{7,5},{8,10},{9,11},{10,... | collective-permute-start | bytes 614408 | tf_op jit(solution)/shard_map/ppermute | solution.py:61
  14.6 16.1 %collective-permute-start = (bf16[2,400,128]{2,1,0:T(8,128)(2,1)S(1)}, bf16[2,400,128]{2,1,0:T(8,128)(2,1)S(1)}, u32[]{:S(2)}, u32[]{:S(2)}) collective-permute-start(bf16[2,400,128]{2,1,0:T(8,128)(2,1)S(1)} %fusion.3), channel_id=1, source_target_pairs={{0,1},{1,0},{2,3},{3,2},{4,5},{5,4},{6,7},{7,6},{8,9},{9,8},{10,11... | collective-permute-start | bytes 614408 | tf_op jit(solution)/shard_map/ppermute | solution.py:61
  36.1 19.5 %copy-start.34 = (s32[1,4]{1,0:T(1,128)S(1)}, s32[1,4]{1,0:T(1,128)}, u32[]{:S(2)}) copy-start(s32[1,4]{1,0:T(1,128)} %param.11) | copy-start | bytes 52
  36.2 42.5 %copy-start.33 = (s32[2,32]{1,0:T(2,128)S(1)}, s32[2,32]{1,0:T(2,128)}, u32[]{:S(2)}) copy-start(s32[2,32]{1,0:T(2,128)} %constant.27.clone) | copy-start | bytes 772
  36.2 12.7 %collective-permute-start.7 = (bf16[4,400,128]{2,1,0:T(8,128)(2,1)S(1)}, bf16[4,400,128]{2,1,0:T(8,128)(2,1)S(1)}, u32[]{:S(2)}, u32[]{:S(2)}) collective-permute-start(bf16[4,400,128]{2,1,0:T(8,128)(2,1)S(1)} %pad_maximum_fusion.1), channel_id=1, source_target_pairs={{0,16},{1,17},{2,18},{3,19},{4,20},{5,21},{6,22},{7,23},{8,24},{9,... | collective-permute-start | bytes 1228808 | tf_op jit(solution)/shard_map/ppermute | solution.py:61
  37.9 17.5 %collective-permute-start.3 = (bf16[4,400,128]{2,1,0:T(8,128)(2,1)S(1)}, bf16[4,400,128]{2,1,0:T(8,128)(2,1)S(1)}, u32[]{:S(2)}, u32[]{:S(2)}) collective-permute-start(bf16[4,400,128]{2,1,0:T(8,128)(2,1)S(1)} %pad_maximum_fusion), channel_id=1, source_target_pairs={{0,8},{1,9},{2,10},{3,11},{4,12},{5,13},{6,14},{7,15},{8,0},{9,1},... | collective-permute-start | bytes 1228808 | tf_op jit(solution)/shard_map/ppermute | solution.py:61
  49.0 32.9 %copy-start.20 = (bf16[8,400,128]{2,1,0:T(8,128)(2,1)}, bf16[8,400,128]{2,1,0:T(8,128)(2,1)S(1)}, u32[]{:S(2)}) copy-start(bf16[8,400,128]{2,1,0:T(8,128)(2,1)S(1)} %constant_dynamic-update-slice_fusion.5.refs_4_) | copy-start | bytes 2457604
  49.0 29.0 %collective-permute-start.8 = (bf16[8,400,128]{2,1,0:T(8,128)(2,1)S(1)}, bf16[8,400,128]{2,1,0:T(8,128)(2,1)}, u32[]{:S(2)}, u32[]{:S(2)}) collective-permute-start(bf16[8,400,128]{2,1,0:T(8,128)(2,1)S(1)} %constant_dynamic-update-slice_fusion.5.refs_4_), channel_id=1, source_target_pairs={{0,8},{1,9},{2,10},{3,11},{4,12},{5,13},{6,14},{7,15},{8,0},{9,1},... | collective-permute-start | bytes 2457608 | tf_op jit(solution)/shard_map/ppermute | solution.py:61
  55.5 39.7 %copy-start.18 = (bf16[8,400,128]{2,1,0:T(8,128)(2,1)}, bf16[8,400,128]{2,1,0:T(8,128)(2,1)S(1)}, u32[]{:S(2)}) copy-start(bf16[8,400,128]{2,1,0:T(8,128)(2,1)S(1)} %constant_dynamic-update-slice_fusion.refs_0_) | copy-start | bytes 2457604
  55.5 22.5 %collective-permute-start.4 = (bf16[8,400,128]{2,1,0:T(8,128)(2,1)S(1)}, bf16[8,400,128]{2,1,0:T(8,128)(2,1)}, u32[]{:S(2)}, u32[]{:S(2)}) collective-permute-start(bf16[8,400,128]{2,1,0:T(8,128)(2,1)S(1)} %constant_dynamic-update-slice_fusion.refs_0_), channel_id=1, source_target_pairs={{0,16},{1,17},{2,18},{3,19},{4,20},{5,21},{6,22},{7,23},{8,24},{9,... | collective-permute-start | bytes 2457608 | tf_op jit(solution)/shard_map/ppermute | solution.py:61
  55.9 23.2 %collective-permute-start.9 = (bf16[8,400,128]{2,1,0:T(8,128)(2,1)S(1)}, bf16[8,400,128]{2,1,0:T(8,128)(2,1)}, u32[]{:S(2)}, u32[]{:S(2)}) collective-permute-start(bf16[8,400,128]{2,1,0:T(8,128)(2,1)S(1)} %constant_dynamic-update-slice_fusion.5.refs_4_), channel_id=1, source_target_pairs={{0,4},{1,5},{2,6},{3,7},{4,0},{5,1},{6,2},{7,3},{8,12},{9,13},{10,... | collective-permute-start | bytes 2457608 | tf_op jit(solution)/shard_map/ppermute | solution.py:61
  55.9 23.1 %collective-permute-start.5 = (bf16[8,400,128]{2,1,0:T(8,128)(2,1)S(1)}, bf16[8,400,128]{2,1,0:T(8,128)(2,1)}, u32[]{:S(2)}, u32[]{:S(2)}) collective-permute-start(bf16[8,400,128]{2,1,0:T(8,128)(2,1)S(1)} %constant_dynamic-update-slice_fusion.refs_0_), channel_id=1, source_target_pairs={{0,4},{1,5},{2,6},{3,7},{4,0},{5,1},{6,2},{7,3},{8,12},{9,13},{10,... | collective-permute-start | bytes 2457608 | tf_op jit(solution)/shard_map/ppermute | solution.py:61
  78.0 2.7 collective-permute-start.10
  78.0 3.8 %collective-permute-start.6 = (bf16[8,400,128]{2,1,0:T(8,128)(2,1)}, bf16[8,400,128]{2,1,0:T(8,128)(2,1)}, u32[]{:S(2)}, u32[]{:S(2)}) collective-permute-start(bf16[8,400,128]{2,1,0:T(8,128)(2,1)} %collective-permute-done.4.refs_1_), channel_id=1, source_target_pairs={{0,4},{1,5},{2,6},{3,7},{4,0},{5,1},{6,2},{7,3},{8,12},{9,13},{10,... | collective-permute-start | bytes 2457608 | tf_op jit(solution)/shard_map/ppermute | solution.py:61
  126.2 10.0 %collective-permute-start.11 = (bf16[2,16,256,128]{3,2,1,0:T(8,128)(2,1)S(1)}, bf16[2,16,256,128]{3,2,1,0:T(8,128)(2,1)S(1)}, u32[]{:S(2)}, u32[]{:S(2)}) collective-permute-start(bf16[2,16,256,128]{3,2,1,0:T(8,128)(2,1)S(1)} %get-tuple-element.115), channel_id=1, source_target_pairs={{0,4},{1,5},{2,6},{3,7},{4,0},{5,1},{6,2},{7,3},{8,12},{9,13},{10,... | collective-permute-start | bytes 6291464 | tf_op jit(solution)/shard_map/ppermute | solution.py:61
  137.9 21.6 %collective-permute-start.12 = (bf16[8,256,128]{2,1,0:T(8,128)(2,1)S(1)}, bf16[8,256,128]{2,1,0:T(8,128)(2,1)S(1)}, u32[]{:S(2)}, u32[]{:S(2)}) collective-permute-start(bf16[8,256,128]{2,1,0:T(8,128)(2,1)S(1)} %get-tuple-element.117), channel_id=1, source_target_pairs={{0,16},{1,17},{2,18},{3,19},{4,20},{5,21},{6,22},{7,23},{8,24},{9,... | collective-permute-start | bytes 1572872 | tf_op jit(solution)/shard_map/ppermute | solution.py:61
  137.9 21.6 %collective-permute-start.13 = (bf16[8,256,128]{2,1,0:T(8,128)(2,1)S(1)}, bf16[8,256,128]{2,1,0:T(8,128)(2,1)S(1)}, u32[]{:S(2)}, u32[]{:S(2)}) collective-permute-start(bf16[8,256,128]{2,1,0:T(8,128)(2,1)S(1)} %get-tuple-element.118), channel_id=1, source_target_pairs={{0,8},{1,9},{2,10},{3,11},{4,12},{5,13},{6,14},{7,15},{8,0},{9,1},... | collective-permute-start | bytes 1572872 | tf_op jit(solution)/shard_map/ppermute | solution.py:61
  159.7 6.2 %collective-permute-start.14 = (bf16[2,16,320,128]{3,2,1,0:T(8,128)(2,1)S(1)}, bf16[2,16,320,128]{3,2,1,0:T(8,128)(2,1)S(1)}, u32[]{:S(2)}, u32[]{:S(2)}) collective-permute-start(bf16[2,16,320,128]{3,2,1,0:T(8,128)(2,1)S(1)} %get-tuple-element.128), channel_id=1, source_target_pairs={{0,4},{1,5},{2,6},{3,7},{4,0},{5,1},{6,2},{7,3},{8,12},{9,13},{10,... | collective-permute-start | bytes 7864328 | tf_op jit(solution)/shard_map/ppermute | solution.py:61
  159.9 8.5 %collective-permute-start.17 = (bf16[4,256,128]{2,1,0:T(8,128)(2,1)S(1)}, bf16[4,256,128]{2,1,0:T(8,128)(2,1)S(1)}, u32[]{:S(2)}, u32[]{:S(2)}) collective-permute-start(bf16[4,256,128]{2,1,0:T(8,128)(2,1)S(1)} %get-tuple-element.126), channel_id=1, source_target_pairs={{0,8},{1,9},{2,10},{3,11},{4,12},{5,13},{6,14},{7,15},{8,0},{9,1},... | collective-permute-start | bytes 786440 | tf_op jit(solution)/shard_map/ppermute | solution.py:61
  160.2 8.6 %collective-permute-start.18 = (bf16[4,256,128]{2,1,0:T(8,128)(2,1)S(1)}, bf16[4,256,128]{2,1,0:T(8,128)(2,1)S(1)}, u32[]{:S(2)}, u32[]{:S(2)}) collective-permute-start(bf16[4,256,128]{2,1,0:T(8,128)(2,1)S(1)} %get-tuple-element.127), channel_id=1, source_target_pairs={{0,16},{1,17},{2,18},{3,19},{4,20},{5,21},{6,22},{7,23},{8,24},{9,... | collective-permute-start | bytes 786440 | tf_op jit(solution)/shard_map/ppermute | solution.py:61
  166.2 19.9 %collective-permute-start.15 = (bf16[8,320,128]{2,1,0:T(8,128)(2,1)S(1)}, bf16[8,320,128]{2,1,0:T(8,128)(2,1)S(1)}, u32[]{:S(2)}, u32[]{:S(2)}) collective-permute-start(bf16[8,320,128]{2,1,0:T(8,128)(2,1)S(1)} %get-tuple-element.132), channel_id=1, source_target_pairs={{0,16},{1,17},{2,18},{3,19},{4,20},{5,21},{6,22},{7,23},{8,24},{9,... | collective-permute-start | bytes 1966088 | tf_op jit(solution)/shard_map/ppermute | solution.py:61
  167.1 19.0 %collective-permute-start.16 = (bf16[8,320,128]{2,1,0:T(8,128)(2,1)S(1)}, bf16[8,320,128]{2,1,0:T(8,128)(2,1)S(1)}, u32[]{:S(2)}, u32[]{:S(2)}) collective-permute-start(bf16[8,320,128]{2,1,0:T(8,128)(2,1)S(1)} %get-tuple-element.133), channel_id=1, source_target_pairs={{0,8},{1,9},{2,10},{3,11},{4,12},{5,13},{6,14},{7,15},{8,0},{9,1},... | collective-permute-start | bytes 1966088 | tf_op jit(solution)/shard_map/ppermute | solution.py:61
  169.0 17.0 %collective-permute-start.19 = (bf16[2,256,128]{2,1,0:T(8,128)(2,1)S(1)}, bf16[2,256,128]{2,1,0:T(8,128)(2,1)S(1)}, u32[]{:S(2)}, u32[]{:S(2)}) collective-permute-start(bf16[2,256,128]{2,1,0:T(8,128)(2,1)S(1)} %get-tuple-element.139), channel_id=1, source_target_pairs={{0,1},{1,0},{2,3},{3,2},{4,5},{5,4},{6,7},{7,6},{8,9},{9,8},{10,11... | collective-permute-start | bytes 393224 | tf_op jit(solution)/shard_map/ppermute | solution.py:61
  169.1 17.0 %collective-permute-start.20 = (bf16[2,256,128]{2,1,0:T(8,128)(2,1)S(1)}, bf16[2,256,128]{2,1,0:T(8,128)(2,1)S(1)}, u32[]{:S(2)}, u32[]{:S(2)}) collective-permute-start(bf16[2,256,128]{2,1,0:T(8,128)(2,1)S(1)} %get-tuple-element.140), channel_id=1, source_target_pairs={{0,2},{1,3},{2,0},{3,1},{4,6},{5,7},{6,4},{7,5},{8,10},{9,11},{10,... | collective-permute-start | bytes 393224 | tf_op jit(solution)/shard_map/ppermute | solution.py:61
  171.0 15.1 %collective-permute-start.21 = (bf16[2,256,128]{2,1,0:T(8,128)(2,1)S(1)}, bf16[2,256,128]{2,1,0:T(8,128)(2,1)S(1)}, u32[]{:S(2)}, u32[]{:S(2)}) collective-permute-start(bf16[2,256,128]{2,1,0:T(8,128)(2,1)S(1)} %get-tuple-element.141), channel_id=1, source_target_pairs={{0,3},{1,2},{2,1},{3,0},{4,7},{5,6},{6,5},{7,4},{8,11},{9,10},{10,... | collective-permute-start | bytes 393224 | tf_op jit(solution)/shard_map/ppermute | solution.py:61
  186.4 18.7 %collective-permute-start.27 = (bf16[2,16,208,128]{3,2,1,0:T(8,128)(2,1)}, bf16[2,16,208,128]{3,2,1,0:T(8,128)(2,1)S(1)}, u32[]{:S(2)}, u32[]{:S(2)}) collective-permute-start(bf16[2,16,208,128]{3,2,1,0:T(8,128)(2,1)} %get-tuple-element.156), channel_id=1, source_target_pairs={{0,4},{1,5},{2,6},{3,7},{4,0},{5,1},{6,2},{7,3},{8,12},{9,13},{10,... | collective-permute-start | bytes 5111816 | tf_op jit(solution)/shard_map/ppermute | solution.py:61
  186.5 16.6 %collective-permute-start.22 = (bf16[4,320,128]{2,1,0:T(8,128)(2,1)S(1)}, bf16[4,320,128]{2,1,0:T(8,128)(2,1)S(1)}, u32[]{:S(2)}, u32[]{:S(2)}) collective-permute-start(bf16[4,320,128]{2,1,0:T(8,128)(2,1)S(1)} %get-tuple-element.144), channel_id=1, source_target_pairs={{0,8},{1,9},{2,10},{3,11},{4,12},{5,13},{6,14},{7,15},{8,0},{9,1},... | collective-permute-start | bytes 983048 | tf_op jit(solution)/shard_map/ppermute | solution.py:61
  188.3 14.8 %collective-permute-start.23 = (bf16[4,320,128]{2,1,0:T(8,128)(2,1)S(1)}, bf16[4,320,128]{2,1,0:T(8,128)(2,1)S(1)}, u32[]{:S(2)}, u32[]{:S(2)}) collective-permute-start(bf16[4,320,128]{2,1,0:T(8,128)(2,1)S(1)} %get-tuple-element.145), channel_id=1, source_target_pairs={{0,16},{1,17},{2,18},{3,19},{4,20},{5,21},{6,22},{7,23},{8,24},{9,... | collective-permute-start | bytes 983048 | tf_op jit(solution)/shard_map/ppermute | solution.py:61
  203.5 1.7 collective-permute-start.28
  205.3 11.7 %collective-permute-start.29 = (bf16[8,208,128]{2,1,0:T(8,128)(2,1)S(1)}, bf16[8,208,128]{2,1,0:T(8,128)(2,1)S(1)}, u32[]{:S(2)}, u32[]{:S(2)}) collective-permute-start(bf16[8,208,128]{2,1,0:T(8,128)(2,1)S(1)} %get-tuple-element.163), channel_id=1, source_target_pairs={{0,16},{1,17},{2,18},{3,19},{4,20},{5,21},{6,22},{7,23},{8,24},{9,... | collective-permute-start | bytes 1277960 | tf_op jit(solution)/shard_map/ppermute | solution.py:61
  205.7 11.5 %collective-permute-start.30 = (bf16[8,208,128]{2,1,0:T(8,128)(2,1)S(1)}, bf16[8,208,128]{2,1,0:T(8,128)(2,1)S(1)}, u32[]{:S(2)}, u32[]{:S(2)}) collective-permute-start(bf16[8,208,128]{2,1,0:T(8,128)(2,1)S(1)} %get-tuple-element.164), channel_id=1, source_target_pairs={{0,8},{1,9},{2,10},{3,11},{4,12},{5,13},{6,14},{7,15},{8,0},{9,1},... | collective-permute-start | bytes 1277960 | tf_op jit(solution)/shard_map/ppermute | solution.py:61
  217.4 6.6 %collective-permute-start.31 = (bf16[4,208,128]{2,1,0:T(8,128)(2,1)S(1)}, bf16[4,208,128]{2,1,0:T(8,128)(2,1)S(1)}, u32[]{:S(2)}, u32[]{:S(2)}) collective-permute-start(bf16[4,208,128]{2,1,0:T(8,128)(2,1)S(1)} %get-tuple-element.165), channel_id=1, source_target_pairs={{0,8},{1,9},{2,10},{3,11},{4,12},{5,13},{6,14},{7,15},{8,0},{9,1},... | collective-permute-start | bytes 638984 | tf_op jit(solution)/shard_map/ppermute | solution.py:61
  219.2 5.8 %collective-permute-start.32 = (bf16[4,208,128]{2,1,0:T(8,128)(2,1)S(1)}, bf16[4,208,128]{2,1,0:T(8,128)(2,1)S(1)}, u32[]{:S(2)}, u32[]{:S(2)}) collective-permute-start(bf16[4,208,128]{2,1,0:T(8,128)(2,1)S(1)} %get-tuple-element.166), channel_id=1, source_target_pairs={{0,16},{1,17},{2,18},{3,19},{4,20},{5,21},{6,22},{7,23},{8,24},{9,... | collective-permute-start | bytes 638984 | tf_op jit(solution)/shard_map/ppermute | solution.py:61
  219.5 8.0 %collective-permute-start.24 = (bf16[2,320,128]{2,1,0:T(8,128)(2,1)S(1)}, bf16[2,320,128]{2,1,0:T(8,128)(2,1)S(1)}, u32[]{:S(2)}, u32[]{:S(2)}) collective-permute-start(bf16[2,320,128]{2,1,0:T(8,128)(2,1)S(1)} %get-tuple-element.152), channel_id=1, source_target_pairs={{0,1},{1,0},{2,3},{3,2},{4,5},{5,4},{6,7},{7,6},{8,9},{9,8},{10,11... | collective-permute-start | bytes 491528 | tf_op jit(solution)/shard_map/ppermute | solution.py:61
  219.5 18.9 %collective-permute-start.25 = (bf16[2,320,128]{2,1,0:T(8,128)(2,1)S(1)}, bf16[2,320,128]{2,1,0:T(8,128)(2,1)S(1)}, u32[]{:S(2)}, u32[]{:S(2)}) collective-permute-start(bf16[2,320,128]{2,1,0:T(8,128)(2,1)S(1)} %get-tuple-element.153), channel_id=1, source_target_pairs={{0,2},{1,3},{2,0},{3,1},{4,6},{5,7},{6,4},{7,5},{8,10},{9,11},{10,... | collective-permute-start | bytes 491528 | tf_op jit(solution)/shard_map/ppermute | solution.py:61
  221.4 22.1 %copy-start.24 = (f32[4,32]{1,0:T(4,128)S(1)}, f32[4,32]{1,0:T(4,128)}, u32[]{:S(2)}) copy-start(f32[4,32]{1,0:T(4,128)} %refs_4_.1) | copy-start | bytes 1540
  221.4 22.1 %copy-start.25 = (f32[4,32]{1,0:T(4,128)S(1)}, f32[4,32]{1,0:T(4,128)}, u32[]{:S(2)}) copy-start(f32[4,32]{1,0:T(4,128)} %refs_5_.1) | copy-start | bytes 1540
  221.4 17.0 %collective-permute-start.26 = (bf16[2,320,128]{2,1,0:T(8,128)(2,1)S(1)}, bf16[2,320,128]{2,1,0:T(8,128)(2,1)S(1)}, u32[]{:S(2)}, u32[]{:S(2)}) collective-permute-start(bf16[2,320,128]{2,1,0:T(8,128)(2,1)S(1)} %get-tuple-element.154), channel_id=1, source_target_pairs={{0,3},{1,2},{2,1},{3,0},{4,7},{5,6},{6,5},{7,4},{8,11},{9,10},{10,... | collective-permute-start | bytes 491528 | tf_op jit(solution)/shard_map/ppermute | solution.py:61
  225.2 13.2 %collective-permute-start.33 = (bf16[2,208,128]{2,1,0:T(8,128)(2,1)S(1)}, bf16[2,208,128]{2,1,0:T(8,128)(2,1)S(1)}, u32[]{:S(2)}, u32[]{:S(2)}) collective-permute-start(bf16[2,208,128]{2,1,0:T(8,128)(2,1)S(1)} %get-tuple-element.171), channel_id=1, source_target_pairs={{0,1},{1,0},{2,3},{3,2},{4,5},{5,4},{6,7},{7,6},{8,9},{9,8},{10,11... | collective-permute-start | bytes 319496 | tf_op jit(solution)/shard_map/ppermute | solution.py:61
  225.3 18.2 %collective-permute-start.34 = (bf16[2,208,128]{2,1,0:T(8,128)(2,1)S(1)}, bf16[2,208,128]{2,1,0:T(8,128)(2,1)S(1)}, u32[]{:S(2)}, u32[]{:S(2)}) collective-permute-start(bf16[2,208,128]{2,1,0:T(8,128)(2,1)S(1)} %get-tuple-element.172), channel_id=1, source_target_pairs={{0,2},{1,3},{2,0},{3,1},{4,6},{5,7},{6,4},{7,5},{8,10},{9,11},{10,... | collective-permute-start | bytes 319496 | tf_op jit(solution)/shard_map/ppermute | solution.py:61
  227.5 16.0 %collective-permute-start.35 = (bf16[2,208,128]{2,1,0:T(8,128)(2,1)S(1)}, bf16[2,208,128]{2,1,0:T(8,128)(2,1)S(1)}, u32[]{:S(2)}, u32[]{:S(2)}) collective-permute-start(bf16[2,208,128]{2,1,0:T(8,128)(2,1)S(1)} %get-tuple-element.173), channel_id=1, source_target_pairs={{0,3},{1,2},{2,1},{3,0},{4,7},{5,6},{6,5},{7,4},{8,11},{9,10},{10,... | collective-permute-start | bytes 319496 | tf_op jit(solution)/shard_map/ppermute | solution.py:61
  245.5 3.6 %collective-permute-start.36 = (f32[8,128]{1,0:T(8,128)S(1)}, f32[8,128]{1,0:T(8,128)S(1)}, u32[]{:S(2)}, u32[]{:S(2)}) collective-permute-start(f32[8,128]{1,0:T(8,128)S(1)} %get-tuple-element.180), channel_id=1, source_target_pairs={{0,1},{1,0},{2,3},{3,2},{4,5},{5,4},{6,7},{7,6},{8,9},{9,8},{10,11... | collective-permute-start | bytes 12296 | tf_op jit(solution)/shard_map/ppermute | solution.py:61
  249.2 4.5 %collective-permute-start.37 = (f32[8,128]{1,0:T(8,128)S(1)}, f32[8,128]{1,0:T(8,128)S(1)}, u32[]{:S(2)}, u32[]{:S(2)}) collective-permute-start(f32[8,128]{1,0:T(8,128)S(1)} %add.21), channel_id=1, source_target_pairs={{0,2},{1,3},{2,0},{3,1},{4,6},{5,7},{6,4},{7,5},{8,10},{9,11},{10,... | collective-permute-start | bytes 12296 | tf_op jit(solution)/shard_map/ppermute | solution.py:61
  253.7 1.2 collective-permute-start.38
  254.8 3.6 %collective-permute-start.39 = (f32[8,128]{1,0:T(8,128)S(1)}, f32[8,128]{1,0:T(8,128)S(1)}, u32[]{:S(2)}, u32[]{:S(2)}) collective-permute-start(f32[8,128]{1,0:T(8,128)S(1)} %add.23), channel_id=1, source_target_pairs={{0,8},{1,9},{2,10},{3,11},{4,12},{5,13},{6,14},{7,15},{8,0},{9,1},... | collective-permute-start | bytes 12296 | tf_op jit(solution)/shard_map/ppermute | solution.py:61
  258.5 3.6 %collective-permute-start.40 = (f32[8,128]{1,0:T(8,128)S(1)}, f32[8,128]{1,0:T(8,128)S(1)}, u32[]{:S(2)}, u32[]{:S(2)}) collective-permute-start(f32[8,128]{1,0:T(8,128)S(1)} %add.24), channel_id=1, source_target_pairs={{0,16},{1,17},{2,18},{3,19},{4,20},{5,21},{6,22},{7,23},{8,24},{9,... | collective-permute-start | bytes 12296 | tf_op jit(solution)/shard_map/ppermute | solution.py:61
  (31 other events, 162.3 us)
Sparse Core Ops, SparseCore 0:
  11.6 78.4 all-gather.1
